TPU v7x, 32 devices: a whole 2x2x4 slice. The times are simulated.
32 devices in a mesh: seq: 2 (over y), row: 4 (over z), col: 4 (over x, core).
Axes of the slice: x: 2, y: 2, z: 4, core: 2. Of those that a mesh axis runs over, the one named last changes fastest.
Arguments:
- tokens: bfloat16 [4, 2048, 1088], P('row', 'seq', 'col'), may hold values from -6 to 6
- prefix: int32 [4], P('row'), may hold values from 204 to 1024, as said below
- ln1_gain: bfloat16 [1088], P('col'), may hold values from 0.5 to 1.5
- ln1_bias: bfloat16 [1088], P('col'), may hold values from -3 to 3
- w_qkv: bfloat16 [1088, 3, 1088], P('row', None, 'col'), may hold values from -1 to 1
- b_qv: bfloat16 [2, 1088], P(None, 'col'), may hold values from -3 to 3
- w_out: bfloat16 [1088, 1088], P('row'), may hold values from -1 to 1
- b_out: bfloat16 [1088], replicated, may hold values from -3 to 3
- ln2_gain: bfloat16 [1088], P('col'), may hold values from 0.5 to 1.5
- ln2_bias: bfloat16 [1088], P('col'), may hold values from -3 to 3
- w_up: bfloat16 [1088, 4352], P('row', 'col'), may hold values from -0.1875 to 0.1875
- b_up: bfloat16 [4352], P('col'), may hold values from -3 to 3
- w_down: bfloat16 [4352, 1088], P('col', 'row'), may hold values from -0.09375 to 0.09375
- b_down: bfloat16 [1088], P('col'), may hold values from -3 to 3
- cotangent: bfloat16 [4, 2048, 1088], P('row', 'seq', 'col'), may hold values from -6 to 6
Outputs:
- block_out: bfloat16 [4, 2048, 1088], P('row', 'seq', 'col')
- grad_tokens: float32 [4, 2048, 1088], P('row', 'seq', 'col')
- grad_ln1_gain: float32 [1088], P('col')
- grad_ln1_bias: float32 [1088], P('col')
- grad_w_qkv: float32 [1088, 3, 1088], P(('seq', 'row'), None, 'col')
- grad_b_qv: float32 [2, 1088], P(None, 'col')
- grad_w_out: float32 [1088, 1088], P(('seq', 'row'))
- grad_b_out: float32 [1088], replicated
- grad_ln2_gain: float32 [1088], P('col')
- grad_ln2_bias: float32 [1088], P('col')
- grad_w_up: float32 [1088, 4352], P(('seq', 'row'), 'col')
- grad_b_up: float32 [4352], P('col')
- grad_w_down: float32 [4352, 1088], P('col', ('seq', 'row'))
- grad_b_down: float32 [1088], P('col')
- clipped_qkv: float32 [1088, 3, 1088], P('row', None, 'col')
- head_max: float32 [17], replicated
Inputs may be any that keep to these rules, and one draw needn't show every extreme that they name: Positions below a sequence's prefix length attend to each other both ways; some sequence has the largest and some the smallest allowed length.
All inputs are finite; a program needn't handle non-finite values.
Results may differ from a plain program's by a relative error of at most 0.019.
Values may be sent and summed in bfloat16 or wider, within the bound.
No kernel may reach another device: no remote copies, remote signals or barrier semaphores. Data moves between devices by JAX's collectives and lax.ppermute only.
A program may use at most 448 MiB of HBM per device.

v0:
```python
import jax
import jax.numpy as jnp
from jax import lax
from jax.sharding import PartitionSpec as P

H = 17
E = 64


norm_eps = 1e-05
neg_fill = -1e30
clip_limit = 8.0


def layer_norm(values, gain_vec, bias_vec):
    center = values - jnp.mean(values, axis=-1, keepdims=True)
    spread = jnp.mean(center * center, axis=-1, keepdims=True)
    return center * lax.rsqrt(spread + norm_eps) * gain_vec + bias_vec


def gelu_exact(values):
    return jax.nn.gelu(values, approximate=False)


def visible(query_pos, key_pos, prefix_len):
    causal = key_pos[None, :] <= query_pos[:, None]
    both_prefix = (query_pos[:, None] < prefix_len) & (key_pos[None, :] < prefix_len)
    return causal | both_prefix


def needed(query_lo, query_hi, key_lo, prefix_len):
    return (key_lo <= query_hi) | (key_lo < prefix_len) & (query_lo < prefix_len)


def head_scores(queries, key_block, score_scale):
    return (
        jnp.einsum("qhe,khe->hqk", queries, key_block, preferred_element_type=jnp.float32)
        * score_scale
    )


def contract_rows(left, right):
    return lax.dot_general(
        left, right, (((0,), (0,)), ((), ())), preferred_element_type=jnp.float32
    )


def contract_cols(left, right):
    return lax.dot_general(
        left, right, (((1,), (1,)), ((), ())), preferred_element_type=jnp.float32
    )


def on_device(
    tokens,
    prefix,
    ln1_gain,
    ln1_bias,
    w_qkv,
    b_qv,
    w_out,
    b_out,
    ln2_gain,
    ln2_bias,
    w_up,
    b_up,
    w_down,
    b_down,
    cotangent,
):
    col_count = lax.axis_size("col")
    col_index = lax.axis_index("col")
    seq_index = lax.axis_index("seq")
    span_len = tokens.shape[1]
    part_width = tokens.shape[2]
    row_count = span_len // col_count
    seq_length = span_len * lax.axis_size("seq")
    score_scale = E ** (-0.5)
    prefix_len = prefix[0]
    gathered = (
        lax.all_gather(tokens, "col", axis=2, tiled=True),
        lax.all_gather(cotangent, "col", axis=2, tiled=True),
        lax.all_gather(ln1_gain, "col", axis=0, tiled=True),
        lax.all_gather(ln1_bias, "col", axis=0, tiled=True),
        lax.all_gather(ln2_gain, "col", axis=0, tiled=True),
        lax.all_gather(ln2_bias, "col", axis=0, tiled=True),
    )
    x_full = gathered[0][0].astype(jnp.float32)
    dy_full = gathered[1][0]
    gain_one = gathered[2].astype(jnp.float32)
    bias_one = gathered[3].astype(jnp.float32)
    gain_two = gathered[4].astype(jnp.float32)
    bias_two = gathered[5].astype(jnp.float32)
    full_width = x_full.shape[1]
    wqkv_all, wout_all, wup_all, wdown_all = (
        lax.all_gather(w_qkv, "row", axis=0, tiled=True),
        lax.all_gather(w_out, "row", axis=0, tiled=True),
        lax.all_gather(w_up, "row", axis=0, tiled=True),
        lax.all_gather(w_down, "row", axis=1, tiled=True),
    )
    normed_one = layer_norm(x_full, gain_one, bias_one)
    normed_one_b = normed_one.astype(jnp.bfloat16)
    projected = jnp.einsum(
        "td,dkf->tkf", normed_one_b, wqkv_all, preferred_element_type=jnp.float32
    )
    bias_q = b_qv[0].astype(jnp.float32)
    bias_v = b_qv[1].astype(jnp.float32)
    bias_three = jnp.stack([bias_q, jnp.zeros_like(bias_q), bias_v])
    qkv_local = (projected + bias_three[None]).astype(jnp.bfloat16)
    qkv_heads = lax.all_to_all(qkv_local[None], "col", split_axis=1, concat_axis=3, tiled=True)[0]
    kv_whole = lax.all_gather(qkv_heads[:, 1:], ("seq", "col"), axis=0, tiled=True)
    keys_all = kv_whole[:, 0].reshape(seq_length, H, E)
    values_all = kv_whole[:, 1].reshape(seq_length, H, E)
    queries = qkv_heads[:, 0].reshape(row_count, H, E)
    query_lo = seq_index * span_len + col_index * row_count
    query_hi = query_lo + row_count - 1
    query_pos = query_lo + jnp.arange(row_count, dtype=jnp.int32)
    block_rows = 2 * row_count
    block_count = seq_length // block_rows
    block_offsets = jnp.arange(block_rows, dtype=jnp.int32)
    block_ids = jnp.arange(block_count, dtype=jnp.int32)

    def stats_step(state, block_index):
        key_lo = block_index * block_rows

        def stats_compute(inner):
            run_max, run_sum, score_top = inner
            key_block = lax.dynamic_slice_in_dim(keys_all, key_lo, block_rows, 0)
            scores = head_scores(queries, key_block, score_scale)
            seen = visible(query_pos, key_lo + block_offsets, prefix_len)[None]
            masked = jnp.where(seen, scores, neg_fill)
            new_max = jnp.maximum(run_max, jnp.max(masked, axis=-1))
            weights_now = jnp.where(seen, jnp.exp(scores - new_max[..., None]), 0.0)
            run_sum = run_sum * jnp.exp(run_max - new_max) + jnp.sum(weights_now, axis=-1)
            score_top = jnp.maximum(score_top, jnp.max(masked, axis=(1, 2)))
            return (new_max, run_sum, score_top)

        return (
            lax.cond(
                needed(query_lo, query_hi, key_lo, prefix_len),
                stats_compute,
                lambda inner: inner,
                state,
            ),
            None,
        )

    stats_init = (
        jnp.full((H, row_count), neg_fill, jnp.float32),
        jnp.zeros((H, row_count), jnp.float32),
        jnp.full((H,), neg_fill, jnp.float32),
    )
    (run_max, run_sum, score_top), _ = lax.scan(stats_step, stats_init, block_ids)
    log_total = run_max + jnp.log(run_sum)

    def value_step(running, block_index):
        key_lo = block_index * block_rows

        def value_compute(inner):
            key_block = lax.dynamic_slice_in_dim(keys_all, key_lo, block_rows, 0)
            value_block = lax.dynamic_slice_in_dim(values_all, key_lo, block_rows, 0)
            scores = head_scores(queries, key_block, score_scale)
            seen = visible(query_pos, key_lo + block_offsets, prefix_len)[None]
            softmax_w = jnp.where(seen, jnp.exp(scores - log_total[..., None]), 0.0).astype(
                jnp.bfloat16
            )
            return inner + jnp.einsum(
                "hqk,khe->qhe", softmax_w, value_block, preferred_element_type=jnp.float32
            )

        return (
            lax.cond(
                needed(query_lo, query_hi, key_lo, prefix_len),
                value_compute,
                lambda inner: inner,
                running,
            ),
            None,
        )

    zero_heads = jnp.zeros((row_count, H, E), jnp.float32)
    attn_sum, _ = lax.scan(value_step, zero_heads, block_ids)
    attn_out = attn_sum.reshape(row_count, full_width)
    attn_low = attn_out.astype(jnp.bfloat16)
    head_max = lax.pmax(score_top, ("seq", "row", "col"))
    branch = jnp.dot(attn_low, wout_all, preferred_element_type=jnp.float32) + b_out.astype(
        jnp.float32
    )
    my_rows = lax.dynamic_slice_in_dim(x_full, col_index * row_count, row_count, 0) + branch
    after_attn = lax.all_gather(my_rows.astype(jnp.bfloat16), "col", axis=0, tiled=True).astype(
        my_rows.dtype
    )
    normed_two = layer_norm(after_attn, gain_two, bias_two)
    normed_two_b = normed_two.astype(jnp.bfloat16)
    pre_act = jnp.dot(normed_two_b, wup_all, preferred_element_type=jnp.float32) + b_up.astype(
        jnp.float32
    )
    act_low = gelu_exact(pre_act).astype(jnp.bfloat16)
    down_part = jnp.dot(act_low, wdown_all, preferred_element_type=jnp.float32)
    down_mine = lax.psum_scatter(
        down_part.astype(jnp.bfloat16), "col", scatter_dimension=1, tiled=True
    ).astype(jnp.float32)
    resid_mine = lax.dynamic_slice_in_dim(after_attn, col_index * part_width, part_width, 1)
    block_out = (resid_mine + down_mine + b_down.astype(jnp.float32)).astype(jnp.bfloat16)[None]
    grad_down = contract_rows(act_low, dy_full)
    grad_bdown = jnp.sum(cotangent[0], axis=0, dtype=jnp.float32)
    grad_act = contract_cols(dy_full, wdown_all)
    grad_pre = jax.vjp(gelu_exact, pre_act)[1](grad_act)[0]
    grad_pre_b = grad_pre.astype(jnp.bfloat16)
    grad_bup = jnp.sum(grad_pre_b, axis=0, dtype=jnp.float32)
    grad_up = contract_rows(normed_two_b, grad_pre_b)
    normed_two_part = contract_cols(grad_pre_b, wup_all)
    grad_normed_two = lax.psum(normed_two_part.astype(jnp.bfloat16), "col").astype(jnp.float32)
    norm_back_two = jax.vjp(layer_norm, after_attn, gain_two, bias_two)[1]
    grad_x1_norm, grad_gain_two, grad_bias_two = norm_back_two(grad_normed_two)
    grad_after = dy_full.astype(jnp.float32) + grad_x1_norm
    grad_after_rows = lax.dynamic_slice_in_dim(grad_after, col_index * row_count, row_count, 0)
    grad_branch = grad_after_rows.astype(jnp.bfloat16)
    grad_wout = contract_rows(attn_low, grad_branch)
    grad_bout = jnp.sum(grad_branch, axis=0, dtype=jnp.float32)
    grad_attn_b = contract_cols(grad_branch, wout_all).astype(jnp.bfloat16)
    grad_attn_heads = grad_attn_b.reshape(row_count, H, E)
    row_dot = jnp.sum(
        (grad_attn_b.astype(jnp.float32) * attn_out).reshape(row_count, H, E), axis=-1
    ).T

    def query_step(running, block_index):
        key_lo = block_index * block_rows

        def query_compute(inner):
            key_block = lax.dynamic_slice_in_dim(keys_all, key_lo, block_rows, 0)
            value_block = lax.dynamic_slice_in_dim(values_all, key_lo, block_rows, 0)
            scores = head_scores(queries, key_block, score_scale)
            seen = visible(query_pos, key_lo + block_offsets, prefix_len)[None]
            softmax_w = jnp.where(seen, jnp.exp(scores - log_total[..., None]), 0.0)
            grad_weights = jnp.einsum(
                "qhe,khe->hqk", grad_attn_heads, value_block, preferred_element_type=jnp.float32
            )
            grad_scores = (softmax_w * (grad_weights - row_dot[..., None])).astype(jnp.bfloat16)
            return inner + jnp.einsum(
                "hqk,khe->qhe", grad_scores, key_block, preferred_element_type=jnp.float32
            )

        return (
            lax.cond(
                needed(query_lo, query_hi, key_lo, prefix_len),
                query_compute,
                lambda inner: inner,
                running,
            ),
            None,
        )

    grad_query_sum, _ = lax.scan(query_step, zero_heads, block_ids)
    grad_queries = grad_query_sum * score_scale
    zero_rows = jnp.zeros((row_count, 2, full_width), jnp.float32)
    local_offsets = jnp.arange(row_count, dtype=jnp.int32)

    def sub_block(key_lo):

        def sub_compute(unused):
            key_block = lax.dynamic_slice_in_dim(keys_all, key_lo, row_count, 0)
            value_block = lax.dynamic_slice_in_dim(values_all, key_lo, row_count, 0)
            scores = head_scores(queries, key_block, score_scale)
            seen = visible(query_pos, key_lo + local_offsets, prefix_len)[None]
            softmax_w = jnp.where(seen, jnp.exp(scores - log_total[..., None]), 0.0)
            grad_values = jnp.einsum(
                "hqk,qhe->khe",
                softmax_w.astype(jnp.bfloat16),
                grad_attn_heads,
                preferred_element_type=jnp.float32,
            )
            grad_weights = jnp.einsum(
                "qhe,khe->hqk", grad_attn_heads, value_block, preferred_element_type=jnp.float32
            )
            grad_scores = (softmax_w * (grad_weights - row_dot[..., None])).astype(jnp.bfloat16)
            grad_keys = (
                jnp.einsum("hqk,qhe->khe", grad_scores, queries, preferred_element_type=jnp.float32)
                * score_scale
            )
            return jnp.stack(
                [
                    grad_keys.reshape(row_count, full_width),
                    grad_values.reshape(row_count, full_width),
                ],
                axis=1,
            )

        return lax.cond(
            needed(query_lo, query_hi, key_lo, prefix_len), sub_compute, lambda unused: zero_rows, 0
        )

    sub_starts = row_count * jnp.arange(
        row_count * lax.axis_size(("seq", "col")) // row_count, dtype=jnp.int32
    )
    key_grads = lax.psum_scatter(
        lax.map(sub_block, sub_starts)
        .reshape(row_count * lax.axis_size(("seq", "col")), 2, full_width)
        .astype(jnp.bfloat16),
        ("seq", "col"),
        scatter_dimension=0,
        tiled=True,
    ).astype(jnp.float32)
    grad_qkv_heads = jnp.stack(
        [grad_queries.reshape(row_count, full_width), key_grads[:, 0], key_grads[:, 1]], axis=1
    ).astype(jnp.bfloat16)
    grad_qkv = lax.all_to_all(grad_qkv_heads[None], "col", split_axis=3, concat_axis=1, tiled=True)[
        0
    ]
    bias_grads = jnp.sum(grad_qkv, axis=0, dtype=jnp.float32)
    grad_wqkv = jnp.einsum(
        "td,tkf->dkf", normed_one_b, grad_qkv, preferred_element_type=jnp.float32
    )
    grad_normed_one = jnp.einsum(
        "tkf,dkf->td", grad_qkv, wqkv_all, preferred_element_type=jnp.float32
    )
    grad_normed_one, grad_wout, grad_bout = (
        lax.psum(grad_normed_one.astype(jnp.bfloat16), "col").astype(jnp.float32),
        lax.psum(grad_wout.astype(jnp.bfloat16), "col").astype(jnp.float32),
        lax.psum(grad_bout.astype(jnp.bfloat16), "col").astype(jnp.float32),
    )
    norm_back_one = jax.vjp(layer_norm, x_full, gain_one, bias_one)[1]
    grad_x_norm, grad_gain_one, grad_bias_one = norm_back_one(grad_normed_one)
    grad_input = lax.dynamic_slice_in_dim(
        grad_after + grad_x_norm, col_index * part_width, part_width, 1
    )[None]

    def own_part(vector):
        return lax.dynamic_slice_in_dim(vector, col_index * part_width, part_width, 0)

    small_rows = jnp.stack(
        [
            own_part(grad_gain_one),
            own_part(grad_bias_one),
            own_part(grad_gain_two),
            own_part(grad_bias_two),
            bias_grads[0],
            bias_grads[2],
            grad_bdown,
        ]
    )
    group_count = lax.axis_size(("seq", "row"))
    tiled_small = jnp.broadcast_to(small_rows[None], (group_count,) + small_rows.shape)
    tiled_bup = jnp.broadcast_to(grad_bup[None], (group_count, grad_bup.shape[0]))
    tiled_bout = jnp.broadcast_to(grad_bout[None], (group_count, full_width))
    reduced = (
        lax.psum_scatter(grad_wqkv, ("seq", "row"), scatter_dimension=0, tiled=True),
        lax.psum_scatter(grad_wout, ("seq", "row"), scatter_dimension=0, tiled=True),
        lax.psum_scatter(grad_up, ("seq", "row"), scatter_dimension=0, tiled=True),
        lax.psum_scatter(grad_down, ("seq", "row"), scatter_dimension=1, tiled=True),
        lax.psum_scatter(tiled_small, ("seq", "row"), scatter_dimension=0, tiled=True),
        lax.psum_scatter(tiled_bup, ("seq", "row"), scatter_dimension=0, tiled=True),
        lax.psum_scatter(tiled_bout, ("seq", "row"), scatter_dimension=0, tiled=True),
    )
    small_sum = reduced[4][0]
    clip_factor = clip_limit / jnp.maximum(head_max, clip_limit)
    root_clip = jnp.sqrt(clip_factor)
    column_head = (col_index * part_width + jnp.arange(part_width, dtype=jnp.int32)) // E
    one_hot = (column_head[:, None] == jnp.arange(H, dtype=jnp.int32)[None, :]).astype(jnp.float32)
    column_root = jnp.sum(one_hot * root_clip[None, :], axis=1)
    scale_three = jnp.stack([column_root, column_root, jnp.ones_like(column_root)])
    clipped_qkv = w_qkv.astype(jnp.float32) * scale_three[None]
    return (
        block_out,
        grad_input,
        small_sum[0],
        small_sum[1],
        reduced[0],
        small_sum[4:6],
        reduced[1],
        reduced[6][0],
        small_sum[2],
        small_sum[3],
        reduced[2],
        reduced[5][0],
        reduced[3],
        small_sum[6],
        clipped_qkv,
        head_max,
    )


def solution(mesh):
    placed = (
        P("row", "seq", "col"),
        P("row"),
        P("col"),
        P("col"),
        P("row", None, "col"),
        P(None, "col"),
        P("row", None),
        P(),
        P("col"),
        P("col"),
        P("row", "col"),
        P("col"),
        P("col", "row"),
        P("col"),
        P("row", "seq", "col"),
    )
    return jax.shard_map(
        on_device,
        mesh=mesh,
        in_specs=placed,
        out_specs=(
            P("row", "seq", "col"),
            P("row", "seq", "col"),
            P("col"),
            P("col"),
            P(("seq", "row"), None, "col"),
            P(None, "col"),
            P(("seq", "row"), None),
            P(),
            P("col"),
            P("col"),
            P(("seq", "row"), "col"),
            P("col"),
            P("col", ("seq", "row")),
            P("col"),
            P("row", None, "col"),
            P(),
        ),
        check_vma=False,
    )
```

profile of v0, /device:TPU:0, one launch (start us, length us, event | category | flops | bytes accessed | tf_op | source)
XLA Modules:
  0.0 1446.7 jit_solution(15950843294780440878)
XLA Ops:
  15.7 13.3 all-reduce.11
  30.0 5.8 all-gather.9.cloned.1.call-done
  40.3 64.5 %all-gather.11.cloned.1.call-done = bf16[1088,3,272]{2,1,0:T(4,128)(2,1)} async-done(((bf16[272,3,272]{2,1,0:T(4,128)(2,1)}), bf16[1088,3,272]{2,1,0:T(4,128)(2,1)}) %all-gather.11.cloned.1.call-update) | async-done | bytes 1775632 | tf_op jit(solution)/shard_map/all_gather | solution.py:96
  104.8 5.8 fusion.131
  110.7 5.4 copy.88
  116.1 42.3 %all_to_all.30 = bf16[1,1024,3,272]{3,2,0,1:T(4,128)(2,1)} all-to-all(bf16[1,1024,3,272]{3,2,0,1:T(4,128)(2,1)} %copy.88), channel_id=1, replica_groups=mesh['seq'=2,'row'=4,'col'=4] {'col'}, dimensions={1} | all-to-all | bytes 3342336 | tf_op jit(solution)/shard_map/all_to_all | solution.py:110
  158.4 5.8 copy.100
  173.5 50.9 %all-gather.13.cloned.1.call-done = bf16[2048,2,1088]{0,2,1:T(8,128)(2,1)} async-done(((bf16[256,2,1088]{0,2,1:T(8,128)(2,1)}), bf16[2048,2,1088]{0,2,1:T(8,128)(2,1)}) %all-gather.13.cloned.1.call-update) | async-done | bytes 8912912 | tf_op jit(solution)/shard_map/all_gather | solution.py:111
  224.3 8.9 fusion.152
  233.3 24.7 %while.62 = (s32[]{:T(128)}, f32[17,256]{1,0:T(8,128)S(1)}, f32[17,256]{1,0:T(8,128)S(1)}, f32[17]{0:T(128)S(1)}, s32[4]{0:T(128)S(1)}, /*index=5*/s32[]{:T(128)...) while((s32[]{:T(128)}, f32[17,256]{1,0:T(8,128)S(1)}, ...), condition=%wide.region_8.9_spmd.clone, body=%wide.region_2.8_spmd.clone.sunk | while | flops 305670144 | bytes 20130952 | solution.py:153
  235.2 8.4 conditional.12
  236.8 3.5 fusion.20
  240.3 3.4 fusion.19
  245.6 8.5 conditional.12
  247.2 3.5 fusion.20
  258.6 20.8 %while.63 = (s32[]{:T(128)}, f32[256,17,64]{0,2,1:T(8,128)S(1)}, s32[4]{0:T(128)S(1)}, s32[]{:T(128)}, s32[]{:T(128)}, /*index=5*/pred[]{:T(512)}, bf16[2048,17,...) while((s32[]{:T(128)}, f32[256,17,64]{0,2,1:T(8,128)S(1)}, ...), condition=%wide.region_12.13_spmd.clone, body=%wide.region_9.12_spmd.clone.sunk | while | flops 580011520 | bytes 5308228 | solution.py:182
  260.6 6.5 conditional.13
  262.1 5.0 fusion.33
  269.0 6.5 conditional.13
  270.6 4.9 fusion.33
  279.6 4.5 fusion.108
  286.7 50.6 %all-gather.17.cloned.1.call-done = bf16[1024,1088]{0,1:T(8,128)(2,1)} async-done(((bf16[256,1088]{0,1:T(8,128)(2,1)}), bf16[1024,1088]{0,1:T(8,128)(2,1)}) %all-gather.17.cloned.1.call-update) | async-done | bytes 2228240 | tf_op jit(solution)/shard_map/all_gather | solution.py:190
  341.8 49.9 %all-gather.19.cloned.1.call-done = bf16[1088,1088]{1,0:T(8,128)(2,1)} async-done(((bf16[272,1088]{1,0:T(8,128)(2,1)}), bf16[1088,1088]{1,0:T(8,128)(2,1)}) %all-gather.19.cloned.1.call-update) | async-done | bytes 2367504 | tf_op jit(solution)/shard_map/all_gather | solution.py:98
  391.7 18.7 %multiply_convert_fusion = (bf16[1024,1088]{0,1:T(8,128)(2,1)}, f32[1024,1088]{0,1:T(8,128)}, f32[1024,1088]{0,1:T(8,128)}) fusion(f32[1088]{0:T(1024)S(1)} %convert_element_type.186, bf16[1088,1088]{1,0:T(8,128)(2,1)} %all-gather.19.cloned.1.call-done, bf16[1024,1088]{0,1:T(8,128)(2,1)S(1)} %copy-done.1, f32[1088]{0:T(1024)S(1)} %convert_element_type.184, ...), kind=kOutput, calls=%fused_computation.118 | convolution fusion | flops 2504523776 | bytes 15758080 | tf_op jit(solution)/shard_map/dot_general | solution.py:195
  410.4 5.0 all-gather.23.cloned.1.call-done
  415.4 54.5 %all-gather.21.cloned.1.call-done = bf16[1088,1088]{0,1:T(8,128)(2,1)} async-done(((bf16[1088,272]{0,1:T(8,128)(2,1)}), bf16[1088,1088]{0,1:T(8,128)(2,1)}) %all-gather.21.cloned.1.call-update) | async-done | bytes 2367504 | tf_op jit(solution)/shard_map/all_gather | solution.py:99
  470.0 9.9 convert_reduce_fusion.2
  481.2 4.2 convolution_convert_fusion.1
  485.5 52.4 %all-reduce.17.cloned.1.call-done = bf16[1024,1088]{0,1:T(8,128)(2,1)} async-done(((bf16[1024,1088]{0,1:T(8,128)(2,1)}), bf16[1024,1088]{0,1:T(8,128)(2,1)}) %all-reduce.17.cloned.1.call-update) | async-done | bytes 2228240 | tf_op jit(solution)/shard_map/psum | solution.py:213
  547.4 70.3 %while.65 = (s32[]{:T(128)}, bf16[8,256,2,1088]{1,3,2,0:T(8,128)(2,1)}, s32[8]{0:T(128)S(1)}, s32[]{:T(128)}, s32[]{:T(128)}, /*index=5*/pred[]{:T(512)}, bf16[2...) while((s32[]{:T(128)}, ...), condition=%wide.region_27.28_spmd.clone, body=%wide.region_24.0_spmd.clone.sunk | while | flops 582878208 | bytes 40365416 | solution.py:297
  550.4 13.4 conditional.15
  558.7 5.0 fusion.78
  567.4 13.4 conditional.15
  575.7 5.0 fusion.78
  584.5 13.4 conditional.15
  592.8 5.0 fusion.78
  617.7 8.2 copy.101
  626.1 41.4 %while.64 = (s32[]{:T(128)}, f32[256,17,64]{0,2,1:T(8,128)S(1)}, s32[4]{0:T(128)S(1)}, s32[]{:T(128)}, s32[]{:T(128)}, /*index=5*/pred[]{:T(512)}, bf16[2048,17,...) while((s32[]{:T(128)}, f32[256,17,64]{0,2,1:T(8,128)S(1)}, ...), condition=%wide.region_23.24_spmd.clone, body=%wide.region_20.0_spmd.clone.sunk | while | flops 869680640 | bytes 24822632 | solution.py:254
  628.0 16.8 %conditional.14 = (f32[256,17,64]{0,2,1:T(8,128)S(1)}) conditional(s32[]{:T(128)} %convert_element_type.344, f32[256,17,64]{0,2,1:T(8,128)S(1)} %get-tuple-element.1557, (s32[]{:T(128)}, bf16[2048,17,64]{0,2,1:T(8,128)(2,1)}, s32[512]{0:T(512)S(1)}, s32[]{:T(128)}, s32[]{:T(128)}, /*index=5*/bf16[256,17,64]{0,2,1:T(8,128)(2,1)S(1)}, ...), branch_computations={%region_21.21_spmd, %region_22.22_spmd} | conditional | flops 869680640 | bytes 24819262 | solution.py:245
  628.1 6.8 fusion.58
  636.4 8.5 fusion.52
  646.8 16.8 %conditional.14 = (f32[256,17,64]{0,2,1:T(8,128)S(1)}) conditional(s32[]{:T(128)} %convert_element_type.344, f32[256,17,64]{0,2,1:T(8,128)S(1)} %get-tuple-element.1557, (s32[]{:T(128)}, bf16[2048,17,64]{0,2,1:T(8,128)(2,1)}, s32[512]{0:T(512)S(1)}, s32[]{:T(128)}, s32[]{:T(128)}, /*index=5*/bf16[256,17,64]{0,2,1:T(8,128)(2,1)S(1)}, ...), branch_computations={%region_21.21_spmd, %region_22.22_spmd} | conditional | flops 869680640 | bytes 24819262 | solution.py:245
  646.8 6.8 fusion.58
  655.1 8.5 fusion.52
  667.6 98.6 %reduce-scatter.15.cloned.1.call-done = bf16[256,2,1088]{0,2,1:T(8,128)(2,1)} async-done(((bf16[2048,2,1088]{0,2,1:T(8,128)(2,1)}), bf16[256,2,1088]{0,2,1:T(8,128)(2,1)}) %reduce-scatter.15.cloned.1.call-update) | async-done | bytes 1114128 | tf_op jit(solution)/shard_map/reduce_scatter | solution.py:296
  767.6 9.8 copy.92
  777.3 3.6 all-to-all-start.1
  783.4 24.6 %all-to-all-done.1 = bf16[1,256,3,1088]{1,2,0,3:T(4,128)(2,1)S(1)} async-done(((bf16[1,256,3,1088]{1,2,0,3:T(4,128)(2,1)}), bf16[1,256,3,1088]{1,2,0,3:T(4,128)(2,1)S(1)}, u32[]{:S(2)}, u32[]{:S(2)}) %all-to-all-start.1) | async-done | bytes 1671200 | tf_op jit(solution)/shard_map/all_to_all | solution.py:307
  812.7 6.3 bitcast_convert_fusion
  820.8 5.9 convolution_convert_fusion.2
  827.1 6.5 psum.31
  835.4 81.9 %all-reduce.21.cloned.1.call-done = (bf16[1024,1088]{0,1:T(8,128)(2,1)}, bf16[1088,1088]{1,0:T(8,128)(2,1)}) async-done(((bf16[1024,1088]{0,1:T(8,128)(2,1)}, bf16[1088,1088]{1,0:T(8,128)(2,1)}), (bf16[1024,1088]{0,1:T(8,128)(2,1)}, bf16[1088,1088]{1,0:T(8,128)(2,1)})) %all-reduce.21.cloned.1.call-update) | async-done | bytes 4595728 | tf_op jit(solution)/shard_map/psum | solution.py:318
  917.3 4.1 fusion.100
  923.5 6.9 fusion.148
  930.5 7.6 fusion.115
  938.8 7.8 fusion.113
  946.7 4.3 convert_element_type.208
  951.8 39.7 %pmax.7 = f32[17]{0:T(128)S(1)} all-reduce(f32[17]{0:T(128)S(1)} %copy-done.33), channel_id=1, replica_groups=mesh['seq'=2,'row'=4,'col'=4] {'seq','row','col'}, use_global_device_ids=true, to_apply=%region_49.50 | all-reduce | flops 17 | bytes 136 | tf_op jit(solution)/shard_map/pmax | solution.py:185
  997.9 3.6 fusion.150
  1004.0 22.0 %all-reduce.19.cloned.1.call-done = (f32[8,7,272]{2,1,0:T(8,128)}, f32[8,1088]{1,0:T(8,128)}, f32[8,1088]{1,0:T(8,128)}) async-done(((f32[8,7,272]{2,1,0:T(8,128)}, f32[8,1088]{1,0:T(8,128)}, f32[8,1088]{1,0:T(8,128)}), (f32[8,7,272]{2,1,0:T(8,128)}, f32[8,1088]{1,0:T(8,128)}, f32[8,1088]{1,0:T(8,128)})) %all-reduce.19.cloned.1.call-update) | async-done | bytes 130576
  1032.3 97.7 %reduce-scatter.21.cloned.1.call-done = f32[136,1088]{1,0:T(8,128)} async-done(((f32[1088,1088]{1,0:T(8,128)}), f32[136,1088]{1,0:T(8,128)}) %reduce-scatter.21.cloned.1.call-update) | async-done | bytes 591888
  1130.0 103.5 %reduce-scatter.23.cloned.1.call-done = f32[1088,136]{0,1:T(8,128)} async-done(((f32[1088,1088]{0,1:T(8,128)}), f32[1088,136]{0,1:T(8,128)}) %reduce-scatter.23.cloned.1.call-update) | async-done | bytes 591888
  1233.5 102.9 %reduce-scatter.17.cloned.1.call-done = f32[136,3,272]{2,0,1:T(8,128)} async-done(((f32[1088,3,272]{2,0,1:T(8,128)}), f32[136,3,272]{2,0,1:T(8,128)}) %reduce-scatter.17.cloned.1.call-update) | async-done | bytes 443920 | tf_op jit(solution)/shard_map/reduce_scatter | solution.py:347
  1336.4 103.5 %reduce-scatter.19.cloned.1.call-done = f32[136,1088]{1,0:T(8,128)} async-done(((f32[1088,1088]{1,0:T(8,128)}), f32[136,1088]{1,0:T(8,128)}) %reduce-scatter.19.cloned.1.call-update) | async-done | bytes 591888
  (320 shorter events, 124.8 us)
Async XLA Ops:
  7.2 28.6 %all-gather.9.cloned.1.call-start = ((), (), s32[]{:S(2)}) async-start(), calls=%async_computation.8 | async-start | bytes 2785280 | tf_op jit(solution)/shard_map/all_gather | solution.py:81
  7.9 96.9 %all-gather.11.cloned.1.call-start = ((), (), s32[]{:S(2)}) async-start(), calls=%async_computation.9 | async-start | bytes 4177920 | tf_op jit(solution)/shard_map/all_gather | solution.py:96
  10.3 214.0 %all-gather.13.cloned.1.call-start = ((), (), s32[]{:S(2)}) async-start(), calls=%async_computation.10 | async-start | bytes 10027008 | tf_op jit(solution)/shard_map/all_gather | solution.py:111
  29.0 81.6 %copy-start.24 = (f32[1088]{0:T(1024)}, f32[1088]{0:T(1024)S(1)}, u32[]{:S(2)}) copy-start(f32[1088]{0:T(1024)S(1)} %convert_element_type.174) | copy-start | bytes 13060
  29.0 81.6 %copy-start.16 = (f32[1088]{0:T(1024)}, f32[1088]{0:T(1024)S(1)}, u32[]{:S(2)}) copy-start(f32[1088]{0:T(1024)S(1)} %convert_element_type.173) | copy-start | bytes 13060
  35.8 69.0 %copy-start.3 = (bf16[1,1024,1088]{1,2,0:T(8,128)(2,1)S(1)}, bf16[1,1024,1088]{1,2,0:T(8,128)(2,1)}, u32[]{:S(2)}) copy-start(bf16[1,1024,1088]{1,2,0:T(8,128)(2,1)} %all-gather.9.cloned.1.call-done) | copy-start | bytes 6684676
  38.0 72.7 %copy-start.18 = (f32[1024]{0:T(1024)}, f32[1024]{0:T(1024)S(1)}, u32[]{:S(2)}) copy-start(f32[1024]{0:T(1024)S(1)} %broadcast_multiply_fusion.1) | copy-start | bytes 12292
  40.2 70.4 %copy-start.22 = (f32[1024]{0:T(1024)}, f32[1024]{0:T(1024)S(1)}, u32[]{:S(2)}) copy-start(f32[1024]{0:T(1024)S(1)} %multiply_reduce_fusion.1) | copy-start | bytes 12292
  40.3 70.4 %copy-start.20 = (f32[1024]{0:T(1024)}, f32[1024]{0:T(1024)S(1)}, u32[]{:S(2)}) copy-start(f32[1024]{0:T(1024)S(1)} %fusion.138) | copy-start | bytes 12292
  164.2 5.5 copy-start.26
  165.9 1.2 copy-start.10
  168.2 111.4 %all-gather.15.cloned.1.call-start = ((), (), s32[]{:S(2)}) async-start(), calls=%async_computation.11 | async-start | bytes 3133440 | tf_op jit(solution)/shard_map/all_gather | solution.py:97
  168.8 168.6 %all-gather.17.cloned.1.call-start = ((), (), s32[]{:S(2)}) async-start(), calls=%async_computation.12 | async-start | bytes 2785280 | tf_op jit(solution)/shard_map/all_gather | solution.py:190
  258.0 0.5 copy-start.32
  279.5 6.8 copy-start.5
  279.5 7.2 copy-start.27
  279.6 7.2 copy-start.12
  284.1 107.6 %all-gather.19.cloned.1.call-start = ((), (), s32[]{:S(2)}) async-start(), calls=%async_computation.13 | async-start | bytes 3133440 | tf_op jit(solution)/shard_map/all_gather | solution.py:98
  284.7 130.7 %all-gather.23.cloned.1.call-start = ((), (), s32[]{:S(2)}) async-start(), calls=%async_computation.16 | async-start | bytes 2785280 | tf_op jit(solution)/shard_map/all_gather | solution.py:82
  285.5 184.5 %all-gather.21.cloned.1.call-start = ((), (), s32[]{:S(2)}) async-start(), calls=%async_computation.14 | async-start | bytes 3133440 | tf_op jit(solution)/shard_map/all_gather | solution.py:99
  286.2 251.7 %all-reduce.17.cloned.1.call-start = ((), (), s32[]{:S(2)}) async-start(), calls=%async_computation.17 | async-start | bytes 4456448 | tf_op jit(solution)/shard_map/psum | solution.py:213
  337.3 54.4 %copy-start.1 = (bf16[1024,1088]{0,1:T(8,128)(2,1)S(1)}, bf16[1024,1088]{0,1:T(8,128)(2,1)}, u32[]{:S(2)}) copy-start(bf16[1024,1088]{0,1:T(8,128)(2,1)} %all-gather.17.cloned.1.call-done) | copy-start | bytes 6684676
  469.9 11.3 copy-start.30
  479.8 1.4 copy-start.35
  485.5 280.7 %reduce-scatter.15.cloned.1.call-start = ((), (), s32[]{:S(2)}) async-start(), calls=%async_computation.18 | async-start | bytes 10027008 | tf_op jit(solution)/shard_map/reduce_scatter | solution.py:296
  537.9 3.1 copy-start.4
  537.9 5.4 copy-start.14
  543.3 2.0 copy-start.6
  543.4 2.0 copy-start.8
  545.0 2.3 copy-start.9
  554.6 2.0 copy-start
  571.7 2.0 copy-start
  588.8 2.0 copy-start
  767.6 13.5 copy-start.13
  777.3 30.7 %all-to-all-start.1 = ((bf16[1,256,3,1088]{1,2,0,3:T(4,128)(2,1)}), bf16[1,256,3,1088]{1,2,0,3:T(4,128)(2,1)S(1)}, u32[]{:S(2)}, u32[]{:S(2)}) async-start(bf16[1,256,3,1088]{1,2,0,3:T(4,128)(2,1)} %copy.92), calls=%async_computation.3 | async-start | bytes 4456448 | tf_op jit(solution)/shard_map/all_to_all | solution.py:307
  781.0 136.3 %all-reduce.21.cloned.1.call-start = ((), (), s32[]{:S(2)}) async-start(), calls=%async_computation.24 | async-start | bytes 9469952 | tf_op jit(solution)/shard_map/psum | solution.py:318
  808.3 1.2 copy-start.7
  819.1 1.7 copy-start.29
  819.1 176.4 %reduce-scatter.13.cloned.1.call-start = ((), (), s32[]{:S(2)}) async-start(), calls=%async_computation.15 | async-start | bytes 2785280 | tf_op jit(solution)/shard_map/reduce_scatter | solution.py:200
  820.8 6.0 copy-start.15
  826.7 90.6 %copy-start.17 = (f32[1088]{0:T(1024)S(1)}, f32[1088]{0:T(1024)}, u32[]{:S(2)}) copy-start(f32[1088]{0:T(1024)} %copy-done.16) | copy-start | bytes 13060
  826.7 90.6 %copy-start.19 = (f32[1024]{0:T(1024)S(1)}, f32[1024]{0:T(1024)}, u32[]{:S(2)}) copy-start(f32[1024]{0:T(1024)} %copy-done.18) | copy-start | bytes 12292
  826.7 90.6 %copy-start.21 = (f32[1024]{0:T(1024)S(1)}, f32[1024]{0:T(1024)}, u32[]{:S(2)}) copy-start(f32[1024]{0:T(1024)} %copy-done.20) | copy-start | bytes 12292
  826.7 96.8 %copy-start.2 = (bf16[1024,1088]{0,1:T(8,128)(2,1)S(1)}, bf16[1024,1088]{0,1:T(8,128)(2,1)}, u32[]{:S(2)}) copy-start(bf16[1024,1088]{0,1:T(8,128)(2,1)} %all-gather.17.cloned.1.call-done) | copy-start | bytes 6684676
  826.7 199.3 %all-reduce.19.cloned.1.call-start = ((), (), s32[]{:S(2)}) async-start(), calls=%async_computation.23 | async-start | bytes 344064
  923.5 206.5 %reduce-scatter.21.cloned.1.call-start = ((), (), s32[]{:S(2)}) async-start(), calls=%async_computation.21 | async-start | bytes 5640192
  930.4 303.0 %reduce-scatter.23.cloned.1.call-start = ((), (), s32[]{:S(2)}) async-start(), calls=%async_computation.22 | async-start | bytes 5640192
  938.1 0.7 copy-start.25
  938.2 398.3 %reduce-scatter.17.cloned.1.call-start = ((), (), s32[]{:S(2)}) async-start(), calls=%async_computation.19 | async-start | bytes 5640192 | tf_op jit(solution)/shard_map/reduce_scatter | solution.py:347
  946.6 493.3 %reduce-scatter.19.cloned.1.call-start = ((), (), s32[]{:S(2)}) async-start(), calls=%async_computation.20 | async-start | bytes 5640192
  946.7 4.4 copy-start.28
  946.7 4.5 copy-start.31
  946.7 5.1 copy-start.33
  946.7 45.0 %copy-start.11 = (bf16[272,3,272]{2,0,1:T(8,128)(2,1)S(1)}, bf16[272,3,272]{2,0,1:T(8,128)(2,1)}, u32[]{:S(2)}) copy-start(bf16[272,3,272]{2,0,1:T(8,128)(2,1)} %param.35) | copy-start | bytes 1331716
  991.6 6.3 copy-start.34
  992.9 5.0 copy-start.23
Sparse Core Ops, SparseCore 0:
  9.6 26.1 all-gather.8
  37.9 66.8 all-gather.10
  168.3 55.9 all-gather.12
  225.7 52.9 all-gather.14
  284.3 53.0 all-gather.16
  338.8 52.9 all-gather.18
  393.3 22.1 all-gather.22
  417.0 52.9 all-gather.20
  485.6 52.2 all-reduce.16
  626.1 140.0 reduce-scatter.14
  819.2 98.0 all-reduce.20
  919.7 32.2 reduce-scatter.12
  956.0 69.9 all-reduce.18
  1030.1 99.7 reduce-scatter.20
  1134.5 98.9 reduce-scatter.22
  1237.6 98.8 reduce-scatter.16
  1340.9 98.9 reduce-scatter.18
where the time goes:
time: 1460 us; the launch traced here: 1450 us
  waiting for transfers between devices  972 us (67%)
  matrix products  157 us (11%)
  blocking collectives  102 us (7%)
  local copies, waits for them, and re-layouts  91.2 us (6%)
  other arithmetic  64.8 us (4%)
  loops' own time  38.9 us (3%)
  between operations  16.1 us (1%)
    unnamed x21, waiting for transfers between devices  330 us
    reduce_scatter x1, waiting for transfers between devices, on_device(): lax.psum_scatter(grad_wqkv, ('seq', 'row'), scatter_dimension=0, tiled=True)  103 us
    reduce_scatter x1, waiting for transfers between devices, on_device(): lax.psum_scatter(lax.map(sub_block, sub_starts).reshape(row_count * lax.a...  98.6 us
    psum x1, waiting for transfers between devices, on_device(): lax.psum(grad_normed_one.astype(jnp.bfloat16), 'col').astype(jnp.float32)  81.9 us
    all_gather x1, waiting for transfers between devices, on_device(): lax.all_gather(w_qkv, 'row', axis=0, tiled=True)  64.5 us
    all_gather x1, waiting for transfers between devices, on_device(): lax.all_gather(w_down, 'row', axis=1, tiled=True)  54.5 us
    psum x1, waiting for transfers between devices, on_device(): lax.psum(normed_two_part.astype(jnp.bfloat16), 'col').astype(jnp.float32)  52.4 us
    all_gather x1, waiting for transfers between devices, on_device(): lax.all_gather(qkv_heads[:, 1:], ('seq', 'col'), axis=0, tiled=True)  50.9 us
  transfers between devices with their start and end apart: 18, of which 16 were waited for; matrix products, arithmetic and copies ran while one was open for 13% of the time, Pallas kernels for 0%

commit v1 on v0

v1 whole, which is shorter than its diff:
```python
import functools

import jax
import jax.numpy as jnp
from jax import lax
from jax.experimental import pallas as pl
from jax.experimental.pallas import tpu as pltpu
from jax.sharding import PartitionSpec as P

H = 17
E = 64

norm_eps = 1e-05
neg_fill = -1e30
clip_limit = 8.0

f32 = jnp.float32
bf16 = jnp.bfloat16


def dot_nn(left, right):
    return lax.dot_general(left, right, (((1,), (0,)), ((), ())), preferred_element_type=f32)


def dot_nt(left, right):
    return lax.dot_general(left, right, (((1,), (1,)), ((), ())), preferred_element_type=f32)


def dot_tn(left, right):
    return lax.dot_general(left, right, (((0,), (0,)), ((), ())), preferred_element_type=f32)


def block_limits(info, block, rows):
    prefix_len = info[0]
    query_lo = info[1] + block * rows
    query_hi = query_lo + rows - 1
    in_prefix = query_lo < prefix_len
    limit_max = jnp.where(in_prefix, jnp.maximum(prefix_len - 1, query_hi), query_hi)
    limit_min = jnp.where(in_prefix, prefix_len - 1, query_lo)
    return prefix_len, query_lo, limit_max, limit_min


def attn_fwd_body(
    slots, rows, keys, info, q_ref, kv_ref, attn_ref, exact_ref, lse_ref, top_ref, m_s, l_s, acc_s
):
    block = pl.program_id(0)
    width = slots * E
    prefix_len, query_lo, limit_max, limit_min = block_limits(info, block, rows)
    n_need = limit_max // keys + 1
    n_full = (limit_min + 1) // keys
    positions = query_lo + lax.broadcasted_iota(jnp.int32, (rows, 1), 0)
    limit = jnp.where(positions < prefix_len, prefix_len - 1, positions)
    m_s[...] = jnp.full_like(m_s, neg_fill)
    l_s[...] = jnp.zeros_like(l_s)
    acc_s[...] = jnp.zeros_like(acc_s)

    def step(index, masked):
        start = pl.multiple_of(index * keys, keys)
        if masked:
            seen = (start + lax.broadcasted_iota(jnp.int32, (rows, keys), 1)) <= limit
        for h in range(slots):
            here = slice(h * E, h * E + E)
            there = slice(width + h * E, width + h * E + E)
            scores = dot_nt(q_ref[:, here], kv_ref[pl.ds(start, keys), here])
            if masked:
                scores = jnp.where(seen, scores, neg_fill)
            old_max = m_s[h]
            new_max = jnp.maximum(old_max, jnp.max(scores, axis=1, keepdims=True))
            weights = jnp.exp(scores - new_max[:, :1])
            shrink = jnp.exp(old_max - new_max)
            l_s[h] = l_s[h] * shrink + jnp.sum(weights, axis=1, keepdims=True)
            acc_s[h] = acc_s[h] * shrink[:, :E] + dot_nn(
                weights.astype(bf16), kv_ref[pl.ds(start, keys), there]
            )
            m_s[h] = new_max

    @pl.loop(0, n_full)
    def _(index):
        step(index, False)

    @pl.loop(n_full, n_need)
    def _(index):
        step(index, True)

    @pl.when(block == 0)
    def _():
        top_ref[...] = jnp.full_like(top_ref, neg_fill)

    for h in range(slots):
        here = slice(h * E, h * E + E)
        row_max, row_sum = m_s[h], l_s[h]
        outcome = acc_s[h] / row_sum[:, :E]
        exact_ref[:, here] = outcome
        attn_ref[:, here] = outcome.astype(bf16)
        lse_ref[:, h : h + 1] = (row_max + jnp.log(row_sum))[:, :1]
        top_ref[h : h + 1, :] = jnp.maximum(
            top_ref[h : h + 1, :], jnp.max(row_max, axis=0, keepdims=True)
        )


def attn_fwd(info, queries, kv_all, slots, rows=256, keys=512):
    count, width = queries.shape
    total = kv_all.shape[0]
    row_block = pl.BlockSpec((rows, width), lambda i, _: (i, 0))
    return pl.pallas_call(
        functools.partial(attn_fwd_body, slots, rows, keys),
        grid_spec=pltpu.PrefetchScalarGridSpec(
            num_scalar_prefetch=1,
            grid=(count // rows,),
            in_specs=[row_block, pl.BlockSpec((total, 2 * width), lambda i, _: (0, 0))],
            out_specs=[
                row_block,
                row_block,
                pl.BlockSpec((rows, 8), lambda i, _: (i, 0)),
                pl.BlockSpec((8, 128), lambda i, _: (0, 0)),
            ],
            scratch_shapes=[
                pltpu.VMEM((slots, rows, 128), f32),
                pltpu.VMEM((slots, rows, 128), f32),
                pltpu.VMEM((slots, rows, E), f32),
            ],
        ),
        out_shape=[
            jax.ShapeDtypeStruct((count, width), bf16),
            jax.ShapeDtypeStruct((count, width), f32),
            jax.ShapeDtypeStruct((count, 8), f32),
            jax.ShapeDtypeStruct((8, 128), f32),
        ],
        compiler_params=pltpu.CompilerParams(vmem_limit_bytes=48 * 2**20),
        cost_estimate=pl.CostEstimate(
            flops=20 * 10**9, bytes_accessed=8 * 10**6, transcendentals=8 * 10**6
        ),
        name="attn_fwd",
    )(info, queries, kv_all)


def attn_bwd_body(
    slots, rows, keys, key_first, info, q_ref, kv_ref, do_ref, lse_ref, dot_ref, dq_ref, dkv_ref
):
    block = pl.program_id(0)
    width = slots * E
    n_blocks = kv_ref.shape[0] // keys
    prefix_len, query_lo, limit_max, limit_min = block_limits(info, block, rows)
    n_need = jnp.clip((limit_max - key_first) // keys + 1, 0, n_blocks)
    n_full = jnp.clip((limit_min - key_first + 1) // keys, 0, n_blocks)
    positions = query_lo + lax.broadcasted_iota(jnp.int32, (1, rows), 1)
    limit = jnp.where(positions < prefix_len, prefix_len - 1, positions) - key_first

    @pl.when(block == 0)
    def _():
        dkv_ref[...] = jnp.zeros_like(dkv_ref)

    dq_ref[...] = jnp.zeros_like(dq_ref)

    def step(index, masked):
        start = pl.multiple_of(index * keys, keys)
        if masked:
            seen = (start + lax.broadcasted_iota(jnp.int32, (keys, rows), 0)) <= limit
        for h in range(slots):
            here = slice(h * E, h * E + E)
            there = slice(width + h * E, width + h * E + E)
            q_head, do_head = q_ref[:, here], do_ref[:, here]
            k_head = kv_ref[pl.ds(start, keys), here]
            v_head = kv_ref[pl.ds(start, keys), there]
            probs = jnp.exp(dot_nt(k_head, q_head) - lse_ref[h : h + 1, :])
            if masked:
                probs = jnp.where(seen, probs, 0.0)
            dkv_ref[pl.ds(start, keys), there] += dot_nn(probs.astype(bf16), do_head)
            grad_probs = dot_nt(v_head, do_head)
            grad_scores = (probs * (grad_probs - dot_ref[h : h + 1, :])).astype(bf16)
            dkv_ref[pl.ds(start, keys), here] += dot_nn(grad_scores, q_head)
            dq_ref[:, here] += dot_tn(grad_scores, k_head)

    @pl.loop(0, n_full)
    def _(index):
        step(index, False)

    @pl.loop(n_full, n_need)
    def _(index):
        step(index, True)


def attn_bwd(info, queries, kv_all, grad_attn, lse_rows, dot_rows, slots, segment, rows=256, keys=256):
    count, width = queries.shape
    row_block = pl.BlockSpec((rows, width), lambda i, _: (i, 0))
    vec_block = pl.BlockSpec((8, rows), lambda i, _: (0, i))
    return pl.pallas_call(
        functools.partial(attn_bwd_body, slots, rows, keys, segment * count),
        grid_spec=pltpu.PrefetchScalarGridSpec(
            num_scalar_prefetch=1,
            grid=(count // rows,),
            in_specs=[
                row_block,
                pl.BlockSpec((count, 2 * width), lambda i, _: (segment, 0)),
                row_block,
                vec_block,
                vec_block,
            ],
            out_specs=[row_block, pl.BlockSpec((count, 2 * width), lambda i, _: (0, 0))],
        ),
        out_shape=[
            jax.ShapeDtypeStruct((count, width), f32),
            jax.ShapeDtypeStruct((count, 2 * width), f32),
        ],
        compiler_params=pltpu.CompilerParams(vmem_limit_bytes=48 * 2**20),
        cost_estimate=pl.CostEstimate(
            flops=25 * 10**9, bytes_accessed=8 * 10**6, transcendentals=8 * 10**6
        ),
        name="attn_bwd",
    )(info, queries, kv_all, grad_attn, lse_rows, dot_rows)


X_SWAP = [(0, 2), (2, 0), (1, 3), (3, 1)]
CORE_SWAP = [(0, 1), (1, 0), (2, 3), (3, 2)]


def swap_x(array):
    return lax.ppermute(array, "col", X_SWAP)


def swap_core(array):
    return lax.ppermute(array, "col", CORE_SWAP)


def ring(array, axis, shift):
    count = lax.axis_size(axis)
    return lax.ppermute(array, axis, [(i, (i + shift) % count) for i in range(count)])


def gather_col(shard, x_bit, core_bit):
    other = swap_x(shard)
    low = jnp.where(x_bit == 0, shard, other)
    high = jnp.where(x_bit == 0, other, shard)
    low_other = swap_core(low)
    high_other = swap_core(high)
    return (
        jnp.where(core_bit == 0, low, low_other),
        jnp.where(core_bit == 0, low_other, low),
        jnp.where(core_bit == 0, high, high_other),
        jnp.where(core_bit == 0, high_other, high),
    )


def scatter_col(parts, x_bit, core_bit):
    low_mine = jnp.where(core_bit == 0, parts[0], parts[1])
    low_theirs = jnp.where(core_bit == 0, parts[1], parts[0])
    high_mine = jnp.where(core_bit == 0, parts[2], parts[3])
    high_theirs = jnp.where(core_bit == 0, parts[3], parts[2])
    low = low_mine.astype(f32) + swap_core(low_theirs).astype(f32)
    high = high_mine.astype(f32) + swap_core(high_theirs).astype(f32)
    mine = jnp.where(x_bit == 0, low, high)
    theirs = jnp.where(x_bit == 0, high, low).astype(bf16)
    return mine + swap_x(theirs).astype(f32)


def gather_row(shard):
    count = lax.axis_size("row")
    index = lax.axis_index("row")
    size = shard.shape[0]
    half = size // 2
    whole = jnp.zeros((count * size,) + shard.shape[1:], shard.dtype)

    def put(whole, piece, owner, extra):
        start = (owner % count) * size + extra
        return lax.dynamic_update_slice_in_dim(whole, piece, start, 0)

    whole = put(whole, shard, index, 0)
    from_left = from_right = shard
    for step in range(1, count // 2):
        from_left = ring(from_left, "row", 1)
        from_right = ring(from_right, "row", -1)
        whole = put(whole, from_left, index - step + count, 0)
        whole = put(whole, from_right, index + step, 0)
    from_left = ring(from_left[:half], "row", 1)
    from_right = ring(from_right[half:], "row", -1)
    whole = put(whole, from_left, index + count // 2, 0)
    return put(whole, from_right, index + count // 2, half)


def scatter_seq_row(partial):
    seq_count, row_count = lax.axis_size("seq"), lax.axis_size("row")
    if seq_count != 2 or row_count != 4:
        return lax.psum_scatter(
            partial.astype(f32), ("seq", "row"), scatter_dimension=0, tiled=True
        )
    seq_index, row_index = lax.axis_index("seq"), lax.axis_index("row")
    half = partial.shape[0] // 2
    chunk = half // 4
    cut = partial.shape[1] // 256 * 128
    theirs = lax.dynamic_slice_in_dim(partial, (1 - seq_index) * half, half, 0)
    mine = lax.dynamic_slice_in_dim(partial, seq_index * half, half, 0)
    received = lax.ppermute(theirs, "seq", [(0, 1), (1, 0)])
    summed = mine.astype(f32) + received.astype(f32)

    def of(offset):
        return lax.dynamic_slice_in_dim(summed, (row_index + offset) % 4 * chunk, chunk, 0)

    far = of(2).astype(bf16)
    right_one = ring(far[:, :cut], "row", 1)
    left_one = ring(far[:, cut:], "row", -1)
    to_right, to_left = of(1), of(3)
    to_right = jnp.concatenate(
        [to_right[:, :cut] + right_one.astype(f32), to_right[:, cut:]], axis=1
    )
    to_left = jnp.concatenate([to_left[:, :cut], to_left[:, cut:] + left_one.astype(f32)], axis=1)
    right_two = ring(to_right.astype(bf16), "row", 1)
    left_two = ring(to_left.astype(bf16), "row", -1)
    return of(0) + right_two.astype(f32) + left_two.astype(f32)


def combine_axis(array, axis, join):
    total = array
    for shift in range(1, lax.axis_size(axis)):
        total = join(total, ring(array, axis, shift))
    return total


def norm_stats(values):
    mean = jnp.mean(values, axis=-1, keepdims=True)
    center = values - mean
    spread = jnp.mean(center * center, axis=-1, keepdims=True)
    return mean, lax.rsqrt(spread + norm_eps)


def gelu_exact(values):
    return jax.nn.gelu(values, approximate=False)


def on_device(
    tokens,
    prefix,
    ln1_gain,
    ln1_bias,
    w_qkv,
    b_qv,
    w_out,
    b_out,
    ln2_gain,
    ln2_bias,
    w_up,
    b_up,
    w_down,
    b_down,
    cotangent,
):
    seq_count = lax.axis_size("seq")
    row_count = lax.axis_size("row")
    col_count = lax.axis_size("col")
    seq_index = lax.axis_index("seq")
    col_index = lax.axis_index("col")
    x_bit = col_index // 2
    core_bit = col_index % 2
    span = tokens.shape[1]
    part = tokens.shape[2]
    full = part * col_count
    quarter = span // col_count
    slots = (H + col_count - 1) // col_count
    width = slots * E
    spare = width - part
    fewer = H // col_count
    head_first = jnp.where(col_index == 0, 0, 1 + fewer * col_index)
    head_count = jnp.where(col_index == 0, fewer + 1, fewer)
    column_shift = head_first * E - col_index * part
    info = jnp.stack([prefix[0], seq_index * span])

    next_to_here = [(i + 1, i) for i in range(col_count - 1)]
    here_to_next = [(i, i + 1) for i in range(col_count - 1)]
    slot_column = lax.broadcasted_iota(jnp.int32, (1, 3 * width), 1)
    slot_part, slot_index = slot_column // width, slot_column % width
    slot_source = jnp.where(slot_index < head_count * E, slot_index + column_shift, -1)
    own_row = lax.broadcasted_iota(jnp.int32, (3 * part, 1), 0)
    pick_own = ((own_row // part == slot_part) & (own_row % part == slot_source)).astype(bf16)
    next_row = lax.broadcasted_iota(jnp.int32, (3 * spare, 1), 0)
    pick_next = (
        (next_row // spare == slot_part) & (next_row % spare + part == slot_source)
    ).astype(bf16)
    qkv_edge = lax.ppermute(w_qkv[:, :, :spare], "col", next_to_here)
    w_heads_shard = (
        dot_nn(w_qkv.reshape(-1, 3 * part), pick_own)
        + dot_nn(qkv_edge.reshape(-1, 3 * spare), pick_next)
    ).astype(bf16)
    bias_own = jnp.concatenate([b_qv[0], jnp.zeros_like(b_qv[0]), b_qv[1]])[None]
    bias_edge = lax.ppermute(bias_own.reshape(3, part)[:, :spare], "col", next_to_here)
    bias_heads = dot_nn(bias_own, pick_own) + dot_nn(bias_edge.reshape(1, 3 * spare), pick_next)
    w_heads = gather_row(w_heads_shard)
    w_queries, w_keyvals = w_heads[:, :width], w_heads[:, width:]

    x_shard = tokens[0]
    x_full = jnp.concatenate(gather_col(x_shard, x_bit, core_bit), axis=1).astype(f32)
    vectors = jnp.stack([ln1_gain, ln1_bias, ln2_gain, ln2_bias])
    vectors = jnp.concatenate(gather_col(vectors, x_bit, core_bit), axis=1).astype(f32)
    gain_one, bias_one, gain_two, bias_two = (vectors[i] for i in range(4))

    def first_norm(values):
        mean, inv = norm_stats(values)
        return mean, inv, ((values - mean) * inv * gain_one + bias_one).astype(bf16)

    mean_one, inv_one, normed_one = first_norm(x_full)
    queries = (
        (dot_nn(normed_one, w_queries) + bias_heads[:, :width]).astype(bf16) * E ** (-0.5)
    ).astype(bf16)
    keyvals = (dot_nn(normed_one, w_keyvals) + bias_heads[:, width:]).astype(bf16)
    if seq_count == 2:
        x_before = lax.ppermute(x_shard, "seq", [(0, 1)])
        x_before = jnp.concatenate(gather_col(x_before, x_bit, core_bit), axis=1).astype(f32)
        normed_before = first_norm(x_before)[2]
        before = (dot_nn(normed_before, w_keyvals) + bias_heads[:, width:]).astype(bf16)
        kv_all = jnp.concatenate(
            [jnp.where(seq_index == 0, keyvals, before), jnp.where(seq_index == 0, before, keyvals)]
        )
    else:
        kv_all = lax.all_gather(keyvals, "seq", axis=0, tiled=True)

    w_out_all = gather_row(w_out)
    w_up_all = gather_row(w_up)
    w_down_t = gather_row(w_down.T)
    dy_full = jnp.concatenate(gather_col(cotangent[0], x_bit, core_bit), axis=1)

    attn_low, attn_exact, lse, tops = attn_fwd(info, queries, kv_all, slots)
    attn_all = jnp.concatenate(gather_col(attn_low, x_bit, core_bit), axis=1)
    lead = (fewer + 1) * E
    blocks = [w_out_all[:lead]]
    for device in range(1, col_count):
        first = (1 + fewer * device) * E
        blocks.append(
            jnp.pad(w_out_all[first : first + fewer * E], ((0, width - fewer * E), (0, 0)))
        )
    w_out_heads = jnp.concatenate(blocks)
    after_attn = x_full + dot_nn(attn_all, w_out_heads) + b_out.astype(f32)

    slot_head = jnp.arange(slots, dtype=jnp.int32)
    my_top = jnp.where(slot_head < head_count, tops[:slots, 0], neg_fill)
    head_ids = jnp.arange(H, dtype=jnp.int32)
    placed_top = jnp.max(
        jnp.where(
            head_ids[None] == (head_first + slot_head)[:, None], my_top[:, None], neg_fill
        ),
        axis=0,
    )[None]
    head_max = placed_top
    for axis in ("seq", "row", "col"):
        head_max = combine_axis(head_max, axis, jnp.maximum)
    head_max = head_max[0]

    mean_two, inv_two = norm_stats(after_attn)
    normed_two = ((after_attn - mean_two) * inv_two * gain_two + bias_two).astype(bf16)
    pre_act = dot_nn(normed_two, w_up_all) + b_up.astype(f32)
    act_low = gelu_exact(pre_act).astype(bf16)
    grad_act = dot_nn(dy_full, w_down_t)
    grad_pre = jax.vjp(gelu_exact, pre_act)[1](grad_act)[0].astype(bf16)
    normed_two_part = dot_nt(grad_pre, w_up_all).astype(bf16)
    back_two = scatter_col(
        [normed_two_part[i * quarter : (i + 1) * quarter] for i in range(col_count)],
        x_bit,
        core_bit,
    )
    down_part = dot_nt(act_low, w_down_t).astype(bf16)
    down_mine = scatter_col(
        [down_part[:, i * part : (i + 1) * part] for i in range(col_count)], x_bit, core_bit
    )

    def own_columns(array):
        picked = array[:, :part]
        for i in range(1, col_count):
            picked = jnp.where(col_index == i, array[:, i * part : (i + 1) * part], picked)
        return picked

    block_out = (own_columns(after_attn) + down_mine + b_down.astype(f32)).astype(bf16)[None]

    def own_rows(array):
        return lax.dynamic_slice_in_dim(array, col_index * quarter, quarter, 0)

    unit_two = (own_rows(after_attn) - own_rows(mean_two)) * own_rows(inv_two)
    unit_grad = back_two * gain_two
    grad_after = own_rows(dy_full).astype(f32) + own_rows(inv_two) * (
        unit_grad
        - jnp.mean(unit_grad, axis=1, keepdims=True)
        - unit_two * jnp.mean(unit_grad * unit_two, axis=1, keepdims=True)
    )
    grad_branch_rows = grad_after.astype(bf16)
    grad_branch = jnp.concatenate(gather_col(grad_branch_rows, x_bit, core_bit), axis=0)
    row_vectors = jnp.stack(
        [
            jnp.sum(back_two * unit_two, axis=0),
            jnp.sum(back_two, axis=0),
            jnp.sum(grad_branch_rows.astype(f32), axis=0),
        ]
    )
    row_vectors = row_vectors + swap_x(row_vectors)
    row_vectors = row_vectors + swap_core(row_vectors)

    grad_w_up = scatter_seq_row(dot_tn(normed_two, grad_pre).astype(bf16))
    grad_w_down = scatter_seq_row(dot_tn(dy_full, act_low).astype(bf16)).T

    w_out_mine = lax.dynamic_slice_in_dim(w_out_heads, col_index * width, width, 0)
    grad_attn = dot_nt(grad_branch, w_out_mine).astype(bf16)
    row_dot = jnp.sum(
        (grad_attn.astype(f32) * attn_exact).reshape(span, slots, E), axis=-1
    )
    dot_rows = jnp.pad(row_dot, ((0, 0), (0, 8 - slots))).T
    lse_rows = lse.T
    if seq_count == 2:
        dq_one, dkv_one = attn_bwd(
            info, queries, kv_all, grad_attn, lse_rows, dot_rows, slots, 0
        )
        dkv_there = lax.ppermute(dkv_one.astype(bf16), "seq", [(1, 0)])
        dq_two, dkv_two = attn_bwd(
            info, queries, kv_all, grad_attn, lse_rows, dot_rows, slots, 1
        )
        grad_queries = dq_one + dq_two
        grad_keyvals = jnp.where(seq_index == 0, dkv_one + dkv_there.astype(f32), dkv_two)
    else:
        grad_queries = 0.0
        pieces = []
        for segment in range(seq_count):
            dq_one, dkv_one = attn_bwd(
                info, queries, kv_all, grad_attn, lse_rows, dot_rows, slots, segment
            )
            grad_queries = grad_queries + dq_one
            pieces.append(dkv_one.astype(bf16))
        grad_keyvals = lax.psum_scatter(
            jnp.concatenate(pieces), "seq", scatter_dimension=0, tiled=True
        ).astype(f32)
    grad_heads = jnp.concatenate([grad_queries * E ** (-0.5), grad_keyvals], axis=1).astype(bf16)

    wide = dot_tn(attn_all, own_columns(grad_branch)).astype(bf16)
    rows_kept = [wide[:lead]]
    for device in range(1, col_count):
        rows_kept.append(wide[device * width : device * width + fewer * E])
    out_columns = scatter_seq_row(jnp.concatenate(rows_kept)).astype(bf16)
    grad_w_out = jnp.concatenate(gather_col(out_columns, x_bit, core_bit), axis=1).astype(f32)

    normed_one_part = dot_nt(grad_heads, w_heads).astype(bf16)
    back_one = scatter_col(
        [normed_one_part[:, i * part : (i + 1) * part] for i in range(col_count)],
        x_bit,
        core_bit,
    )
    grad_edge = dot_nt(grad_heads, pick_next).astype(bf16)
    edge = lax.ppermute(dot_tn(normed_one, grad_edge).astype(bf16), "col", here_to_next)
    grad_own = dot_nt(grad_heads, pick_own).astype(bf16)
    bias_grads = jnp.sum(grad_own.astype(f32), axis=0)[None]
    bias_more = lax.ppermute(
        jnp.sum(grad_edge.astype(f32), axis=0)[None], "col", here_to_next
    )

    def widen(narrow):
        return jnp.concatenate(
            [
                jnp.pad(narrow[:, i * spare : (i + 1) * spare], ((0, 0), (0, part - spare)))
                for i in range(3)
            ],
            axis=1,
        )

    qkv_partial = (dot_tn(normed_one, grad_own) + widen(edge).astype(f32)).astype(bf16)
    bias_grads = bias_grads + widen(bias_more)
    grad_w_qkv = scatter_seq_row(qkv_partial).reshape(-1, 3, part)

    unit_one = (x_shard.astype(f32) - mean_one) * inv_one
    unit_grad_one = back_one * ln1_gain.astype(f32)
    sums = jnp.stack(
        [jnp.sum(unit_grad_one, axis=1), jnp.sum(unit_grad_one * unit_one, axis=1)]
    )
    sums = sums + swap_x(sums)
    sums = (sums + swap_core(sums)) / full
    grad_tokens = (
        own_columns(grad_branch).astype(f32)
        + inv_one * (unit_grad_one - sums[0][:, None] - unit_one * sums[1][:, None])
    )[None]

    own_vectors = own_columns(row_vectors)
    small = jnp.concatenate(
        [
            jnp.sum(back_one * unit_one, axis=0),
            jnp.sum(back_one, axis=0),
            own_vectors[0],
            own_vectors[1],
            bias_grads[0, :part],
            bias_grads[0, 2 * part :],
            jnp.sum(cotangent[0].astype(f32), axis=0),
            jnp.sum(grad_pre.astype(f32), axis=0),
            row_vectors[2],
        ]
    )[None]
    for axis in ("seq", "row"):
        small = combine_axis(small, axis, jnp.add)
    small = small[0]

    def piece(start, length):
        return small[start : start + length]

    root_clip = jnp.sqrt(clip_limit / jnp.maximum(head_max, clip_limit))
    column_head = (col_index * part + jnp.arange(part, dtype=jnp.int32)) // E
    one_hot = (column_head[:, None] == head_ids[None, :]).astype(f32)
    column_root = jnp.sum(one_hot * root_clip[None, :], axis=1)
    scale_three = jnp.stack([column_root, column_root, jnp.ones_like(column_root)])
    clipped_qkv = w_qkv.astype(f32) * scale_three[None]
    return (
        block_out,
        grad_tokens,
        piece(0, part),
        piece(part, part),
        grad_w_qkv,
        jnp.stack([piece(4 * part, part), piece(5 * part, part)]),
        grad_w_out,
        piece(11 * part, full),
        piece(2 * part, part),
        piece(3 * part, part),
        grad_w_up,
        piece(7 * part, w_up.shape[1]),
        grad_w_down,
        piece(6 * part, part),
        clipped_qkv,
        head_max,
    )


def solution(mesh):
    placed = (
        P("row", "seq", "col"),
        P("row"),
        P("col"),
        P("col"),
        P("row", None, "col"),
        P(None, "col"),
        P("row", None),
        P(),
        P("col"),
        P("col"),
        P("row", "col"),
        P("col"),
        P("col", "row"),
        P("col"),
        P("row", "seq", "col"),
    )
    return jax.shard_map(
        on_device,
        mesh=mesh,
        in_specs=placed,
        out_specs=(
            P("row", "seq", "col"),
            P("row", "seq", "col"),
            P("col"),
            P("col"),
            P(("seq", "row"), None, "col"),
            P(None, "col"),
            P(("seq", "row"), None),
            P(),
            P("col"),
            P("col"),
            P(("seq", "row"), "col"),
            P("col"),
            P("col", ("seq", "row")),
            P("col"),
            P("row", None, "col"),
            P(),
        ),
        check_vma=False,
    )
```

time: 1460 us -> 634 us (0.43)
  waiting for transfers between devices: 972 us -> 243 us
  starting transfers between devices: 4.89 us -> 133 us
  blocking collectives: 102 us -> 0 us
  matrix products: 157 us -> 77.1 us
  Pallas kernels: 0 us -> 50.1 us
  loops' own time: 38.9 us -> 0 us
  local copies, waits for them, and re-layouts: 91.2 us -> 62.8 us
    unnamed x21 -> x0, waiting for transfers between devices: 330 us -> none
    all_gather x8 -> x0, waiting for transfers between devices: 281 us -> none  [the longest x1 64.5 us: on_device(): lax.all_gather(w_qkv, 'row', axis=0, tiled=True)]
    ppermute x0 -> x87, waiting for transfers between devices: none -> 243 us  [the longest x43 123 us: ring(): lax.ppermute(array, axis, [(i, (i + shift) % count) for i in range(count)])]
    reduce_scatter x3 -> x0, waiting for transfers between devices: 202 us -> none  [the longest x1 103 us: on_device(): lax.psum_scatter(grad_wqkv, ('seq', 'row'), scatter_dimension=0, tiled=True)]
    psum x2 -> x0, waiting for transfers between devices: 134 us -> none  [the longest x1 81.9 us: on_device(): lax.psum(grad_normed_one.astype(jnp.bfloat16), 'col').astype(jnp.float32)]
    ppermute x0 -> x87, starting transfers between devices: none -> 133 us  [the longest x43 82.1 us: ring(): lax.ppermute(array, axis, [(i, (i + shift) % count) for i in range(count)])]
    dot_general x29 -> x21, matrix products: 157 us -> 77.1 us  [the longest x10 43.7 us: dot_nn(): lax.dot_general(left, right, (((1,), (0,)), ((), ())), preferred_element_...]
    pallas_call x0 -> x3, Pallas kernels: none -> 50.1 us  [the longest x2 27 us: attn_bwd(): pl.pallas_call(functools.partial(attn_bwd_body, slots, rows, keys, segmen...]
  transfers between devices with their start and end apart: 18 -> 87, of which waited for: 16 -> 36; matrix products, arithmetic and copies ran while one was open for 13% -> 17% of each run, Pallas kernels for 0% -> 0%
where the time goes in v1:
time: 634 us; the launch traced here: 627 us
  waiting for transfers between devices  243 us (38%)
  starting transfers between devices  133 us (21%)
  matrix products  77.1 us (12%)
  local copies, waits for them, and re-layouts  62.8 us (10%)
  other arithmetic  56.7 us (9%)
  Pallas kernels  50.1 us (8%)
    ppermute x43, waiting for transfers between devices, ring(): lax.ppermute(array, axis, [(i, (i + shift) % count) for i in range(count)])  123 us
    ppermute x43, starting transfers between devices, ring(): lax.ppermute(array, axis, [(i, (i + shift) % count) for i in range(count)])  82.1 us
    dot_general x10, matrix products, dot_nn(): lax.dot_general(left, right, (((1,), (0,)), ((), ())), preferred_element_...  43.7 us
    ppermute x12, waiting for transfers between devices, swap_x(): return lax.ppermute(array, 'col', X_SWAP)  43.7 us
    ppermute x4, waiting for transfers between devices, scatter_seq_row(): received = lax.ppermute(theirs, 'seq', [(0, 1), (1, 0)])  39.9 us
    ppermute x1, waiting for transfers between devices, on_device(): dkv_there = lax.ppermute(dkv_one.astype(bf16), 'seq', [(1, 0)])  31.5 us
    pallas_call x2, Pallas kernels, attn_bwd(): pl.pallas_call(functools.partial(attn_bwd_body, slots, rows, keys, segmen...  27 us
    pallas_call x1, Pallas kernels, attn_fwd(): pl.pallas_call(functools.partial(attn_fwd_body, slots, rows, keys), grid_...  23.1 us
  transfers between devices with their start and end apart: 87, of which 36 were waited for; matrix products, arithmetic and copies ran while one was open for 17% of the time, Pallas kernels for 0%

profile of v1, /device:TPU:0, one launch (start us, length us, event | category | flops | bytes accessed | tf_op | source)
XLA Modules:
  0.0 626.7 jit_solution(2424052369969397196)
XLA Ops:
  0.7 3.1 collective-permute-start.27
  35.1 8.7 %collective-permute-start.34 = (bf16[1024,272]{0,1:T(8,128)(2,1)}, bf16[1024,272]{0,1:T(8,128)(2,1)S(1)}, u32[]{:S(2)}, u32[]{:S(2)}) collective-permute-start(bf16[1024,272]{0,1:T(8,128)(2,1)} %bitcast.71), channel_id=1, source_target_pairs={{0,2},{2,0},{1,3},{3,1},{4,6},{6,4},{5,7},{7,5},{8,10},{10,8},{9,1... | collective-permute-start | bytes 1671176 | tf_op jit(solution)/shard_map/ppermute | solution.py:218
  44.7 3.9 collective-permute-start.24
  49.7 7.4 %collective-permute-done.34 = bf16[1024,272]{0,1:T(8,128)(2,1)S(1)} collective-permute-done((bf16[1024,272]{0,1:T(8,128)(2,1)}, bf16[1024,272]{0,1:T(8,128)(2,1)S(1)}, u32[]{:S(2)}, u32[]{:S(2)}) %collective-permute-start.34) | collective-permute-done | bytes 557088 | tf_op jit(solution)/shard_map/ppermute | solution.py:218
  58.6 3.5 collective-permute-start.12
  64.0 2.5 collective-permute-start.20
  68.5 8.6 %collective-permute-done.19 = bf16[272,1088]{1,0:T(8,128)(2,1)S(1)} collective-permute-done((bf16[272,1088]{1,0:T(8,128)(2,1)S(1)}, bf16[272,1088]{1,0:T(8,128)(2,1)S(1)}, u32[]{:S(2)}, u32[]{:S(2)}) %collective-permute-start.19) | collective-permute-done | bytes 591904 | tf_op jit(solution)/shard_map/ppermute | solution.py:227
  84.1 18.5 %collective-permute-done.7 = bf16[272,960]{1,0:T(8,128)(2,1)S(1)} collective-permute-done((bf16[272,960]{1,0:T(8,128)(2,1)S(1)}, bf16[272,960]{1,0:T(8,128)(2,1)S(1)}, u32[]{:S(2)}, u32[]{:S(2)}) %collective-permute-start.7) | collective-permute-done | bytes 522272 | tf_op jit(solution)/shard_map/ppermute | solution.py:227
  109.1 5.2 collective-permute-done.8
  114.3 4.0 collective-permute-start.10
  118.4 8.8 %collective-permute-done.9 = bf16[136,960]{1,0:T(8,128)(2,1)S(1)} collective-permute-done((bf16[136,960]{1,0:T(8,128)(2,1)S(1)}, bf16[136,960]{1,0:T(8,128)(2,1)S(1)}, u32[]{:S(2)}, u32[]{:S(2)}) %collective-permute-start.9) | collective-permute-done | bytes 261152 | tf_op jit(solution)/shard_map/ppermute | solution.py:227
  127.2 5.8 collective-permute-done.10
  133.0 3.6 collective-permute-start.22
  136.8 7.7 %collective-permute-done.22 = bf16[136,1088]{1,0:T(8,128)(2,1)S(1)} collective-permute-done((bf16[136,1088]{1,0:T(8,128)(2,1)S(1)}, bf16[136,1088]{1,0:T(8,128)(2,1)S(1)}, u32[]{:S(2)}, u32[]{:S(2)}) %collective-permute-start.22) | collective-permute-done | bytes 295968 | tf_op jit(solution)/shard_map/ppermute | solution.py:227
  144.4 4.4 collective-permute-start.30
  149.1 8.3 %fusion.29 = bf16[1280,1088]{1,0:T(8,128)(2,1)} fusion(bf16[256,1088]{1,0:T(8,128)(2,1)S(1)} %get-tuple-element.134, bf16[256,1088]{1,0:T(8,128)(2,1)S(1)} %get-tuple-element.135, bf16[256,1088]{1,0:T(8,128)(2,1)S(1)} %get-tuple-element.133, bf16[320,1088]{1,0:T(8,128)(2,1)S(1)} %slice.449), kind=kLoop, calls=%fused_computation.66 | loop fusion | flops 25067520 | bytes 5152768 | tf_op jit(solution)/shard_map/concatenate | solution.py:428
  158.3 3.9 collective-permute-start.26
  162.9 6.7 %collective-permute-done.25 = bf16[136,1088]{1,0:T(8,128)(2,1)S(1)} collective-permute-done((bf16[136,1088]{1,0:T(8,128)(2,1)S(1)}, bf16[136,1088]{1,0:T(8,128)(2,1)S(1)}, u32[]{:S(2)}, u32[]{:S(2)}) %collective-permute-start.25) | collective-permute-done | bytes 295968 | tf_op jit(solution)/shard_map/ppermute | solution.py:227
  175.0 12.4 %collective-permute-done.13 = bf16[1024,272]{0,1:T(8,128)(2,1)S(1)} collective-permute-done((bf16[1024,272]{0,1:T(8,128)(2,1)S(1)}, bf16[1024,272]{0,1:T(8,128)(2,1)S(1)}, u32[]{:S(2)}, u32[]{:S(2)}) %collective-permute-start.13) | collective-permute-done | bytes 557088 | tf_op jit(solution)/shard_map/ppermute | solution.py:218
  189.0 2.5 fusion.13
  196.5 2.7 add_convert_fusion.3
  199.2 2.6 broadcast_select_fusion.1
  203.6 23.1 %attn_fwd.1 = (bf16[1024,320]{1,0:T(8,128)(2,1)S(1)}, f32[1024,320]{1,0:T(8,128)S(1)}, f32[1024,8]{1,0:T(8,128)S(1)}, f32[8,128]{1,0:T(8,128)S(1)}) custom-call(s32[2]{0:T(128)S(1)} %pad_add_fusion.info, bf16[1024,320]{1,0:T(8,128)(2,1)S(1)} %fusion.58.q_ref, bf16[2048,640]{1,0:T(8,128)(2,1)} %pad_maximum_fusion.kv_ref), custom_call_target="tpu_custom_call" | custom-call | flops 20000000000 | bytes 8000000 | tf_op jit(solution)/shard_map/attn_fwd/pallas_call | solution.py:105
  228.3 15.3 %collective-permute-start.80 = (f32[1,17]{1,0:T(1,128)S(1)}, f32[1,17]{1,0:T(1,128)S(1)}, u32[]{:S(2)}, u32[]{:S(2)}) collective-permute-start(f32[1,17]{1,0:T(1,128)S(1)} %bitcast.92), channel_id=1, source_target_pairs={{0,16},{16,0},{1,17},{17,1},{2,18},{18,2},{3,19},{19,3},{4,20},{20... | collective-permute-start | bytes 212 | tf_op jit(solution)/shard_map/ppermute | solution.py:227
  267.2 2.8 broadcast_select_fusion.6
  274.7 5.8 concatenate.92
  280.5 8.5 %fusion.137 = (f32[1024]{0:T(1024)S(1)}, f32[1024,1088]{0,1:T(8,128)S(1)}) fusion(f32[1088]{0:T(1024)S(1)} %convert_element_type.309, bf16[1024,1280]{1,0:T(8,128)(2,1)} %concatenate.92, bf16[256,1088]{1,0:T(8,128)(2,1)} %copy-done.15, bf16[256,1088]{1,0:T(8,128)(2,1)} %copy-done.16, bf16[256,1088]{1,0:T(8,128)(2,1)} %copy-done.14, ...), kind=kOutput, calls=%fused_computation.402 | convolution fusion | flops 2889448448 | bytes 11682048 | tf_op jit(solution)/shard_map/dot_general | solution.py:22
  289.8 17.0 %multiply_convert_fusion = (bf16[1024,1088]{0,1:T(8,128)(2,1)S(1)}, f32[1024,1088]{0,1:T(8,128)S(1)}, f32[1024,1088]{0,1:T(8,128)}) fusion(f32[1088]{0:T(1024)S(1)} %convert_element_type.311, bf16[1088,1088]{1,0:T(8,128)(2,1)} %constant_dynamic-update-slice_fusion.5, f32[1024,1088]{0,1:T(8,128)S(1)} %get-tuple-element.204, ...), kind=kOutput, calls=%fused_computation.37 | convolution fusion | flops 2503409664 | bytes 17986304 | tf_op jit(solution)/shard_map/dot_general | solution.py:22
  306.8 7.4 %convert_reduce_fusion.2 = (f32[1088]{0:T(1024)S(1)}, bf16[1024,1088]{0,1:T(8,128)(2,1)S(1)}) fusion(f32[1024,1088]{0,1:T(8,128)S(1)} %get-tuple-element.130, f32[1024,1088]{0,1:T(8,128)} %get-tuple-element.205, bf16[1088,1088]{1,0:T(8,128)(2,1)} %constant_dynamic-update-slice_fusion, bf16[1024,272]{0,1:T(8,128)(2,1)S(1)} %copy-done.21, ...), kind=kOutput, calls=%fused_computation.35 | convolution fusion | flops 2451045376 | bytes 15741184 | tf_op jit(solution)/shard_map/dot_general | solution.py:22
  314.2 5.0 convolution_convert_fusion.3
  319.2 3.7 convolution_convert_fusion.1
  323.0 5.0 convolution_convert_fusion.4
  329.4 5.5 convolution_convert_fusion
  337.0 4.4 collective-permute-start.70
  343.9 6.9 %collective-permute-done.39 = bf16[256,1088]{0,1:T(8,128)(2,1)S(1)} collective-permute-done((bf16[256,1088]{0,1:T(8,128)(2,1)S(1)}, bf16[256,1088]{0,1:T(8,128)(2,1)S(1)}, u32[]{:S(2)}, u32[]{:S(2)}) %collective-permute-start.39) | collective-permute-done | bytes 557088 | tf_op jit(solution)/shard_map/ppermute | solution.py:218
  355.3 4.5 collective-permute-start.75
  365.4 4.4 collective-permute-done.70
  370.1 25.7 %collective-permute-done.75 = bf16[544,1088]{1,0:T(8,128)(2,1)S(1)} collective-permute-done((bf16[544,1088]{1,0:T(8,128)(2,1)S(1)}, bf16[544,1088]{1,0:T(8,128)(2,1)S(1)}, u32[]{:S(2)}, u32[]{:S(2)}) %collective-permute-start.75) | collective-permute-done | bytes 1183776 | tf_op jit(solution)/shard_map/ppermute | solution.py:292
  398.3 2.6 collective-permute-start.78
  401.0 5.0 collective-permute-done.71
  407.5 5.4 collective-permute-done.76
  414.3 2.7 collective-permute-start.74
  416.9 6.7 %collective-permute-done.78 = bf16[136,576]{1,0:T(8,128)(2,1)S(1)} collective-permute-done((bf16[136,576]{1,0:T(8,128)(2,1)S(1)}, bf16[136,576]{1,0:T(8,128)(2,1)S(1)}, u32[]{:S(2)}, u32[]{:S(2)}) %collective-permute-start.78) | collective-permute-done | bytes 156704 | tf_op jit(solution)/shard_map/ppermute | solution.py:227
  424.0 7.7 %collective-permute-done.74 = bf16[136,1088]{1,0:T(8,128)(2,1)S(1)} collective-permute-done((bf16[136,1088]{1,0:T(8,128)(2,1)S(1)}, bf16[136,1088]{1,0:T(8,128)(2,1)S(1)}, u32[]{:S(2)}, u32[]{:S(2)}) %collective-permute-start.74) | collective-permute-done | bytes 295968 | tf_op jit(solution)/shard_map/ppermute | solution.py:227
  432.8 5.6 collective-permute-done.79
  439.5 3.0 convolution_convert_fusion.7.do_ref
  443.8 3.0 copy.77
  448.4 24.6 %attn_bwd.2 = (f32[1024,320]{1,0:T(8,128)S(1)}, f32[1024,640]{1,0:T(8,128)S(1)}) custom-call(s32[2]{0:T(128)S(1)} %pad_add_fusion.info, bf16[1024,320]{1,0:T(8,128)(2,1)S(1)} %copy-done.1, bf16[2048,640]{1,0:T(8,128)(2,1)} %pad_maximum_fusion.kv_ref, bf16[1024,320]{1,0:T(8,128)(2,1)S(1)} %convolution_convert_fusion.7.do_ref, f32[8,1024]{1,0:T(8,128)S(1)} %bitcast.65, ...), custom_call_target="tpu_custom_call" | custom-call | flops 24999999488 | bytes 8000000 | tf_op jit(solution)/shard_map/attn_bwd/pallas_call | solution.py:187
  474.4 2.5 attn_bwd.3
  478.4 31.5 %collective-permute-done.43 = bf16[1024,640]{1,0:T(8,128)(2,1)S(1)} collective-permute-done((bf16[1024,640]{1,0:T(8,128)(2,1)S(1)}, bf16[1024,640]{1,0:T(8,128)(2,1)S(1)}, u32[]{:S(2)}, u32[]{:S(2)}) %collective-permute-start.43) | collective-permute-done | bytes 1310752 | tf_op jit(solution)/shard_map/ppermute | solution.py:506
  511.5 2.5 convolution_convert_fusion.2
  520.9 3.6 collective-permute-start.56
  525.6 14.5 %collective-permute-done.46 = bf16[1024,272]{0,1:T(8,128)(2,1)S(1)} collective-permute-done((bf16[1024,272]{0,1:T(8,128)(2,1)S(1)}, bf16[1024,272]{0,1:T(8,128)(2,1)S(1)}, u32[]{:S(2)}, u32[]{:S(2)}) %collective-permute-start.46) | collective-permute-done | bytes 557088 | tf_op jit(solution)/shard_map/ppermute | solution.py:218
  543.0 3.7 add_convert_fusion.2
  548.2 2.7 constant_dynamic-slice_fusion.3
  558.0 3.1 add_bitcast_fusion
  568.0 9.9 %collective-permute-done.57 = bf16[544,816]{1,0:T(8,128)(2,1)} collective-permute-done((bf16[544,816]{1,0:T(8,128)(2,1)}, bf16[544,816]{1,0:T(8,128)(2,1)}, u32[]{:S(2)}, u32[]{:S(2)}) %collective-permute-start.57) | collective-permute-done | bytes 887840 | tf_op jit(solution)/shard_map/ppermute | solution.py:292
  583.0 7.7 %collective-permute-done.58 = bf16[136,384]{0,1:T(8,128)(2,1)S(1)} collective-permute-done((bf16[136,384]{0,1:T(8,128)(2,1)S(1)}, bf16[136,384]{0,1:T(8,128)(2,1)S(1)}, u32[]{:S(2)}, u32[]{:S(2)}) %collective-permute-start.58) | collective-permute-done | bytes 104480 | tf_op jit(solution)/shard_map/ppermute | solution.py:227
  594.6 2.5 collective-permute-start.65
  597.2 7.0 %collective-permute-done.63 = bf16[136,128]{0,1:T(8,128)(2,1)S(1)} collective-permute-done((bf16[136,128]{0,1:T(8,128)(2,1)S(1)}, bf16[136,128]{0,1:T(8,128)(2,1)S(1)}, u32[]{:S(2)}, u32[]{:S(2)}) %collective-permute-start.63) | collective-permute-done | bytes 34848 | tf_op jit(solution)/shard_map/ppermute | solution.py:227
  605.2 3.3 collective-permute-start.66
  608.7 2.8 collective-permute-done.64
  613.8 2.9 collective-permute-start.61
  617.6 4.7 collective-permute-done.61
  (476 shorter events, 172.3 us)
Async XLA Ops:
  0.7 57.9 %collective-permute-start.27 = (bf16[272,1088]{1,0:T(8,128)(2,1)}, bf16[272,1088]{1,0:T(8,128)(2,1)}, u32[]{:S(2)}, u32[]{:S(2)}) collective-permute-start(bf16[272,1088]{1,0:T(8,128)(2,1)} %bitcast.73), channel_id=1, source_target_pairs={{0,4},{4,8},{8,12},{12,0},{1,5},{5,9},{9,13},{13,1},{2,6},{6,10},{... | collective-permute-start | bytes 1775624 | tf_op jit(solution)/shard_map/ppermute | solution.py:227
  3.7 75.4 %collective-permute-start.28 = (bf16[272,1088]{1,0:T(8,128)(2,1)}, bf16[272,1088]{1,0:T(8,128)(2,1)}, u32[]{:S(2)}, u32[]{:S(2)}) collective-permute-start(bf16[272,1088]{1,0:T(8,128)(2,1)} %bitcast.74), channel_id=1, source_target_pairs={{0,12},{4,0},{8,4},{12,8},{1,13},{5,1},{9,5},{13,9},{2,14},{6,2},{... | collective-permute-start | bytes 1775624 | tf_op jit(solution)/shard_map/ppermute | solution.py:227
  5.8 58.2 %collective-permute-start.23 = (bf16[272,1088]{1,0:T(8,128)(2,1)}, bf16[272,1088]{1,0:T(8,128)(2,1)}, u32[]{:S(2)}, u32[]{:S(2)}) collective-permute-start(bf16[272,1088]{1,0:T(8,128)(2,1)} %param.25), channel_id=1, source_target_pairs={{0,4},{4,8},{8,12},{12,0},{1,5},{5,9},{9,13},{13,1},{2,6},{6,10},{... | collective-permute-start | bytes 1775624 | tf_op jit(solution)/shard_map/ppermute | solution.py:227
  8.6 20.9 %collective-permute-start.3 = (bf16[4,272]{1,0:T(4,128)(2,1)S(1)}, bf16[4,272]{1,0:T(4,128)(2,1)S(1)}, u32[]{:S(2)}, u32[]{:S(2)}) collective-permute-start(bf16[4,272]{1,0:T(4,128)(2,1)S(1)} %pad_maximum_fusion.19), channel_id=1, source_target_pairs={{0,2},{2,0},{1,3},{3,1},{4,6},{6,4},{5,7},{7,5},{8,10},{10,8},{9,1... | collective-permute-start | bytes 6536 | tf_op jit(solution)/shard_map/ppermute | solution.py:218
  11.2 16.3 %collective-permute-start.11 = (bf16[3,48]{1,0:T(4,128)(2,1)S(1)}, bf16[3,48]{1,0:T(4,128)(2,1)S(1)}, u32[]{:S(2)}, u32[]{:S(2)}) collective-permute-start(bf16[3,48]{1,0:T(4,128)(2,1)S(1)} %slice.443), channel_id=1, source_target_pairs={{1,0},{2,1},{3,2},{5,4},{6,5},{7,6},{9,8},{10,9},{11,10},{13,12},{... | collective-permute-start | bytes 872 | tf_op jit(solution)/shard_map/ppermute | solution.py:383
  27.6 17.1 %collective-permute-start = (bf16[1024,272]{0,1:T(8,128)(2,1)S(1)}, bf16[1024,272]{0,1:T(8,128)(2,1)}, u32[]{:S(2)}, u32[]{:S(2)}) collective-permute-start(bf16[1024,272]{0,1:T(8,128)(2,1)S(1)} %bitcast.68), channel_id=1, source_target_pairs={{0,2},{2,0},{1,3},{3,1},{4,6},{6,4},{5,7},{7,5},{8,10},{10,8},{9,1... | collective-permute-start | bytes 1671176 | tf_op jit(solution)/shard_map/ppermute | solution.py:218
  35.1 22.1 %collective-permute-start.34 = (bf16[1024,272]{0,1:T(8,128)(2,1)}, bf16[1024,272]{0,1:T(8,128)(2,1)S(1)}, u32[]{:S(2)}, u32[]{:S(2)}) collective-permute-start(bf16[1024,272]{0,1:T(8,128)(2,1)} %bitcast.71), channel_id=1, source_target_pairs={{0,2},{2,0},{1,3},{3,1},{4,6},{6,4},{5,7},{7,5},{8,10},{10,8},{9,1... | collective-permute-start | bytes 1671176 | tf_op jit(solution)/shard_map/ppermute | solution.py:218
  44.7 38.4 %collective-permute-start.24 = (bf16[272,1088]{1,0:T(8,128)(2,1)S(1)}, bf16[272,1088]{1,0:T(8,128)(2,1)S(1)}, u32[]{:S(2)}, u32[]{:S(2)}) collective-permute-start(bf16[272,1088]{1,0:T(8,128)(2,1)S(1)} %copy-done.39), channel_id=1, source_target_pairs={{0,12},{4,0},{8,4},{12,8},{1,13},{5,1},{9,5},{13,9},{2,14},{6,2},{... | collective-permute-start | bytes 1775624 | tf_op jit(solution)/shard_map/ppermute | solution.py:227
  57.1 20.0 %collective-permute-start.19 = (bf16[272,1088]{1,0:T(8,128)(2,1)S(1)}, bf16[272,1088]{1,0:T(8,128)(2,1)S(1)}, u32[]{:S(2)}, u32[]{:S(2)}) collective-permute-start(bf16[272,1088]{1,0:T(8,128)(2,1)S(1)} %copy-done.40), channel_id=1, source_target_pairs={{0,4},{4,8},{8,12},{12,0},{1,5},{5,9},{9,13},{13,1},{2,6},{6,10},{... | collective-permute-start | bytes 1775624 | tf_op jit(solution)/shard_map/ppermute | solution.py:227
  58.6 111.8 %collective-permute-start.12 = (bf16[1024,272]{0,1:T(8,128)(2,1)S(1)}, bf16[1024,272]{0,1:T(8,128)(2,1)S(1)}, u32[]{:S(2)}, u32[]{:S(2)}) collective-permute-start(bf16[1024,272]{0,1:T(8,128)(2,1)S(1)} %bitcast.69), channel_id=1, source_target_pairs={{0,16},{1,17},{2,18},{3,19},{4,20},{5,21},{6,22},{7,23},{8,24},{9,... | collective-permute-start | bytes 1671176 | tf_op jit(solution)/shard_map/ppermute | solution.py:404
  64.0 40.5 %collective-permute-start.20 = (bf16[272,1088]{1,0:T(8,128)(2,1)S(1)}, bf16[272,1088]{1,0:T(8,128)(2,1)S(1)}, u32[]{:S(2)}, u32[]{:S(2)}) collective-permute-start(bf16[272,1088]{1,0:T(8,128)(2,1)S(1)} %copy-done.40), channel_id=1, source_target_pairs={{0,12},{4,0},{8,4},{12,8},{1,13},{5,1},{9,5},{13,9},{2,14},{6,2},{... | collective-permute-start | bytes 1775624 | tf_op jit(solution)/shard_map/ppermute | solution.py:227
  77.1 25.4 %collective-permute-start.7 = (bf16[272,960]{1,0:T(8,128)(2,1)S(1)}, bf16[272,960]{1,0:T(8,128)(2,1)S(1)}, u32[]{:S(2)}, u32[]{:S(2)}) collective-permute-start(bf16[272,960]{1,0:T(8,128)(2,1)S(1)} %get-tuple-element.202), channel_id=1, source_target_pairs={{0,4},{4,8},{8,12},{12,0},{1,5},{5,9},{9,13},{13,1},{2,6},{6,10},{... | collective-permute-start | bytes 1566728 | tf_op jit(solution)/shard_map/ppermute | solution.py:227
  79.1 35.1 %collective-permute-start.8 = (bf16[272,960]{1,0:T(8,128)(2,1)S(1)}, bf16[272,960]{1,0:T(8,128)(2,1)S(1)}, u32[]{:S(2)}, u32[]{:S(2)}) collective-permute-start(bf16[272,960]{1,0:T(8,128)(2,1)S(1)} %get-tuple-element.202), channel_id=1, source_target_pairs={{0,12},{4,0},{8,4},{12,8},{1,13},{5,1},{9,5},{13,9},{2,14},{6,2},{... | collective-permute-start | bytes 1566728 | tf_op jit(solution)/shard_map/ppermute | solution.py:227
  83.1 91.3 %collective-permute-start.2 = (bf16[1024,272]{0,1:T(8,128)(2,1)S(1)}, bf16[1024,272]{0,1:T(8,128)(2,1)S(1)}, u32[]{:S(2)}, u32[]{:S(2)}) collective-permute-start(bf16[1024,272]{0,1:T(8,128)(2,1)S(1)} %get-tuple-element.169), channel_id=1, source_target_pairs={{0,1},{1,0},{2,3},{3,2},{4,5},{5,4},{6,7},{7,6},{8,9},{9,8},{10,11... | collective-permute-start | bytes 1671176 | tf_op jit(solution)/shard_map/ppermute | solution.py:222
  102.5 34.1 %collective-permute-start.21 = (bf16[136,1088]{1,0:T(8,128)(2,1)S(1)}, bf16[136,1088]{1,0:T(8,128)(2,1)S(1)}, u32[]{:S(2)}, u32[]{:S(2)}) collective-permute-start(bf16[136,1088]{1,0:T(8,128)(2,1)S(1)} %slice.447), channel_id=1, source_target_pairs={{0,4},{4,8},{8,12},{12,0},{1,5},{5,9},{9,13},{13,1},{2,6},{6,10},{... | collective-permute-start | bytes 887816 | tf_op jit(solution)/shard_map/ppermute | solution.py:227
  104.5 22.7 %collective-permute-start.9 = (bf16[136,960]{1,0:T(8,128)(2,1)S(1)}, bf16[136,960]{1,0:T(8,128)(2,1)S(1)}, u32[]{:S(2)}, u32[]{:S(2)}) collective-permute-start(bf16[136,960]{1,0:T(8,128)(2,1)S(1)} %slice.440), channel_id=1, source_target_pairs={{0,4},{4,8},{8,12},{12,0},{1,5},{5,9},{9,13},{13,1},{2,6},{6,10},{... | collective-permute-start | bytes 783368 | tf_op jit(solution)/shard_map/ppermute | solution.py:227
  114.3 18.7 %collective-permute-start.10 = (bf16[136,960]{1,0:T(8,128)(2,1)S(1)}, bf16[136,960]{1,0:T(8,128)(2,1)S(1)}, u32[]{:S(2)}, u32[]{:S(2)}) collective-permute-start(bf16[136,960]{1,0:T(8,128)(2,1)S(1)} %slice.441), channel_id=1, source_target_pairs={{0,12},{4,0},{8,4},{12,8},{1,13},{5,1},{9,5},{13,9},{2,14},{6,2},{... | collective-permute-start | bytes 783368 | tf_op jit(solution)/shard_map/ppermute | solution.py:227
  127.2 47.2 %collective-permute-start.1 = (bf16[1024,272]{0,1:T(8,128)(2,1)S(1)}, bf16[1024,272]{0,1:T(8,128)(2,1)S(1)}, u32[]{:S(2)}, u32[]{:S(2)}) collective-permute-start(bf16[1024,272]{0,1:T(8,128)(2,1)S(1)} %get-tuple-element.168), channel_id=1, source_target_pairs={{0,1},{1,0},{2,3},{3,2},{4,5},{5,4},{6,7},{7,6},{8,9},{9,8},{10,11... | collective-permute-start | bytes 1671176 | tf_op jit(solution)/shard_map/ppermute | solution.py:222
  133.0 11.4 %collective-permute-start.22 = (bf16[136,1088]{1,0:T(8,128)(2,1)S(1)}, bf16[136,1088]{1,0:T(8,128)(2,1)S(1)}, u32[]{:S(2)}, u32[]{:S(2)}) collective-permute-start(bf16[136,1088]{1,0:T(8,128)(2,1)S(1)} %slice.448), channel_id=1, source_target_pairs={{0,12},{4,0},{8,4},{12,8},{1,13},{5,1},{9,5},{13,9},{2,14},{6,2},{... | collective-permute-start | bytes 887816 | tf_op jit(solution)/shard_map/ppermute | solution.py:227
  136.6 20.8 %collective-permute-start.29 = (bf16[136,1088]{1,0:T(8,128)(2,1)S(1)}, bf16[136,1088]{1,0:T(8,128)(2,1)S(1)}, u32[]{:S(2)}, u32[]{:S(2)}) collective-permute-start(bf16[136,1088]{1,0:T(8,128)(2,1)S(1)} %slice.457), channel_id=1, source_target_pairs={{0,4},{4,8},{8,12},{12,0},{1,5},{5,9},{9,13},{13,1},{2,6},{6,10},{... | collective-permute-start | bytes 887816 | tf_op jit(solution)/shard_map/ppermute | solution.py:227
  144.4 13.8 %collective-permute-start.30 = (bf16[136,1088]{1,0:T(8,128)(2,1)S(1)}, bf16[136,1088]{1,0:T(8,128)(2,1)S(1)}, u32[]{:S(2)}, u32[]{:S(2)}) collective-permute-start(bf16[136,1088]{1,0:T(8,128)(2,1)S(1)} %slice.458), channel_id=1, source_target_pairs={{0,12},{4,0},{8,4},{12,8},{1,13},{5,1},{9,5},{13,9},{2,14},{6,2},{... | collective-permute-start | bytes 887816 | tf_op jit(solution)/shard_map/ppermute | solution.py:227
  157.4 12.2 %collective-permute-start.25 = (bf16[136,1088]{1,0:T(8,128)(2,1)S(1)}, bf16[136,1088]{1,0:T(8,128)(2,1)S(1)}, u32[]{:S(2)}, u32[]{:S(2)}) collective-permute-start(bf16[136,1088]{1,0:T(8,128)(2,1)S(1)} %slice.461), channel_id=1, source_target_pairs={{0,4},{4,8},{8,12},{12,0},{1,5},{5,9},{9,13},{13,1},{2,6},{6,10},{... | collective-permute-start | bytes 887816 | tf_op jit(solution)/shard_map/ppermute | solution.py:227
  158.3 14.7 %collective-permute-start.26 = (bf16[136,1088]{1,0:T(8,128)(2,1)S(1)}, bf16[136,1088]{1,0:T(8,128)(2,1)S(1)}, u32[]{:S(2)}, u32[]{:S(2)}) collective-permute-start(bf16[136,1088]{1,0:T(8,128)(2,1)S(1)} %slice.462), channel_id=1, source_target_pairs={{0,12},{4,0},{8,4},{12,8},{1,13},{5,1},{9,5},{13,9},{2,14},{6,2},{... | collective-permute-start | bytes 887816 | tf_op jit(solution)/shard_map/ppermute | solution.py:227
  169.6 19.2 %collective-permute-start.36 = (bf16[1024,272]{0,1:T(8,128)(2,1)S(1)}, bf16[1024,272]{0,1:T(8,128)(2,1)S(1)}, u32[]{:S(2)}, u32[]{:S(2)}) collective-permute-start(bf16[1024,272]{0,1:T(8,128)(2,1)S(1)} %get-tuple-element.157), channel_id=1, source_target_pairs={{0,1},{1,0},{2,3},{3,2},{4,5},{5,4},{6,7},{7,6},{8,9},{9,8},{10,11... | collective-permute-start | bytes 1671176 | tf_op jit(solution)/shard_map/ppermute | solution.py:222
  170.3 21.1 %collective-permute-start.35 = (bf16[1024,272]{0,1:T(8,128)(2,1)S(1)}, bf16[1024,272]{0,1:T(8,128)(2,1)S(1)}, u32[]{:S(2)}, u32[]{:S(2)}) collective-permute-start(bf16[1024,272]{0,1:T(8,128)(2,1)S(1)} %get-tuple-element.156), channel_id=1, source_target_pairs={{0,1},{1,0},{2,3},{3,2},{4,5},{5,4},{6,7},{7,6},{8,9},{9,8},{10,11... | collective-permute-start | bytes 1671176 | tf_op jit(solution)/shard_map/ppermute | solution.py:222
  172.9 14.5 %collective-permute-start.13 = (bf16[1024,272]{0,1:T(8,128)(2,1)S(1)}, bf16[1024,272]{0,1:T(8,128)(2,1)S(1)}, u32[]{:S(2)}, u32[]{:S(2)}) collective-permute-start(bf16[1024,272]{0,1:T(8,128)(2,1)S(1)} %collective-permute-done.12), channel_id=1, source_target_pairs={{0,2},{2,0},{1,3},{3,1},{4,6},{6,4},{5,7},{7,5},{8,10},{10,8},{9,1... | collective-permute-start | bytes 1671176 | tf_op jit(solution)/shard_map/ppermute | solution.py:218
  187.5 7.6 %collective-permute-start.15 = (bf16[1024,272]{0,1:T(8,128)(2,1)S(1)}, bf16[1024,272]{0,1:T(8,128)(2,1)S(1)}, u32[]{:S(2)}, u32[]{:S(2)}) collective-permute-start(bf16[1024,272]{0,1:T(8,128)(2,1)S(1)} %get-tuple-element.163), channel_id=1, source_target_pairs={{0,1},{1,0},{2,3},{3,2},{4,5},{5,4},{6,7},{7,6},{8,9},{9,8},{10,11... | collective-permute-start | bytes 1671176 | tf_op jit(solution)/shard_map/ppermute | solution.py:222
  187.6 7.6 %collective-permute-start.14 = (bf16[1024,272]{0,1:T(8,128)(2,1)S(1)}, bf16[1024,272]{0,1:T(8,128)(2,1)S(1)}, u32[]{:S(2)}, u32[]{:S(2)}) collective-permute-start(bf16[1024,272]{0,1:T(8,128)(2,1)S(1)} %get-tuple-element.162), channel_id=1, source_target_pairs={{0,1},{1,0},{2,3},{3,2},{4,5},{5,4},{6,7},{7,6},{8,9},{9,8},{10,11... | collective-permute-start | bytes 1671176 | tf_op jit(solution)/shard_map/ppermute | solution.py:222
  227.8 26.7 %collective-permute-start.16 = (bf16[1024,320]{0,1:T(8,128)(2,1)}, bf16[1024,320]{0,1:T(8,128)(2,1)}, u32[]{:S(2)}, u32[]{:S(2)}) collective-permute-start(bf16[1024,320]{0,1:T(8,128)(2,1)} %copy.66), channel_id=1, source_target_pairs={{0,2},{2,0},{1,3},{3,1},{4,6},{6,4},{5,7},{7,5},{8,10},{10,8},{9,1... | collective-permute-start | bytes 1966088 | tf_op jit(solution)/shard_map/ppermute | solution.py:218
  228.3 16.9 %collective-permute-start.80 = (f32[1,17]{1,0:T(1,128)S(1)}, f32[1,17]{1,0:T(1,128)S(1)}, u32[]{:S(2)}, u32[]{:S(2)}) collective-permute-start(f32[1,17]{1,0:T(1,128)S(1)} %bitcast.92), channel_id=1, source_target_pairs={{0,16},{16,0},{1,17},{17,1},{2,18},{18,2},{3,19},{19,3},{4,20},{20... | collective-permute-start | bytes 212 | tf_op jit(solution)/shard_map/ppermute | solution.py:227
  252.6 9.2 %collective-permute-start.86 = (f32[1,17]{1,0:T(1,128)S(1)}, f32[1,17]{1,0:T(1,128)S(1)}, u32[]{:S(2)}, u32[]{:S(2)}) collective-permute-start(f32[1,17]{1,0:T(1,128)S(1)} %maximum_maximum_fusion.2), channel_id=1, source_target_pairs={{0,3},{1,0},{2,1},{3,2},{4,7},{5,4},{6,5},{7,6},{8,11},{9,8},{10,9... | collective-permute-start | bytes 212 | tf_op jit(solution)/shard_map/ppermute | solution.py:227
  252.6 9.2 %collective-permute-start.85 = (f32[1,17]{1,0:T(1,128)S(1)}, f32[1,17]{1,0:T(1,128)S(1)}, u32[]{:S(2)}, u32[]{:S(2)}) collective-permute-start(f32[1,17]{1,0:T(1,128)S(1)} %maximum_maximum_fusion.2), channel_id=1, source_target_pairs={{0,2},{1,3},{2,0},{3,1},{4,6},{5,7},{6,4},{7,5},{8,10},{9,11},{10,... | collective-permute-start | bytes 212 | tf_op jit(solution)/shard_map/ppermute | solution.py:227
  328.1 13.3 %collective-permute-start.31 = (bf16[1024,272]{0,1:T(8,128)(2,1)S(1)}, bf16[1024,272]{0,1:T(8,128)(2,1)S(1)}, u32[]{:S(2)}, u32[]{:S(2)}) collective-permute-start(bf16[1024,272]{0,1:T(8,128)(2,1)S(1)} %get-tuple-element.141), channel_id=1, source_target_pairs={{0,1},{1,0},{2,3},{3,2},{4,5},{5,4},{6,7},{7,6},{8,9},{9,8},{10,11... | collective-permute-start | bytes 1671176 | tf_op jit(solution)/shard_map/ppermute | solution.py:222
  328.4 13.0 %collective-permute-start.32 = (bf16[1024,272]{0,1:T(8,128)(2,1)S(1)}, bf16[1024,272]{0,1:T(8,128)(2,1)S(1)}, u32[]{:S(2)}, u32[]{:S(2)}) collective-permute-start(bf16[1024,272]{0,1:T(8,128)(2,1)S(1)} %get-tuple-element.140), channel_id=1, source_target_pairs={{0,1},{1,0},{2,3},{3,2},{4,5},{5,4},{6,7},{7,6},{8,9},{9,8},{10,11... | collective-permute-start | bytes 1671176 | tf_op jit(solution)/shard_map/ppermute | solution.py:222
  335.3 15.5 %collective-permute-start.39 = (bf16[256,1088]{0,1:T(8,128)(2,1)S(1)}, bf16[256,1088]{0,1:T(8,128)(2,1)S(1)}, u32[]{:S(2)}, u32[]{:S(2)}) collective-permute-start(bf16[256,1088]{0,1:T(8,128)(2,1)S(1)} %select_convert_fusion.2), channel_id=1, source_target_pairs={{0,2},{2,0},{1,3},{3,1},{4,6},{6,4},{5,7},{7,5},{8,10},{10,8},{9,1... | collective-permute-start | bytes 1671176 | tf_op jit(solution)/shard_map/ppermute | solution.py:218
  337.0 32.8 %collective-permute-start.70 = (bf16[544,1088]{1,0:T(8,128)(2,1)S(1)}, bf16[544,1088]{1,0:T(8,128)(2,1)S(1)}, u32[]{:S(2)}, u32[]{:S(2)}) collective-permute-start(bf16[544,1088]{1,0:T(8,128)(2,1)S(1)} %constant_dynamic-slice_fusion.1), channel_id=1, source_target_pairs={{0,16},{16,0},{1,17},{17,1},{2,18},{18,2},{3,19},{19,3},{4,20},{20... | collective-permute-start | bytes 3551240 | tf_op jit(solution)/shard_map/ppermute | solution.py:292
  342.1 21.2 %collective-permute-start.33 = (bf16[1024,272]{0,1:T(8,128)(2,1)S(1)}, bf16[1024,272]{0,1:T(8,128)(2,1)S(1)}, u32[]{:S(2)}, u32[]{:S(2)}) collective-permute-start(bf16[1024,272]{0,1:T(8,128)(2,1)S(1)} %select_convert_fusion.3), channel_id=1, source_target_pairs={{0,2},{2,0},{1,3},{3,1},{4,6},{6,4},{5,7},{7,5},{8,10},{10,8},{9,1... | collective-permute-start | bytes 1671176 | tf_op jit(solution)/shard_map/ppermute | solution.py:218
  353.6 9.5 %collective-permute-start.49 = (f32[3,1088]{1,0:T(4,128)S(1)}, f32[3,1088]{1,0:T(4,128)S(1)}, u32[]{:S(2)}, u32[]{:S(2)}) collective-permute-start(f32[3,1088]{1,0:T(4,128)S(1)} %pad_maximum_fusion.17), channel_id=1, source_target_pairs={{0,2},{2,0},{1,3},{3,1},{4,6},{6,4},{5,7},{7,5},{8,10},{10,8},{9,1... | collective-permute-start | bytes 39176 | tf_op jit(solution)/shard_map/ppermute | solution.py:218
  355.3 40.5 %collective-permute-start.75 = (bf16[544,1088]{1,0:T(8,128)(2,1)S(1)}, bf16[544,1088]{1,0:T(8,128)(2,1)S(1)}, u32[]{:S(2)}, u32[]{:S(2)}) collective-permute-start(bf16[544,1088]{1,0:T(8,128)(2,1)S(1)} %constant_dynamic-slice_fusion), channel_id=1, source_target_pairs={{0,16},{16,0},{1,17},{17,1},{2,18},{18,2},{3,19},{19,3},{4,20},{20... | collective-permute-start | bytes 3551240 | tf_op jit(solution)/shard_map/ppermute | solution.py:292
  359.8 64.0 %collective-permute-start.40 = (bf16[256,1088]{0,1:T(8,128)(2,1)S(1)}, bf16[256,1088]{0,1:T(8,128)(2,1)S(1)}, u32[]{:S(2)}, u32[]{:S(2)}) collective-permute-start(bf16[256,1088]{0,1:T(8,128)(2,1)S(1)} %get-tuple-element.124), channel_id=1, source_target_pairs={{0,2},{2,0},{1,3},{3,1},{4,6},{6,4},{5,7},{7,5},{8,10},{10,8},{9,1... | collective-permute-start | bytes 1671176 | tf_op jit(solution)/shard_map/ppermute | solution.py:218
  396.2 18.0 %collective-permute-start.73 = (bf16[136,576]{1,0:T(8,128)(2,1)S(1)}, bf16[136,576]{1,0:T(8,128)(2,1)S(1)}, u32[]{:S(2)}, u32[]{:S(2)}) collective-permute-start(bf16[136,576]{1,0:T(8,128)(2,1)S(1)} %slice.511), channel_id=1, source_target_pairs={{0,12},{4,0},{8,4},{12,8},{1,13},{5,1},{9,5},{13,9},{2,14},{6,2},{... | collective-permute-start | bytes 470024 | tf_op jit(solution)/shard_map/ppermute | solution.py:227
  397.0 9.0 %collective-permute-start.71 = (bf16[136,512]{1,0:T(8,128)(2,1)S(1)}, bf16[136,512]{1,0:T(8,128)(2,1)S(1)}, u32[]{:S(2)}, u32[]{:S(2)}) collective-permute-start(bf16[136,512]{1,0:T(8,128)(2,1)S(1)} %slice.510), channel_id=1, source_target_pairs={{0,4},{4,8},{8,12},{12,0},{1,5},{5,9},{9,13},{13,1},{2,6},{6,10},{... | collective-permute-start | bytes 417800 | tf_op jit(solution)/shard_map/ppermute | solution.py:227
  398.3 25.3 %collective-permute-start.78 = (bf16[136,576]{1,0:T(8,128)(2,1)S(1)}, bf16[136,576]{1,0:T(8,128)(2,1)S(1)}, u32[]{:S(2)}, u32[]{:S(2)}) collective-permute-start(bf16[136,576]{1,0:T(8,128)(2,1)S(1)} %slice.514), channel_id=1, source_target_pairs={{0,12},{4,0},{8,4},{12,8},{1,13},{5,1},{9,5},{13,9},{2,14},{6,2},{... | collective-permute-start | bytes 470024 | tf_op jit(solution)/shard_map/ppermute | solution.py:227
  401.0 11.9 %collective-permute-start.76 = (bf16[136,512]{1,0:T(8,128)(2,1)S(1)}, bf16[136,512]{1,0:T(8,128)(2,1)S(1)}, u32[]{:S(2)}, u32[]{:S(2)}) collective-permute-start(bf16[136,512]{1,0:T(8,128)(2,1)S(1)} %slice.513), channel_id=1, source_target_pairs={{0,4},{4,8},{8,12},{12,0},{1,5},{5,9},{9,13},{13,1},{2,6},{6,10},{... | collective-permute-start | bytes 417800 | tf_op jit(solution)/shard_map/ppermute | solution.py:227
  406.1 17.9 %collective-permute-start.72 = (bf16[136,1088]{1,0:T(8,128)(2,1)S(1)}, bf16[136,1088]{1,0:T(8,128)(2,1)S(1)}, u32[]{:S(2)}, u32[]{:S(2)}) collective-permute-start(bf16[136,1088]{1,0:T(8,128)(2,1)S(1)} %pad_maximum_fusion.11), channel_id=1, source_target_pairs={{0,4},{4,8},{8,12},{12,0},{1,5},{5,9},{9,13},{13,1},{2,6},{6,10},{... | collective-permute-start | bytes 887816 | tf_op jit(solution)/shard_map/ppermute | solution.py:227
  412.9 19.8 %collective-permute-start.77 = (bf16[136,1088]{1,0:T(8,128)(2,1)S(1)}, bf16[136,1088]{1,0:T(8,128)(2,1)S(1)}, u32[]{:S(2)}, u32[]{:S(2)}) collective-permute-start(bf16[136,1088]{1,0:T(8,128)(2,1)S(1)} %pad_maximum_fusion.13), channel_id=1, source_target_pairs={{0,4},{4,8},{8,12},{12,0},{1,5},{5,9},{9,13},{13,1},{2,6},{6,10},{... | collective-permute-start | bytes 887816 | tf_op jit(solution)/shard_map/ppermute | solution.py:227
  414.3 17.5 %collective-permute-start.74 = (bf16[136,1088]{1,0:T(8,128)(2,1)S(1)}, bf16[136,1088]{1,0:T(8,128)(2,1)S(1)}, u32[]{:S(2)}, u32[]{:S(2)}) collective-permute-start(bf16[136,1088]{1,0:T(8,128)(2,1)S(1)} %pad_maximum_fusion.12), channel_id=1, source_target_pairs={{0,12},{4,0},{8,4},{12,8},{1,13},{5,1},{9,5},{13,9},{2,14},{6,2},{... | collective-permute-start | bytes 887816 | tf_op jit(solution)/shard_map/ppermute | solution.py:227
  423.7 14.6 %collective-permute-start.79 = (bf16[136,1088]{1,0:T(8,128)(2,1)S(1)}, bf16[136,1088]{1,0:T(8,128)(2,1)S(1)}, u32[]{:S(2)}, u32[]{:S(2)}) collective-permute-start(bf16[136,1088]{1,0:T(8,128)(2,1)S(1)} %pad_maximum_fusion.14), channel_id=1, source_target_pairs={{0,12},{4,0},{8,4},{12,8},{1,13},{5,1},{9,5},{13,9},{2,14},{6,2},{... | collective-permute-start | bytes 887816 | tf_op jit(solution)/shard_map/ppermute | solution.py:227
  423.9 15.3 %collective-permute-start.42 = (bf16[256,1088]{0,1:T(8,128)(2,1)S(1)}, bf16[256,1088]{0,1:T(8,128)(2,1)S(1)}, u32[]{:S(2)}, u32[]{:S(2)}) collective-permute-start(bf16[256,1088]{0,1:T(8,128)(2,1)S(1)} %get-tuple-element.151), channel_id=1, source_target_pairs={{0,1},{1,0},{2,3},{3,2},{4,5},{5,4},{6,7},{7,6},{8,9},{9,8},{10,11... | collective-permute-start | bytes 1671176 | tf_op jit(solution)/shard_map/ppermute | solution.py:222
  473.1 36.8 %collective-permute-start.43 = (bf16[1024,640]{1,0:T(8,128)(2,1)S(1)}, bf16[1024,640]{1,0:T(8,128)(2,1)S(1)}, u32[]{:S(2)}, u32[]{:S(2)}) collective-permute-start(bf16[1024,640]{1,0:T(8,128)(2,1)S(1)} %convert_element_type.335), channel_id=1, source_target_pairs={{16,0},{17,1},{18,2},{19,3},{20,4},{21,5},{22,6},{23,7},{24,8},{25... | collective-permute-start | bytes 3932168 | tf_op jit(solution)/shard_map/ppermute | solution.py:506
  525.4 14.7 %collective-permute-start.46 = (bf16[1024,272]{0,1:T(8,128)(2,1)S(1)}, bf16[1024,272]{0,1:T(8,128)(2,1)S(1)}, u32[]{:S(2)}, u32[]{:S(2)}) collective-permute-start(bf16[1024,272]{0,1:T(8,128)(2,1)S(1)} %select_convert_fusion.1), channel_id=1, source_target_pairs={{0,2},{2,0},{1,3},{3,1},{4,6},{6,4},{5,7},{7,5},{8,10},{10,8},{9,1... | collective-permute-start | bytes 1671176 | tf_op jit(solution)/shard_map/ppermute | solution.py:218
  546.7 8.2 %collective-permute-start.52 = (f32[1,4080]{1,0:T(1,128)S(1)}, f32[1,4080]{1,0:T(1,128)S(1)}, u32[]{:S(2)}, u32[]{:S(2)}) collective-permute-start(f32[1,4080]{1,0:T(1,128)S(1)} %bitcast.82), channel_id=1, source_target_pairs={{0,16},{16,0},{1,17},{17,1},{2,18},{18,2},{3,19},{19,3},{4,20},{20... | collective-permute-start | bytes 48968 | tf_op jit(solution)/shard_map/ppermute | solution.py:227
  546.8 11.1 %collective-permute-start.48 = (f32[2,1024]{1,0:T(2,128)S(1)}, f32[2,1024]{1,0:T(2,128)S(1)}, u32[]{:S(2)}, u32[]{:S(2)}) collective-permute-start(f32[2,1024]{1,0:T(2,128)S(1)} %fusion.125), channel_id=1, source_target_pairs={{0,1},{1,0},{2,3},{3,2},{4,5},{5,4},{6,7},{7,6},{8,9},{9,8},{10,11... | collective-permute-start | bytes 24584 | tf_op jit(solution)/shard_map/ppermute | solution.py:222
  553.2 24.8 %collective-permute-start.57 = (bf16[544,816]{1,0:T(8,128)(2,1)}, bf16[544,816]{1,0:T(8,128)(2,1)}, u32[]{:S(2)}, u32[]{:S(2)}) collective-permute-start(bf16[544,816]{1,0:T(8,128)(2,1)} %copy.78), channel_id=1, source_target_pairs={{0,16},{16,0},{1,17},{17,1},{2,18},{18,2},{3,19},{19,3},{4,20},{20... | collective-permute-start | bytes 2663432 | tf_op jit(solution)/shard_map/ppermute | solution.py:292
  555.6 9.7 %collective-permute-start.55 = (f32[1,4080]{1,0:T(1,128)}, f32[1,4080]{1,0:T(1,128)}, u32[]{:S(2)}, u32[]{:S(2)}) collective-permute-start(f32[1,4080]{1,0:T(1,128)} %add.621), channel_id=1, source_target_pairs={{0,12},{4,0},{8,4},{12,8},{1,13},{5,1},{9,5},{13,9},{2,14},{6,2},{... | collective-permute-start | bytes 48968 | tf_op jit(solution)/shard_map/ppermute | solution.py:227
  556.4 8.9 %collective-permute-start.54 = (f32[1,4080]{1,0:T(1,128)}, f32[1,4080]{1,0:T(1,128)}, u32[]{:S(2)}, u32[]{:S(2)}) collective-permute-start(f32[1,4080]{1,0:T(1,128)} %add.621), channel_id=1, source_target_pairs={{0,8},{4,12},{8,0},{12,4},{1,9},{5,13},{9,1},{13,5},{2,10},{6,14},... | collective-permute-start | bytes 48968 | tf_op jit(solution)/shard_map/ppermute | solution.py:227
  557.5 7.7 %collective-permute-start.53 = (f32[1,4080]{1,0:T(1,128)}, f32[1,4080]{1,0:T(1,128)}, u32[]{:S(2)}, u32[]{:S(2)}) collective-permute-start(f32[1,4080]{1,0:T(1,128)} %add.621), channel_id=1, source_target_pairs={{0,4},{4,8},{8,12},{12,0},{1,5},{5,9},{9,13},{13,1},{2,6},{6,10},{... | collective-permute-start | bytes 48968 | tf_op jit(solution)/shard_map/ppermute | solution.py:227
  565.0 26.8 %collective-permute-start.62 = (bf16[544,272]{0,1:T(8,128)(2,1)}, bf16[544,272]{0,1:T(8,128)(2,1)}, u32[]{:S(2)}, u32[]{:S(2)}) collective-permute-start(bf16[544,272]{0,1:T(8,128)(2,1)} %constant_dynamic-slice_fusion.2), channel_id=1, source_target_pairs={{0,16},{16,0},{1,17},{17,1},{2,18},{18,2},{3,19},{19,3},{4,20},{20... | collective-permute-start | bytes 887816 | tf_op jit(solution)/shard_map/ppermute | solution.py:292
  580.6 27.8 %collective-permute-start.60 = (bf16[136,432]{0,1:T(8,128)(2,1)S(1)}, bf16[136,432]{0,1:T(8,128)(2,1)S(1)}, u32[]{:S(2)}, u32[]{:S(2)}) collective-permute-start(bf16[136,432]{0,1:T(8,128)(2,1)S(1)} %slice.499), channel_id=1, source_target_pairs={{0,12},{4,0},{8,4},{12,8},{1,13},{5,1},{9,5},{13,9},{2,14},{6,2},{... | collective-permute-start | bytes 352520 | tf_op jit(solution)/shard_map/ppermute | solution.py:227
  581.7 9.1 %collective-permute-start.58 = (bf16[136,384]{0,1:T(8,128)(2,1)S(1)}, bf16[136,384]{0,1:T(8,128)(2,1)S(1)}, u32[]{:S(2)}, u32[]{:S(2)}) collective-permute-start(bf16[136,384]{0,1:T(8,128)(2,1)S(1)} %slice.498), channel_id=1, source_target_pairs={{0,4},{4,8},{8,12},{12,0},{1,5},{5,9},{9,13},{13,1},{2,6},{6,10},{... | collective-permute-start | bytes 313352 | tf_op jit(solution)/shard_map/ppermute | solution.py:227
  591.0 26.6 %collective-permute-start.59 = (bf16[136,816]{0,1:T(8,128)(2,1)S(1)}, bf16[136,816]{0,1:T(8,128)(2,1)S(1)}, u32[]{:S(2)}, u32[]{:S(2)}) collective-permute-start(bf16[136,816]{0,1:T(8,128)(2,1)S(1)} %pad_maximum_fusion.9), channel_id=1, source_target_pairs={{0,4},{4,8},{8,12},{12,0},{1,5},{5,9},{9,13},{13,1},{2,6},{6,10},{... | collective-permute-start | bytes 665864 | tf_op jit(solution)/shard_map/ppermute | solution.py:227
  593.1 11.2 %collective-permute-start.63 = (bf16[136,128]{0,1:T(8,128)(2,1)S(1)}, bf16[136,128]{0,1:T(8,128)(2,1)S(1)}, u32[]{:S(2)}, u32[]{:S(2)}) collective-permute-start(bf16[136,128]{0,1:T(8,128)(2,1)S(1)} %slice.505), channel_id=1, source_target_pairs={{0,4},{4,8},{8,12},{12,0},{1,5},{5,9},{9,13},{13,1},{2,6},{6,10},{... | collective-permute-start | bytes 104456 | tf_op jit(solution)/shard_map/ppermute | solution.py:227
  594.6 10.4 %collective-permute-start.65 = (bf16[136,144]{0,1:T(8,128)(2,1)S(1)}, bf16[136,144]{0,1:T(8,128)(2,1)S(1)}, u32[]{:S(2)}, u32[]{:S(2)}) collective-permute-start(bf16[136,144]{0,1:T(8,128)(2,1)S(1)} %slice.506), channel_id=1, source_target_pairs={{0,12},{4,0},{8,4},{12,8},{1,13},{5,1},{9,5},{13,9},{2,14},{6,2},{... | collective-permute-start | bytes 117512 | tf_op jit(solution)/shard_map/ppermute | solution.py:227
  613.8 8.5 %collective-permute-start.61 = (bf16[136,816]{0,1:T(8,128)(2,1)S(1)}, bf16[136,816]{0,1:T(8,128)(2,1)S(1)}, u32[]{:S(2)}, u32[]{:S(2)}) collective-permute-start(bf16[136,816]{0,1:T(8,128)(2,1)S(1)} %pad_maximum_fusion.10), channel_id=1, source_target_pairs={{0,12},{4,0},{8,4},{12,8},{1,13},{5,1},{9,5},{13,9},{2,14},{6,2},{... | collective-permute-start | bytes 665864 | tf_op jit(solution)/shard_map/ppermute | solution.py:227
  (84 other events, 743.7 us)

commit v2 on v1

v2 whole, which is shorter than its diff:
```python
import functools

import jax
import jax.numpy as jnp
from jax import lax
from jax.experimental import pallas as pl
from jax.experimental.pallas import tpu as pltpu
from jax.sharding import PartitionSpec as P


H = 17
E = 64

norm_eps = 1e-05
neg_fill = -1e30
clip_limit = 8.0

f32 = jnp.float32
bf16 = jnp.bfloat16

VMEM = pl.BlockSpec(memory_space=pltpu.VMEM)
SMEM = pl.BlockSpec(memory_space=pltpu.SMEM)
ANY = pl.BlockSpec(memory_space=pl.ANY)


def dot_nn(left, right):
    return lax.dot_general(left, right, (((1,), (0,)), ((), ())), preferred_element_type=f32)


def dot_nt(left, right):
    return lax.dot_general(left, right, (((1,), (1,)), ((), ())), preferred_element_type=f32)


def dot_tn(left, right):
    return lax.dot_general(left, right, (((0,), (0,)), ((), ())), preferred_element_type=f32)


def params():
    return pltpu.CompilerParams(vmem_limit_bytes=50 * 2**20)


def cost(flops, moved, exps=0):
    return pl.CostEstimate(flops=int(flops), bytes_accessed=int(moved), transcendentals=int(exps))


def shape(dims, kind):
    return jax.ShapeDtypeStruct(dims, kind)


def rows_at(start, length):
    return pl.ds(pl.multiple_of(start, 16), length)


def assemble_body(plan, fill, starts, *refs):
    pieces, out_ref = refs[:-1], refs[-1]
    for piece, source, length, where in plan:
        out_ref[rows_at(starts[where], length), :] = pieces[piece][source : source + length, :]
    if fill:
        out_ref[out_ref.shape[0] - fill :, :] = jnp.zeros((fill, out_ref.shape[1]), bf16)


def whole(array):
    return pl.BlockSpec(array.shape, lambda *_: (0,) * array.ndim)


def assemble(starts, pieces, plan, rows, fill=0):
    result = shape((rows + fill, pieces[0].shape[1]), bf16)
    return pl.pallas_call(
        functools.partial(assemble_body, tuple(plan), fill),
        grid_spec=pltpu.PrefetchScalarGridSpec(
            num_scalar_prefetch=1,
            grid=(1,),
            in_specs=[whole(piece) for piece in pieces],
            out_specs=whole(result),
        ),
        out_shape=result,
        compiler_params=params(),
        cost_estimate=cost(0, rows * result.shape[1] * 4),
        name="assemble",
    )(starts, *pieces)


def first_norm_body(own, order, p0, p1, p2, p3, *refs):
    vec_ref, x_ref, n_ref, stat_ref = (refs[3], *refs[:3]) if own else refs
    part = p0.shape[0]
    full, count = x_ref.shape
    if own:
        vec_ref[full:, :] = jnp.zeros((vec_ref.shape[0] - full, vec_ref.shape[1]), f32)
    for n, piece in enumerate((p0, p1, p2, p3)):
        where = rows_at(order[n] * part, part)
        x_ref[where, :] = piece[:, :count]
        if own:
            vec_ref[where, :] = piece[:, count : count + 128].astype(f32)
    for start in range(0, count, 256):
        cols = slice(start, start + 256)
        x = x_ref[:, cols].astype(f32)
        mean = jnp.sum(x, axis=0, keepdims=True) * (1.0 / full)
        center = x - mean
        inv = lax.rsqrt(jnp.sum(center * center, axis=0, keepdims=True) * (1.0 / full) + norm_eps)
        n_ref[:, cols] = (center * inv * vec_ref[:full, 0:1] + vec_ref[:full, 1:2]).astype(bf16)
        stat_ref[0:1, cols] = mean
        stat_ref[1:2, cols] = inv


def first_norm(order, pieces, count, vectors=None):
    own = vectors is None
    full = pieces[0].shape[0] * 4
    results = [shape((full, count), bf16), shape((full, count), bf16), shape((8, count), f32)]
    operands = list(pieces)
    if own:
        results.append(shape((full + E, 128), f32))
    else:
        operands.append(vectors)
    return pl.pallas_call(
        functools.partial(first_norm_body, own),
        grid_spec=pltpu.PrefetchScalarGridSpec(
            num_scalar_prefetch=1,
            grid=(1,),
            in_specs=[whole(array) for array in operands],
            out_specs=[whole(result) for result in results],
        ),
        out_shape=results,
        compiler_params=params(),
        cost_estimate=cost(20 * full * count, full * count * 8),
        name="first_norm",
    )(order, *operands)


def head_weights_body(order, own, left, right, far_a, far_b, near, far, pick_own, pick_next, out_ref):
    size, cut = own.shape[0], far_a.shape[0]

    def put(owner, extra, rows, piece, edge):
        out_ref[rows_at(owner * size + extra, rows), :] = (
            dot_nn(piece, pick_own[...]) + dot_nn(edge, pick_next[...])
        ).astype(bf16)

    put(order[0], 0, size, own[...], near[:size, :])
    put(order[1], 0, size, left[...], near[size : 2 * size, :])
    put(order[3], 0, size, right[...], near[2 * size :, :])
    put(order[2], 0, cut, far_a[...], far[:cut, :])
    put(order[2], cut, size - cut, far_b[...], far[cut:, :])


def head_weights(order, pieces, pick_own, pick_next):
    result = shape((pieces[0].shape[0] * 4, pick_own.shape[1]), bf16)
    return pl.pallas_call(
        head_weights_body,
        grid_spec=pltpu.PrefetchScalarGridSpec(
            num_scalar_prefetch=1,
            grid=(1,),
            in_specs=[whole(array) for array in (*pieces, pick_own, pick_next)],
            out_specs=whole(result),
        ),
        out_shape=result,
        compiler_params=params(),
        cost_estimate=cost(2 * 960 * 960 * 1088, 6 * 10**6),
        name="head_weights",
    )(order, *pieces, pick_own, pick_next)


def project_body(width, info, w_ref, bias_ref, own_ref, before_ref, q_ref, kv_ref, w_s):
    step = pl.program_id(0)
    half = pl.num_programs(0) // 2
    mine = (step // half) == info[0]

    @pl.when(step == 0)
    def _():
        w_s[...] = w_ref[...].T

    def keyvals(n_ref):
        kv_ref[:width, :] = dot_nn(w_s[width : 2 * width, :], n_ref[...]).astype(bf16)
        kv_ref[width:, :] = (
            dot_nn(w_s[2 * width :, :], n_ref[...]) + bias_ref[rows_at(info[1], width), 5:6]
        ).astype(bf16)

    @pl.when(mine)
    def _():
        out = dot_nn(w_s[:width, :], own_ref[...]) + bias_ref[rows_at(info[1], width), 4:5]
        q_ref[...] = (out.astype(bf16).astype(f32) * E ** (-0.5)).astype(bf16)
        keyvals(own_ref)

    @pl.when(jnp.logical_not(mine))
    def _():
        keyvals(before_ref)


def project(info, w_heads, bias, own, before, block=512):
    full, count = own.shape
    wide = w_heads.shape[1]
    width = wide // 3
    steps = count // block
    return pl.pallas_call(
        functools.partial(project_body, width),
        grid_spec=pltpu.PrefetchScalarGridSpec(
            num_scalar_prefetch=1,
            grid=(2 * steps,),
            in_specs=[
                pl.BlockSpec((full, wide), lambda i, s: (0, 0)),
                pl.BlockSpec(bias.shape, lambda i, s: (0, 0)),
                pl.BlockSpec((full, block), lambda i, s: (0, jnp.clip(i - s[0] * steps, 0, steps - 1))),
                pl.BlockSpec(
                    (full, block), lambda i, s: (0, jnp.clip(i - (1 - s[0]) * steps, 0, steps - 1))
                ),
            ],
            out_specs=[
                pl.BlockSpec((width, block), lambda i, s: (0, jnp.clip(i - s[0] * steps, 0, steps - 1))),
                pl.BlockSpec((2 * width, block), lambda i, s: (0, i)),
            ],
            scratch_shapes=[pltpu.VMEM((wide, full), bf16)],
        ),
        out_shape=[shape((width, count), bf16), shape((2 * width, 2 * count), bf16)],
        compiler_params=params(),
        cost_estimate=cost(2 * full * count * 5 * width, 10 * 10**6),
        name="project",
    )(info, w_heads, bias, own, before)


def block_limits(info, block, rows):
    prefix_len = info[0]
    query_lo = info[1] + block * rows
    query_hi = query_lo + rows - 1
    in_prefix = query_lo < prefix_len
    limit_max = jnp.where(in_prefix, jnp.maximum(prefix_len - 1, query_hi), query_hi)
    limit_min = jnp.where(in_prefix, prefix_len - 1, query_lo)
    positions = query_lo + lax.broadcasted_iota(jnp.int32, (1, rows), 1)
    return limit_max, limit_min, jnp.where(positions < prefix_len, prefix_len - 1, positions)


def attn_fwd_body(
    slots, keys, first, info, q_ref, kv_ref, attn_ref, exact_ref, lse_ref, top_ref, k_s, m_s, l_s, acc_s
):
    width, rows = q_ref.shape
    limit_max, limit_min, limit = block_limits(info, first, rows)
    n_need = limit_max // keys + 1
    n_full = (limit_min + 1) // keys
    for h in range(slots):
        k_s[h] = kv_ref[h * E : h * E + E, :].T
    m_s[...] = jnp.full_like(m_s, neg_fill)
    l_s[...] = jnp.zeros_like(l_s)
    acc_s[...] = jnp.zeros_like(acc_s)

    def step(index, masked):
        start = pl.multiple_of(index * keys, keys)
        if masked:
            seen = (start + lax.broadcasted_iota(jnp.int32, (keys, rows), 0)) <= limit
        for h in range(slots):
            here, row = slice(h * E, h * E + E), slice(h, h + 1)
            scores = dot_nn(k_s[h, pl.ds(start, keys), :], q_ref[here, :])
            if masked:
                scores = jnp.where(seen, scores, neg_fill)
            old_max = m_s[row, :]
            new_max = jnp.maximum(old_max, jnp.max(scores, axis=0, keepdims=True))
            weights = jnp.exp(scores - new_max)
            shrink = jnp.exp(old_max - new_max)
            l_s[row, :] = l_s[row, :] * shrink + jnp.sum(weights, axis=0, keepdims=True)
            values = kv_ref[width + h * E : width + h * E + E, pl.ds(start, keys)]
            acc_s[here, :] = acc_s[here, :] * shrink + dot_nn(values, weights.astype(bf16))
            m_s[row, :] = new_max

    @pl.loop(0, n_full)
    def _(index):
        step(index, False)

    @pl.loop(n_full, n_need)
    def _(index):
        step(index, True)

    for h in range(slots):
        here, row = slice(h * E, h * E + E), slice(h, h + 1)
        outcome = acc_s[here, :] / l_s[row, :]
        exact_ref[here, :] = outcome
        attn_ref[here, :] = outcome.astype(bf16)
    row_max = m_s[...]
    lse_ref[...] = row_max + jnp.log(l_s[...])
    top = row_max[:, :128]
    for start in range(128, rows, 128):
        top = jnp.maximum(top, row_max[:, start : start + 128])
    top_ref[...] = top


def attn_fwd(info, queries, kv_all, slots, first, rows=512, keys=512):
    width = queries.shape[0]
    total = kv_all.shape[1]
    return pl.pallas_call(
        functools.partial(attn_fwd_body, slots, keys, first),
        grid_spec=pltpu.PrefetchScalarGridSpec(
            num_scalar_prefetch=1,
            grid=(1,),
            in_specs=[
                pl.BlockSpec((width, rows), lambda i, _: (0, first)),
                pl.BlockSpec((2 * width, total), lambda i, _: (0, 0)),
            ],
            out_specs=[
                pl.BlockSpec((width, rows), lambda i, _: (0, 0)),
                pl.BlockSpec((width, rows), lambda i, _: (0, 0)),
                pl.BlockSpec((8, rows), lambda i, _: (0, 0)),
                pl.BlockSpec((8, 128), lambda i, _: (0, 0)),
            ],
            scratch_shapes=[
                pltpu.VMEM((slots, total, E), bf16),
                pltpu.VMEM((8, rows), f32),
                pltpu.VMEM((8, rows), f32),
                pltpu.VMEM((width, rows), f32),
            ],
        ),
        out_shape=[
            shape((width, rows), bf16),
            shape((width, rows), f32),
            shape((8, rows), f32),
            shape((8, 128), f32),
        ],
        compiler_params=params(),
        cost_estimate=cost(8 * 10**9, 6 * 10**6, 4 * 10**6),
        name="attn_fwd",
    )(info, queries, kv_all)


def attn_bwd_body(slots, keys, key_first, more, last, info, *refs):
    if more:
        q_ref, kv_ref, do_ref, o_ref, lse_ref, dq_in, dq_ref, dkv_ref, k_s, v_s, acc_s, dkv_s = refs
    else:
        q_ref, kv_ref, do_ref, o_ref, lse_ref, dq_ref, dkv_ref, k_s, v_s, acc_s, dkv_s = refs
    block = pl.program_id(0)
    width, rows = q_ref.shape
    n_blocks = kv_ref.shape[1] // keys
    limit_max, limit_min, limit = block_limits(info, block, rows)
    n_need = jnp.clip((limit_max - key_first) // keys + 1, 0, n_blocks)
    n_full = jnp.clip((limit_min - key_first + 1) // keys, 0, n_blocks)
    limit = limit - key_first

    @pl.when(block == 0)
    def _():
        dkv_s[...] = jnp.zeros_like(dkv_s)
        for h in range(slots):
            k_s[h] = kv_ref[h * E : h * E + E, :].T
            v_s[h] = kv_ref[width + h * E : width + h * E + E, :].T

    if more:
        acc_s[...] = dq_in[...]
    else:
        acc_s[...] = jnp.zeros_like(acc_s)
    dots = [
        jnp.sum(
            do_ref[h * E : h * E + E, :].astype(f32) * o_ref[h * E : h * E + E, :],
            axis=0,
            keepdims=True,
        )
        for h in range(slots)
    ]

    def step(index, masked):
        start = pl.multiple_of(index * keys, keys)
        where = pl.ds(start, keys)
        if masked:
            seen = (start + lax.broadcasted_iota(jnp.int32, (keys, rows), 0)) <= limit
        for h in range(slots):
            here = slice(h * E, h * E + E)
            there = slice(width + h * E, width + h * E + E)
            q_head, do_head = q_ref[here, :], do_ref[here, :]
            probs = jnp.exp(dot_nn(k_s[h, where, :], q_head) - lse_ref[h : h + 1, :])
            if masked:
                probs = jnp.where(seen, probs, 0.0)
            grad_probs = dot_nn(v_s[h, where, :], do_head)
            grad_scores = (probs * (grad_probs - dots[h])).astype(bf16)
            dkv_s[there, where] += dot_nt(do_head, probs.astype(bf16))
            dkv_s[here, where] += dot_nt(q_head, grad_scores)
            acc_s[here, :] += dot_nn(kv_ref[here, where], grad_scores)

    @pl.loop(0, n_full)
    def _(index):
        step(index, False)

    @pl.loop(n_full, n_need)
    def _(index):
        step(index, True)

    if last:
        dq_ref[...] = (acc_s[...] * E ** (-0.5)).astype(bf16)
    else:
        dq_ref[...] = acc_s[...]

    @pl.when(block == pl.num_programs(0) - 1)
    def _():
        dkv_ref[...] = dkv_s[...].astype(bf16)


def attn_bwd(
    info, queries, kv_all, grad_attn, exact, lse, dq_in, slots, segment, last, rows=512, keys=512
):
    width, count = queries.shape
    more = dq_in is not None
    block = pl.BlockSpec((width, rows), lambda i, _: (0, i))
    return pl.pallas_call(
        functools.partial(attn_bwd_body, slots, keys, segment * count, more, last),
        grid_spec=pltpu.PrefetchScalarGridSpec(
            num_scalar_prefetch=1,
            grid=(count // rows,),
            in_specs=[
                block,
                pl.BlockSpec((2 * width, count), lambda i, _: (0, segment)),
                block,
                block,
                pl.BlockSpec((8, rows), lambda i, _: (0, i)),
            ]
            + [block] * more,
            out_specs=[block, pl.BlockSpec((2 * width, count), lambda i, _: (0, 0))],
            scratch_shapes=[
                pltpu.VMEM((slots, count, E), bf16),
                pltpu.VMEM((slots, count, E), bf16),
                pltpu.VMEM((width, rows), f32),
                pltpu.VMEM((2 * width, count), f32),
            ],
        ),
        out_shape=[
            shape((width, count), bf16 if last else f32),
            shape((2 * width, count), bf16),
        ],
        compiler_params=params(),
        cost_estimate=cost(16 * 10**9, 6 * 10**6, 4 * 10**6),
        name="attn_bwd",
    )(info, queries, kv_all, grad_attn, exact, lse, *([dq_in] if more else []))


def out_norm_body(starts, p0, p1, p2, p3, w_ref, x_ref, vec_ref, after_ref, n_ref, stat_ref, attn_ref, w_s):
    fewer = (attn_ref.shape[0] // E) // 4 * E
    w_s[...] = w_ref[: w_s.shape[1], :].T
    for n, piece in enumerate((p0, p1, p2, p3)):
        attn_ref[rows_at(starts[n], fewer), :] = piece[:fewer, :]

        @pl.when(starts[n] == 0)
        def _():
            attn_ref[fewer : piece.shape[0], :] = piece[fewer:, :]

    full, count = x_ref.shape
    for start in range(0, count, 256):
        cols = slice(start, start + 256)
        after = x_ref[:, cols].astype(f32) + (
            dot_nn(w_s[...], attn_ref[:, cols]) + vec_ref[:full, 6:7]
        )
        mean = jnp.sum(after, axis=0, keepdims=True) * (1.0 / full)
        center = after - mean
        inv = lax.rsqrt(jnp.sum(center * center, axis=0, keepdims=True) * (1.0 / full) + norm_eps)
        after_ref[:, cols] = after
        n_ref[:, cols] = (center * inv * vec_ref[:full, 2:3] + vec_ref[:full, 3:4]).astype(bf16)
        stat_ref[0:1, cols] = mean
        stat_ref[1:2, cols] = inv


def out_norm(starts, pieces, w_out, x_full, vectors, first):
    full = x_full.shape[0]
    rows, count = pieces[0].shape
    grid_spec = pltpu.PrefetchScalarGridSpec(
        num_scalar_prefetch=1,
        grid=(1,),
        in_specs=[whole(piece) for piece in pieces]
        + [
            pl.BlockSpec(w_out.shape, lambda i, _: (0, 0)),
            pl.BlockSpec((full, count), lambda i, _: (0, first)),
            pl.BlockSpec(vectors.shape, lambda i, _: (0, 0)),
        ],
        out_specs=[
            pl.BlockSpec((full, count), lambda i, _: (0, 0)),
            pl.BlockSpec((full, count), lambda i, _: (0, 0)),
            pl.BlockSpec((8, count), lambda i, _: (0, 0)),
            pl.BlockSpec((full, count), lambda i, _: (0, 0)),
        ],
        scratch_shapes=[pltpu.VMEM((full, full), bf16)],
    )
    return pl.pallas_call(
        out_norm_body,
        grid_spec=grid_spec,
        out_shape=[
            shape((full, count), f32),
            shape((full, count), bf16),
            shape((8, count), f32),
            shape((full, count), bf16),
        ],
        compiler_params=params(),
        cost_estimate=cost(2 * full * full * count, 10**7),
        name="out_norm",
    )(starts, *pieces, w_out, x_full, vectors)


def erf_parts(v):
    return 0.5 * (1.0 + lax.erf(v * (0.5**0.5))), jnp.exp(-0.5 * v * v)


def feed_body(n_ref, dy_ref, up_ref, down_t_ref, b_ref, act_ref, grad_ref, part_ref, bias_ref, up_s, down_s):
    step = pl.program_id(0)

    @pl.when(step == 0)
    def _():
        up_s[...] = up_ref[...].T
        down_s[...] = down_t_ref[...].T
        bias_ref[...] = jnp.zeros_like(bias_ref)

    pre = dot_nn(up_s[...], n_ref[...]) + b_ref[:, 0:1]
    grad_act = dot_nn(down_s[...], dy_ref[...])
    cdf, bell = erf_parts(pre)
    act_ref[...] = (pre * cdf).astype(bf16)
    grad = (grad_act * (cdf + pre * bell * 0.3989422804014327)).astype(bf16)
    grad_ref[...] = grad
    bias_ref[...] += dot_nn(grad, jnp.ones((grad.shape[1], 128), bf16))
    part_ref[0] = dot_nn(up_ref[...], grad).astype(bf16)


def feed(normed, dy, w_up, w_down_t, bias, block=256):
    full, count = normed.shape
    hidden = w_up.shape[1]
    cols = pl.BlockSpec((full, block), lambda i: (0, i))
    hid = pl.BlockSpec((hidden, block), lambda i: (0, i))
    return pl.pallas_call(
        feed_body,
        grid=(count // block,),
        in_specs=[
            cols,
            cols,
            pl.BlockSpec((full, hidden), lambda i: (0, 0)),
            pl.BlockSpec((full, hidden), lambda i: (0, 0)),
            pl.BlockSpec((hidden, 1), lambda i: (0, 0)),
        ],
        out_specs=[
            hid,
            hid,
            pl.BlockSpec((1, full, block), lambda i: (i, 0, 0)),
            pl.BlockSpec((hidden, 128), lambda i: (0, 0)),
        ],
        out_shape=[
            shape((hidden, count), bf16),
            shape((hidden, count), bf16),
            shape((count // block, full, block), bf16),
            shape((hidden, 128), f32),
        ],
        scratch_shapes=[pltpu.VMEM((hidden, full), bf16), pltpu.VMEM((hidden, full), bf16)],
        compiler_params=params(),
        cost_estimate=cost(6 * full * hidden * count, 2 * 10**7, 2 * hidden * count),
        name="feed",
    )(normed, dy, w_up, w_down_t, bias)


def second_back_body(index, mine_ref, got_ref, after_ref, dy_ref, stat_ref, vec_ref, out_ref, sums_ref):
    back = mine_ref[...] + got_ref[...].astype(f32)
    full = back.shape[0]
    mean, inv = stat_ref[0:1, :], stat_ref[1:2, :]
    unit = (after_ref[...] - mean) * inv
    grad = back * vec_ref[:full, 2:3]
    first = jnp.sum(grad, axis=0, keepdims=True) * (1.0 / full)
    second = jnp.sum(grad * unit, axis=0, keepdims=True) * (1.0 / full)
    total = dy_ref[...].astype(f32) + inv * (grad - first - unit * second)
    low = total.astype(bf16)
    out_ref[...] = low
    sums_ref[:, 0:1] = jnp.sum(back * unit, axis=1, keepdims=True)
    sums_ref[:, 1:2] = jnp.sum(back, axis=1, keepdims=True)
    sums_ref[:, 2:3] = jnp.sum(low.astype(f32), axis=1, keepdims=True)


def second_back(index, mine, got, after, dy, stats, vectors):
    full, count = mine.shape
    fixed = pl.BlockSpec((full, count), lambda i, c: (0, 0))
    moved = pl.BlockSpec((full, count), lambda i, c: (0, c[0]))
    return pl.pallas_call(
        second_back_body,
        grid_spec=pltpu.PrefetchScalarGridSpec(
            num_scalar_prefetch=1,
            grid=(1,),
            in_specs=[
                fixed,
                fixed,
                moved,
                moved,
                pl.BlockSpec((8, count), lambda i, c: (0, c[0])),
                pl.BlockSpec(vectors.shape, lambda i, c: (0, 0)),
            ],
            out_specs=[fixed, pl.BlockSpec((full, 8), lambda i, c: (0, 0))],
        ),
        out_shape=[shape((full, count), bf16), shape((full, 8), f32)],
        compiler_params=params(),
        cost_estimate=cost(20 * full * count, 5 * 10**6),
        name="second_back",
    )(index, mine, got, after, dy, stats, vectors)


def attn_grad_body(info, p0, p1, p2, p3, w_ref, branch_ref, out_ref):
    count = p0.shape[1]
    width = out_ref.shape[0]
    weights = w_ref[rows_at(info[0], width), :]
    real = lax.broadcasted_iota(jnp.int32, (width, 1), 0) < info[1]
    for n, piece in enumerate((p0, p1, p2, p3)):
        cols = pl.ds(pl.multiple_of(info[2 + n] * count, 128), count)
        branch_ref[:, cols] = piece[...]
        out_ref[:, cols] = jnp.where(real, dot_nn(weights, piece[...]), 0.0).astype(bf16)


def attn_grad(info, pieces, w_out, width):
    full, quarter = pieces[0].shape
    results = [shape((full, 4 * quarter), bf16), shape((width, 4 * quarter), bf16)]
    return pl.pallas_call(
        attn_grad_body,
        grid_spec=pltpu.PrefetchScalarGridSpec(
            num_scalar_prefetch=1,
            grid=(1,),
            in_specs=[whole(array) for array in (*pieces, w_out)],
            out_specs=[whole(result) for result in results],
        ),
        out_shape=results,
        compiler_params=params(),
        cost_estimate=cost(8 * full * quarter * width, 10**7),
        name="attn_grad",
    )(info, *pieces, w_out)


X_SWAP = [(0, 2), (2, 0), (1, 3), (3, 1)]
CORE_SWAP = [(0, 1), (1, 0), (2, 3), (3, 2)]


def swap_x(array):
    return lax.ppermute(array, "col", X_SWAP)


def swap_core(array):
    return lax.ppermute(array, "col", CORE_SWAP)


def swap_seq(array):
    return lax.ppermute(array, "seq", [(0, 1), (1, 0)])


def ring(array, axis, shift):
    count = lax.axis_size(axis)
    return lax.ppermute(array, axis, [(i, (i + shift) % count) for i in range(count)])


def after(array, *done):
    return lax.optimization_barrier((array,) + done)[0]


def gather_col(shard):
    other = swap_x(shard)
    beside = swap_core(jnp.stack([shard, other]))
    return shard, other, beside[0], beside[1]


def gather_col_after(shard, *done):
    other = after(swap_x(shard), *done)
    beside = swap_core(jnp.stack([shard, other]))
    return shard, other, beside[0], beside[1]


def scatter_col(parts, x_bit, core_bit):
    by_core = parts.reshape((2, 2) + parts.shape[1:])
    mine = lax.dynamic_index_in_dim(by_core, core_bit, 1, keepdims=False)
    theirs = lax.dynamic_index_in_dim(by_core, 1 - core_bit, 1, keepdims=False)
    got = swap_core(theirs)

    def of(index):
        return lax.dynamic_index_in_dim(mine, index, 0, keepdims=False).astype(
            f32
        ) + lax.dynamic_index_in_dim(got, index, 0, keepdims=False).astype(f32)

    return got, of(x_bit), swap_x(of(1 - x_bit).astype(bf16))


def seq_halves(partials):
    seq_index = lax.axis_index("seq")
    chunks = [p.reshape(2, 4, p.shape[0] // 8, p.shape[1]) for p in partials]
    mine = [lax.dynamic_index_in_dim(c, seq_index, 0, keepdims=False) for c in chunks]
    theirs = jnp.stack(
        [lax.dynamic_index_in_dim(c, 1 - seq_index, 0, keepdims=False) for c in chunks]
    )
    return jnp.stack(mine), swap_seq(theirs)


def row_chunk(halves, offset):
    index = (lax.axis_index("row") + offset) % 4

    def of(array):
        return lax.dynamic_index_in_dim(array, index, 1, keepdims=False).astype(f32)

    return of(halves[0]) + of(halves[1])


def row_sum_one(halves):
    far = row_chunk(halves, 2).astype(bf16)
    if far.shape[0] == 2:
        return ring(far[0], "row", 1), ring(far[1], "row", -1)
    cut = far.shape[2] // 256 * 128
    return ring(far[0, :, :cut], "row", 1), ring(far[0, :, cut:], "row", -1)


def row_sum_two(halves, far):
    to_right, to_left = row_chunk(halves, 1), row_chunk(halves, 3)
    one, two = (part.astype(f32) for part in far)
    if to_right.shape[0] == 2:
        to_right = jnp.stack([to_right[0] + one, to_right[1]])
        to_left = jnp.stack([to_left[0], to_left[1] + two])
    else:
        cut = one.shape[1]
        to_right = jnp.concatenate([to_right[0, :, :cut] + one, to_right[0, :, cut:]], axis=1)[None]
        to_left = jnp.concatenate([to_left[0, :, :cut], to_left[0, :, cut:] + two], axis=1)[None]
    return ring(to_right.astype(bf16), "row", 1), ring(to_left.astype(bf16), "row", -1)


def row_sum_end(halves, near):
    return row_chunk(halves, 0) + near[0].astype(f32) + near[1].astype(f32)


def scatter_plain(partial):
    return lax.psum_scatter(partial.astype(f32), ("seq", "row"), scatter_dimension=0, tiled=True)


def combine_axis(array, axis, join):
    total = array
    for shift in range(1, lax.axis_size(axis)):
        total = join(total, ring(array, axis, shift))
    return total


def on_device(
    tokens,
    prefix,
    ln1_gain,
    ln1_bias,
    w_qkv,
    b_qv,
    w_out,
    b_out,
    ln2_gain,
    ln2_bias,
    w_up,
    b_up,
    w_down,
    b_down,
    cotangent,
):
    seq_count = lax.axis_size("seq")
    row_count = lax.axis_size("row")
    col_count = lax.axis_size("col")
    fast = seq_count == 2 and row_count == 4
    seq_index = lax.axis_index("seq")
    row_index = lax.axis_index("row")
    col_index = lax.axis_index("col")
    x_bit = col_index // 2
    core_bit = col_index % 2
    span, part = tokens.shape[1], tokens.shape[2]
    full = part * col_count
    quarter = span // col_count
    fewer = H // col_count
    slots = fewer + 1
    width = slots * E
    spare = width - part

    def by_index(pieces):
        own, across, beside, other = pieces
        even = (jnp.where(core_bit == 0, own, beside), jnp.where(core_bit == 0, across, other))
        odd = (jnp.where(core_bit == 0, beside, own), jnp.where(core_bit == 0, other, across))
        return jnp.concatenate(
            [
                jnp.where(x_bit == 0, even[0], even[1]),
                jnp.where(x_bit == 0, odd[0], odd[1]),
                jnp.where(x_bit == 0, even[1], even[0]),
                jnp.where(x_bit == 0, odd[1], odd[0]),
            ],
            axis=1,
        )

    def first_head(device):
        return jnp.where(device == 0, 0, 1 + fewer * device)

    head_first = first_head(col_index)
    head_count = jnp.where(col_index == 0, fewer + 1, fewer)
    column_shift = head_first * E - col_index * part
    info = jnp.stack([prefix[0], seq_index * span]).astype(jnp.int32)
    order = jnp.stack([col_index, col_index ^ 2, col_index ^ 1, col_index ^ 3]).astype(jnp.int32)

    x_shard = tokens[0].T
    dy_shard = cotangent[0].T
    part_rows = w_qkv.shape[0]
    w_flat = w_qkv.reshape(part_rows, 3 * part)

    def own_rows(array):
        return lax.dynamic_slice_in_dim(array, col_index * part, part, 0)

    vectors = jnp.stack(
        [ln1_gain, ln1_bias, ln2_gain, ln2_bias, b_qv[0], b_qv[1], own_rows(b_out)], axis=1
    )
    x_sent = jnp.concatenate([x_shard, jnp.pad(vectors, ((0, 0), (0, 121)))], axis=1)

    slot_column = lax.broadcasted_iota(jnp.int32, (1, 3 * width), 1)
    slot_part, slot_index = slot_column // width, slot_column % width
    slot_source = jnp.where(slot_index < head_count * E, slot_index + column_shift, -1)
    own_row = lax.broadcasted_iota(jnp.int32, (3 * part, 1), 0)
    pick_own = ((own_row // part == slot_part) & (own_row % part == slot_source)).astype(bf16)
    next_row = lax.broadcasted_iota(jnp.int32, (3 * spare, 1), 0)
    pick_next = (
        (next_row // spare == slot_part) & (next_row % spare + part == slot_source)
    ).astype(bf16)
    next_to_here = [(i + 1, i) for i in range(col_count - 1)]
    here_to_next = [(i, i + 1) for i in range(col_count - 1)]

    def edge_of(array):
        return jnp.concatenate([array[:, p * part : p * part + spare] for p in range(3)], axis=1)

    if fast:
        left = ring(w_flat, "row", 1)
        right = ring(w_flat, "row", -1)
        x_pieces = gather_col(x_sent)
        x_before = lax.ppermute(x_shard, "seq", [(0, 1)])
        x_full, normed_one, stats_one, columns = first_norm(order, x_pieces, span)
        before_pieces = gather_col_after(after(x_before, x_pieces[1]), normed_one)
        near_edge = lax.ppermute(
            jnp.concatenate([edge_of(w_flat), edge_of(left), edge_of(right)]), "col", next_to_here
        )
        cut = part_rows // 32 * 16 + 16
        far_a = ring(after(left[:cut], normed_one), "row", 1)
        far_b = ring(after(right[cut:], normed_one), "row", -1)
        far_edge = lax.ppermute(
            jnp.concatenate([edge_of(far_a), edge_of(far_b)]), "col", next_to_here
        )
        w_order = ((row_index - jnp.arange(4, dtype=jnp.int32)) % 4).astype(jnp.int32)
        _, normed_before, _ = first_norm(order, before_pieces, span, columns)
        w_heads = head_weights(
            w_order,
            [w_flat, left, right, far_a, far_b, near_edge, after(far_edge, normed_before)],
            pick_own,
            pick_next,
        )
        where = jnp.stack([seq_index, head_first * E]).astype(jnp.int32)
        queries, kv_all = project(where, w_heads, columns, normed_one, normed_before)
        attn_one = attn_fwd(info, queries, kv_all, slots, 0)
        attn_pieces_one = gather_col(attn_one[0])
        attn_two = attn_fwd(info, after(queries, attn_one[3]), kv_all, slots, 1)
        attn_pieces_two = gather_col(attn_two[0])
        dy_pieces = gather_col(after(dy_shard, attn_two[3], attn_pieces_one[1]))

        some = part_rows // 64 * 16 + 16
        piece = after(
            lax.dynamic_slice_in_dim(w_out, col_index * (some - 16), some, 0), far_a, far_b
        )
        mine = jnp.concatenate([ring(piece, "row", 1), ring(piece, "row", 2), ring(piece, "row", -1)])
        mine = after(mine, attn_one[3])
        across = swap_x(mine)
        beside = swap_core(jnp.concatenate([mine, across]))
        starts = [row_index * part_rows]
        plan = [(0, 0, part_rows, 0)]
        for which, base, device in ((1, 0, 0), (2, 0, 1), (3, 0, 2), (3, 3 * some, 3)):
            for index, away in enumerate((1, 2, 3)):
                plan.append((which, base + index * some, some, len(starts)))
                starts.append((row_index - away) % 4 * part_rows + order[device] * (some - 16))
        w_out_all = assemble(
            jnp.stack(starts).astype(jnp.int32), [w_out, mine, across, beside], plan, full, E
        )

        some = part_rows // 32 * 16 + 16
        other = part_rows - some
        w_down_rows = w_down.T
        piece = jnp.concatenate(
            [
                lax.dynamic_slice_in_dim(w_up, seq_index * other, some, 0),
                lax.dynamic_slice_in_dim(w_down_rows, seq_index * other, some, 0),
            ]
        )
        piece = after(piece, far_a, far_b)
        up_left = ring(piece, "row", 1)
        up_right = ring(piece, "row", -1)
        near_mine = after(jnp.concatenate([up_left, up_right]), attn_one[3])
        near_theirs = swap_seq(near_mine)
        far_mine = jnp.concatenate(
            [ring(near_mine[:some], "row", 1), ring(near_mine[3 * some :], "row", -1)]
        )
        far_mine = after(far_mine, attn_two[3])
        far_theirs = swap_seq(far_mine)

        def weight(shard, base):
            starts = [row_index * part_rows]
            plan = [(0, 0, part_rows, 0)]
            for which, start, away, bit in (
                (1, base, 1, seq_index),
                (1, 2 * some + base, 3, seq_index),
                (2, base, 1, 1 - seq_index),
                (2, 2 * some + base, 3, 1 - seq_index),
                (3, base, 2, seq_index),
                (4, base, 2, 1 - seq_index),
            ):
                plan.append((which, start, some, len(starts)))
                starts.append((row_index - away) % 4 * part_rows + bit * other)
            return assemble(
                jnp.stack(starts).astype(jnp.int32),
                [shard, near_mine, near_theirs, far_mine, far_theirs],
                plan,
                full,
            )

        w_up_all = weight(w_up, 0)
        w_down_t = weight(w_down_rows, some)
    else:
        x_pieces = gather_col(x_sent)
        x_full, normed_one, stats_one, columns = first_norm(order, x_pieces, span)
        w_all = lax.all_gather(w_flat, "row", axis=0, tiled=True)
        edges = lax.ppermute(edge_of(w_all), "col", next_to_here)
        w_heads = (dot_nn(w_all, pick_own) + dot_nn(edges, pick_next)).astype(bf16)
        bias = lax.dynamic_slice_in_dim(columns, head_first * E, width, 0)
        projected = dot_tn(w_heads, normed_one)
        queries = (
            (projected[:width] + bias[:, 4:5]).astype(bf16) * E ** (-0.5)
        ).astype(bf16)
        keyvals = jnp.concatenate(
            [projected[width : 2 * width], projected[2 * width :] + bias[:, 5:6]]
        ).astype(bf16)
        kv_all = lax.all_gather(keyvals, "seq", axis=1, tiled=True)
        attn_one = attn_fwd(info, queries, kv_all, slots, 0)
        attn_two = attn_fwd(info, queries, kv_all, slots, 1)
        attn_pieces_one = gather_col(attn_one[0])
        attn_pieces_two = gather_col(attn_two[0])
        dy_pieces = gather_col(dy_shard)
        w_out_all = jnp.pad(lax.all_gather(w_out, "row", axis=0, tiled=True), ((0, E), (0, 0)))
        w_up_all = lax.all_gather(w_up, "row", axis=0, tiled=True)
        w_down_t = lax.all_gather(w_down.T, "row", axis=0, tiled=True)
    dy_full = assemble(
        (order * part).astype(jnp.int32), dy_pieces, [(n, 0, part, n) for n in range(4)], full
    )

    head_rows = (first_head(order) * E).astype(jnp.int32)
    normal_one = out_norm(head_rows, attn_pieces_one, w_out_all, x_full, columns, 0)
    normal_two = out_norm(head_rows, attn_pieces_two, w_out_all, x_full, columns, 1)

    def joined(index):
        return jnp.concatenate([normal_one[index], normal_two[index]], axis=1)

    after_attn, normed_two, stats_two, attn_all = (joined(i) for i in range(4))
    exact = jnp.concatenate([attn_one[1], attn_two[1]], axis=1)
    lse = jnp.concatenate([attn_one[2], attn_two[2]], axis=1)
    tops = jnp.max(jnp.maximum(attn_one[3], attn_two[3]), axis=1)

    slot_head = jnp.arange(slots, dtype=jnp.int32)
    head_ids = jnp.arange(H, dtype=jnp.int32)
    my_top = jnp.where(slot_head < head_count, tops[:slots], neg_fill)
    placed_top = jnp.max(
        jnp.where(head_ids[None] == (head_first + slot_head)[:, None], my_top[:, None], neg_fill),
        axis=0,
    )
    placed_top = jnp.pad(placed_top, (0, full - H))

    act, grad_pre, back_parts, bup_sums = feed(
        normed_two, dy_full, w_up_all, w_down_t, b_up.astype(f32)[:, None]
    )
    back_core, back_mine, back_got = scatter_col(back_parts, x_bit, core_bit)
    act_then = after(act, back_core)
    up_partial = dot_nt(normed_two, after(grad_pre, back_core)).astype(bf16)
    down_partial = dot_nt(dy_full, act_then).astype(bf16)

    branch_rows, row_sums = second_back(
        col_index[None].astype(jnp.int32),
        back_mine,
        back_got,
        after_attn,
        dy_full,
        stats_two,
        columns,
    )
    branch_pieces = gather_col(branch_rows)
    down = dot_nn(w_down_t, after(act, branch_rows)).astype(bf16).reshape(col_count, part, span)
    head_info = jnp.concatenate([jnp.stack([head_first * E, head_count * E]), order]).astype(jnp.int32)
    branch, grad_attn = attn_grad(head_info, branch_pieces, w_out_all, width)
    out_partial = dot_nt(attn_all, own_rows(branch)).astype(bf16)
    middle = jnp.concatenate([row_sums[:, :3].T, placed_top[None]])

    def join(one, two):
        return jnp.concatenate([one[:3] + two[:3], jnp.maximum(one[3:4], two[3:4]), one[4:] + two[4:]])

    middle = after(middle, grad_attn)
    middle = join(middle, swap_x(middle))
    middle = join(middle, swap_core(middle))

    if fast:
        feed_halves = seq_halves([up_partial, down_partial])
        feed_halves = (feed_halves[0], after(feed_halves[1], grad_attn))
        feed_far = row_sum_one(feed_halves)
        out_halves = seq_halves([out_partial])
        dq_one, dkv_one = attn_bwd(
            info, queries, kv_all, after(grad_attn, out_partial), exact, lse, None, slots, 0, False
        )
        dkv_there = lax.ppermute(dkv_one, "seq", [(1, 0)])
        feed_near = row_sum_two(feed_halves, (after(feed_far[0], dq_one), after(feed_far[1], dq_one)))
        dq, dkv_two = attn_bwd(
            info, after(queries, dq_one), kv_all, grad_attn, exact, lse, dq_one, slots, 1, True
        )
        dkv = jnp.where(
            seq_index == 0,
            (dkv_one.astype(f32) + after(dkv_there, dq).astype(f32)).astype(bf16),
            dkv_two,
        )
        heads_grad = jnp.concatenate([dq, dkv])
        one_parts = dot_nn(w_heads, heads_grad).astype(bf16).reshape(col_count, part, span)
        one_core, one_mine, one_got = scatter_col(one_parts, x_bit, core_bit)
        partial = dot_nt(normed_one, after(heads_grad, one_parts)).astype(bf16)
        halves = seq_halves([partial])
        feed_sums = row_sum_end(
            feed_halves, (after(feed_near[0], one_core, partial), after(feed_near[1], one_core, partial))
        )
        grad_w_up, grad_w_down = feed_sums[0], feed_sums[1].T
        _, down_mine, down_got = scatter_col(after(down, one_mine), x_bit, core_bit)
        last_halves = (
            jnp.concatenate([halves[0], out_halves[0]], axis=3),
            jnp.concatenate([after(halves[1], one_got), after(out_halves[1], one_core)], axis=3),
        )
        last_far = row_sum_one(last_halves)
        last_near = row_sum_two(last_halves, last_far)
        last = row_sum_end(last_halves, last_near)[0]
        summed, out_columns = last[:, : 3 * width], last[:, 3 * width :].astype(bf16)
    else:
        dq, pieces = None, []
        for segment in range(seq_count):
            dq, dkv_one = attn_bwd(
                info, queries, kv_all, grad_attn, exact, lse, dq, slots, segment, segment == seq_count - 1
            )
            pieces.append(dkv_one)
        dkv = lax.psum_scatter(
            jnp.concatenate(pieces, axis=1), "seq", scatter_dimension=1, tiled=True
        )
        grad_w_up = scatter_plain(up_partial)
        grad_w_down = scatter_plain(down_partial).T
        out_columns = scatter_plain(out_partial).astype(bf16)
        heads_grad = jnp.concatenate([dq, dkv])
        one_parts = dot_nn(w_heads, heads_grad).astype(bf16).reshape(col_count, part, span)
        _, one_mine, one_got = scatter_col(one_parts, x_bit, core_bit)
        summed = scatter_plain(dot_nt(normed_one, heads_grad).astype(bf16))
        _, down_mine, down_got = scatter_col(down, x_bit, core_bit)
    summed = summed.reshape(-1, 3, width)
    grad_w_out = by_index(gather_col(out_columns)).astype(f32)
    block_out = (
        own_rows(after_attn) + down_mine + down_got.astype(f32) + b_down.astype(f32)[:, None]
    ).astype(bf16)

    def to_owner(array):
        wide_array = jnp.pad(array, ((0, 0), (0, 0), (spare, 0)))
        shifted = wide_array[:, :, spare : spare + width]
        for shift in range(1, col_count):
            amount = 1 + fewer * shift
            offset = amount * E - shift * part
            shifted = jnp.where(
                col_index == shift, wide_array[:, :, spare - offset : spare - offset + width], shifted
            )
        sent = lax.ppermute(shifted[:, :, part:].reshape(-1, 3 * spare), "col", here_to_next)
        return shifted[:, :, :part] + jnp.pad(
            sent.reshape(-1, 3, spare), ((0, 0), (0, 0), (0, part - spare))
        )

    grad_w_qkv = to_owner(summed)
    head_sums = jnp.sum(heads_grad.astype(f32), axis=1)
    head_sums = jnp.stack([head_sums[:width], head_sums[2 * width :]])
    head_sums = lax.dynamic_update_slice_in_dim(
        jnp.zeros((2, full + E), f32), head_sums, head_first * E, 1
    )[:, :full]

    back_one = one_mine + one_got.astype(f32)
    unit_one = (x_shard.astype(f32) - stats_one[0:1]) * stats_one[1:2]
    unit_grad = back_one * ln1_gain.astype(f32)[:, None]
    sums = jnp.stack([jnp.sum(unit_grad, axis=0), jnp.sum(unit_grad * unit_one, axis=0)])
    sums = jnp.concatenate([jnp.pad(sums, ((0, 0), (0, full - span))) if full > span else sums, head_sums])
    sums = sums + swap_x(sums)
    sums = sums + swap_core(sums)
    bias_grads = lax.dynamic_slice_in_dim(sums[2:], col_index * part, part, 1)
    sums = sums[:2, :span] / full
    grad_tokens = own_rows(branch).astype(f32) + stats_one[1:2] * (
        unit_grad - sums[0:1] - unit_one * sums[1:2]
    )

    small = jnp.concatenate(
        [
            jnp.sum(back_one * unit_one, axis=1),
            jnp.sum(back_one, axis=1),
            jnp.sum(dy_shard.astype(f32), axis=1),
            jnp.zeros((part,), f32),
        ]
    )
    middle = jnp.concatenate(
        [
            middle,
            bup_sums[:, 0][None],
            small[None],
            jnp.pad(bias_grads.reshape(1, -1), ((0, 0), (0, full - 2 * part))),
        ]
    )
    for axis in ("seq", "row"):
        middle = combine_axis(middle, axis, join)
    row_vectors, head_max, grad_b_up = middle[:3], middle[3, :H], middle[4]
    own_vectors = lax.dynamic_slice_in_dim(row_vectors, col_index * part, part, 1)

    def piece(start, length):
        return middle[5, start : start + length]

    root_clip = jnp.sqrt(clip_limit / jnp.maximum(head_max, clip_limit))
    column_head = (col_index * part + jnp.arange(part, dtype=jnp.int32)) // E
    one_hot = (column_head[:, None] == head_ids[None, :]).astype(f32)
    column_root = jnp.sum(one_hot * root_clip[None, :], axis=1)
    scale_three = jnp.stack([column_root, column_root, jnp.ones_like(column_root)])
    clipped_qkv = w_qkv.astype(f32) * scale_three[None]
    return (
        block_out.T[None],
        grad_tokens.T[None],
        piece(0, part),
        piece(part, part),
        grad_w_qkv,
        middle[6, : 2 * part].reshape(2, part),
        grad_w_out,
        row_vectors[2],
        own_vectors[0],
        own_vectors[1],
        grad_w_up,
        grad_b_up,
        grad_w_down,
        piece(2 * part, part),
        clipped_qkv,
        head_max,
    )


def solution(mesh):
    placed = (
        P("row", "seq", "col"),
        P("row"),
        P("col"),
        P("col"),
        P("row", None, "col"),
        P(None, "col"),
        P("row", None),
        P(),
        P("col"),
        P("col"),
        P("row", "col"),
        P("col"),
        P("col", "row"),
        P("col"),
        P("row", "seq", "col"),
    )
    return jax.shard_map(
        on_device,
        mesh=mesh,
        in_specs=placed,
        out_specs=(
            P("row", "seq", "col"),
            P("row", "seq", "col"),
            P("col"),
            P("col"),
            P(("seq", "row"), None, "col"),
            P(None, "col"),
            P(("seq", "row"), None),
            P(),
            P("col"),
            P("col"),
            P(("seq", "row"), "col"),
            P("col"),
            P("col", ("seq", "row")),
            P("col"),
            P("row", None, "col"),
            P(),
        ),
        check_vma=False,
    )
```

time: 634 us -> 514 us (0.81)
  waiting for transfers between devices: 243 us -> 169 us
  Pallas kernels: 50.1 us -> 115 us
  matrix products: 77.1 us -> 21.5 us
  starting transfers between devices: 133 us -> 82.7 us
  other arithmetic: 56.7 us -> 47.7 us
    pallas_call x3 -> x17, Pallas kernels: 50.1 us -> 115 us  [the longest x2 21 us: attn_bwd(): pl.pallas_call(functools.partial(attn_bwd_body, slots, keys, segment * co...]
    ppermute x43 -> x23, waiting for transfers between devices: 123 us -> 66.1 us  [ring(): lax.ppermute(array, axis, [(i, (i + shift) % count) for i in range(count)])]
    ppermute x9, waiting for transfers between devices: 73.1 us -> 37 us  [the longest x5 20.5 us: swap_seq(): return lax.ppermute(array, 'seq', [(0, 1), (1, 0)])]
    ppermute x43 -> x23, starting transfers between devices: 82.1 us -> 46.5 us  [ring(): lax.ppermute(array, axis, [(i, (i + shift) % count) for i in range(count)])]
    dot_general x10 -> x2, matrix products: 43.7 us -> 8.74 us  [dot_nn(): lax.dot_general(left, right, (((1,), (0,)), ((), ())), preferred_element_...]
    ppermute x12 -> x13, waiting for transfers between devices: 43.7 us -> 65.4 us  [swap_x(): return lax.ppermute(array, 'col', X_SWAP)]
    dot_general x5 -> x0, matrix products: 14.6 us -> none  [dot_tn(): lax.dot_general(left, right, (((0,), (0,)), ((), ())), preferred_element_...]
    unnamed x125 -> x112, local copies, waits for them, and re-layouts: 5.25 us -> 19.4 us
  transfers between devices with their start and end apart: 87 -> 59, of which waited for: 36 -> 23; matrix products, arithmetic and copies ran while one was open for 17% -> 22% of each run, Pallas kernels for 0% -> 13%
where the time goes in v2:
time: 514 us; the launch traced here: 506 us
  waiting for transfers between devices  169 us (33%)
  Pallas kernels  115 us (22%)
  starting transfers between devices  82.7 us (16%)
  local copies, waits for them, and re-layouts  68.1 us (13%)
  other arithmetic  47.7 us (9%)
  matrix products  21.5 us (4%)
    ppermute x23, waiting for transfers between devices, ring(): lax.ppermute(array, axis, [(i, (i + shift) % count) for i in range(count)])  66.1 us
    ppermute x13, waiting for transfers between devices, swap_x(): return lax.ppermute(array, 'col', X_SWAP)  65.4 us
    ppermute x23, starting transfers between devices, ring(): lax.ppermute(array, axis, [(i, (i + shift) % count) for i in range(count)])  46.5 us
    pallas_call x2, Pallas kernels, attn_bwd(): pl.pallas_call(functools.partial(attn_bwd_body, slots, keys, segment * co...  21 us
    ppermute x5, waiting for transfers between devices, swap_seq(): return lax.ppermute(array, 'seq', [(0, 1), (1, 0)])  20.5 us
    pallas_call x1, Pallas kernels, feed(): pl.pallas_call(feed_body, grid=(count // block,), in_specs=[cols, cols, p...  19.7 us
    unnamed x112, local copies, waits for them, and re-layouts  19.4 us
    ppermute x13, starting transfers between devices, swap_x(): return lax.ppermute(array, 'col', X_SWAP)  17.5 us
  transfers between devices with their start and end apart: 59, of which 23 were waited for; matrix products, arithmetic and copies ran while one was open for 22% of the time, Pallas kernels for 13%

profile of v2, /device:TPU:0, one launch (start us, length us, event | category | flops | bytes accessed | tf_op | source)
XLA Modules:
  0.0 506.1 jit_solution(5244793341203598265)
XLA Ops:
  2.5 5.1 %collective-permute-start.1 = (bf16[272,816]{1,0:T(8,128)(2,1)S(1)}, bf16[272,816]{1,0:T(8,128)(2,1)}, u32[]{:S(2)}, u32[]{:S(2)}) collective-permute-start(bf16[272,816]{1,0:T(8,128)(2,1)S(1)} %copy.119.own), channel_id=1, source_target_pairs={{0,12},{4,0},{8,4},{12,8},{1,13},{5,1},{9,5},{13,9},{2,14},{6,2},{... | collective-permute-start | bytes 1331720 | tf_op jit(solution)/shard_map/ppermute | solution.py:630
  7.6 3.4 collective-permute-start.8
  12.1 2.0 fusion.75
  36.0 4.6 first_norm.2
  40.6 6.6 %collective-permute-done.9.p1 = bf16[272,1024]{1,0:T(8,128)(2,1)S(1)} collective-permute-done((bf16[272,1024]{1,0:T(8,128)(2,1)S(1)}, bf16[272,1024]{1,0:T(8,128)(2,1)S(1)}, u32[]{:S(2)}, u32[]{:S(2)}) %collective-permute-start.9) | collective-permute-done | bytes 557088 | tf_op jit(solution)/shard_map/ppermute | solution.py:617
  47.2 3.5 collective-permute-start.5
  50.9 5.8 %collective-permute-done.5.far_b = bf16[128,816]{1,0:T(8,128)(2,1)S(1)} collective-permute-done((bf16[128,816]{1,0:T(8,128)(2,1)S(1)}, bf16[128,816]{1,0:T(8,128)(2,1)S(1)}, u32[]{:S(2)}, u32[]{:S(2)}) %collective-permute-start.5) | collective-permute-done | bytes 208928 | tf_op jit(solution)/shard_map/ppermute | solution.py:630
  56.7 5.0 collective-permute-done.4.far_a
  63.7 3.5 collective-permute-start.15
  67.5 29.6 %collective-permute-done.15 = bf16[80,1088]{1,0:T(8,128)(2,1)S(1)} collective-permute-done((bf16[80,1088]{1,0:T(8,128)(2,1)S(1)}, bf16[80,1088]{1,0:T(8,128)(2,1)S(1)}, u32[]{:S(2)}, u32[]{:S(2)}) %collective-permute-start.15) | collective-permute-done | bytes 174112 | tf_op jit(solution)/shard_map/ppermute | solution.py:630
  97.1 10.2 %collective-permute-start.13 = (bf16[80,1088]{1,0:T(8,128)(2,1)S(1)}, bf16[80,1088]{1,0:T(8,128)(2,1)S(1)}, u32[]{:S(2)}, u32[]{:S(2)}) collective-permute-start(bf16[80,1088]{1,0:T(8,128)(2,1)S(1)} %copy-done.32), channel_id=1, source_target_pairs={{0,4},{4,8},{8,12},{12,0},{1,5},{5,9},{9,13},{13,1},{2,6},{6,10},{... | collective-permute-start | bytes 522248 | tf_op jit(solution)/shard_map/ppermute | solution.py:630
  112.1 4.5 first_norm.3
  116.6 6.8 %head_weights.1.w_ref = bf16[1088,960]{1,0:T(8,128)(2,1)} custom-call(s32[4]{0:T(128)S(1)} %and_select_fusion.2.order, bf16[272,816]{1,0:T(8,128)(2,1)S(1)} %copy.119.own, bf16[272,816]{1,0:T(8,128)(2,1)} %collective-permute-done.left, bf16[272,816]{1,0:T(8,128)(2,1)} %collective-permute-done.1.right, bf16[144,816]{1,0:T(8,128)(2,1)S(1)} %collective-permute-done.4.far_a, ...), custom_call_target="tpu_custom_call" | custom-call | flops 2005401600 | bytes 6000000 | tf_op jit(solution)/shard_map/head_weights/pallas_call | solution.py:146
  125.0 9.2 %project.1 = (bf16[320,1024]{1,0:T(8,128)(2,1)S(1)}, bf16[640,2048]{1,0:T(8,128)(2,1)}) custom-call(s32[2]{0:T(128)S(1)} %pad_add_fusion.2.info, bf16[1088,960]{1,0:T(8,128)(2,1)S(1)} %copy-done.6, f32[1152,128]{1,0:T(8,128)S(1)} %get-tuple-element.83.refs_0_.bias_ref.vec_ref, bf16[1088,1024]{1,0:T(8,128)(2,1)} %get-tuple-element.78.own_ref, ...), custom_call_target="tpu_custom_call" | custom-call | flops 3565158400 | bytes 10000000 | tf_op jit(solution)/shard_map/project/pallas_call | solution.py:192
  134.2 8.3 %attn_fwd.2 = (bf16[320,512]{1,0:T(8,128)(2,1)S(1)}, f32[320,512]{1,0:T(8,128)S(1)}, f32[8,512]{1,0:T(8,128)S(1)}, f32[8,128]{1,0:T(8,128)S(1)}) custom-call(s32[2]{0:T(128)S(1)} %pad_add_fusion.1.info, bf16[320,1024]{1,0:T(8,128)(2,1)S(1)} %get-tuple-element.120.q_ref.refs_0_, bf16[640,2048]{1,0:T(8,128)(2,1)} %get-tuple-element.87.kv_ref.refs_1_), custom_call_target="tpu_custom_call" | custom-call | flops 8000000000 | bytes 6000000 | tf_op jit(solution)/shard_map/attn_fwd/pallas_call | solution.py:284
  142.6 2.1 collective-permute-start.22
  144.7 3.0 collective-permute-start.11
  149.3 2.6 collective-permute-start.24
  152.0 8.3 %attn_fwd.3 = (bf16[320,512]{1,0:T(8,128)(2,1)S(1)}, f32[320,512]{1,0:T(8,128)S(1)}, f32[8,512]{1,0:T(8,128)S(1)}, f32[8,128]{1,0:T(8,128)S(1)}) custom-call(s32[2]{0:T(128)S(1)} %pad_add_fusion.1.info, bf16[320,1024]{1,0:T(8,128)(2,1)S(1)} %get-tuple-element.120.q_ref.refs_0_, bf16[640,2048]{1,0:T(8,128)(2,1)} %get-tuple-element.87.kv_ref.refs_1_), custom_call_target="tpu_custom_call" | custom-call | flops 8000000000 | bytes 6000000 | tf_op jit(solution)/shard_map/attn_fwd/pallas_call | solution.py:284
  161.4 2.0 collective-permute-start.18
  163.5 4.2 collective-permute-done.16.refs_2_
  167.8 2.5 collective-permute-start.26
  171.3 3.5 collective-permute-done.18.p1
  175.9 10.8 %collective-permute-done.26.refs_1_ = bf16[272,1024]{1,0:T(8,128)(2,1)S(1)} collective-permute-done((bf16[272,1024]{1,0:T(8,128)(2,1)S(1)}, bf16[272,1024]{1,0:T(8,128)(2,1)S(1)}, u32[]{:S(2)}, u32[]{:S(2)}) %collective-permute-start.26) | collective-permute-done | bytes 557088 | tf_op jit(solution)/shard_map/ppermute | solution.py:617
  186.7 2.3 collective-permute-start.25
  190.2 13.6 %collective-permute-done.25.refs_4_ = bf16[288,1088]{1,0:T(8,128)(2,1)S(1)} collective-permute-done((bf16[288,1088]{1,0:T(8,128)(2,1)S(1)}, bf16[288,1088]{1,0:T(8,128)(2,1)S(1)}, u32[]{:S(2)}, u32[]{:S(2)}) %collective-permute-start.25) | collective-permute-done | bytes 626720 | tf_op jit(solution)/shard_map/ppermute | solution.py:625
  204.9 3.6 assemble.7.up_ref
  208.5 3.5 assemble.5.down_t_ref
  212.0 2.3 assemble.4.w_ref
  214.4 6.6 %out_norm.3 = (f32[1088,512]{1,0:T(8,128)}, bf16[1088,512]{1,0:T(8,128)(2,1)S(1)}, f32[8,512]{1,0:T(8,128)S(1)}, bf16[1088,512]{1,0:T(8,128)(2,1)}) custom-call(s32[4]{0:T(128)S(1)} %fusion.70.starts, bf16[320,512]{1,0:T(8,128)(2,1)S(1)} %get-tuple-element.95.p0, bf16[320,512]{1,0:T(8,128)(2,1)S(1)} %collective-permute-done.18.p1, ...), custom_call_target="tpu_custom_call" | custom-call | flops 1212153856 | bytes 10000000 | tf_op jit(solution)/shard_map/out_norm/pallas_call | solution.py:469
  220.9 6.7 %out_norm.2 = (f32[1088,512]{1,0:T(8,128)}, bf16[1088,512]{1,0:T(8,128)(2,1)S(1)}, f32[8,512]{1,0:T(8,128)S(1)}, bf16[1088,512]{1,0:T(8,128)(2,1)}) custom-call(s32[4]{0:T(128)S(1)} %fusion.70.starts, bf16[320,512]{1,0:T(8,128)(2,1)S(1)} %get-tuple-element.88.p0, bf16[320,512]{1,0:T(8,128)(2,1)S(1)} %collective-permute-done.11.p1, ...), custom_call_target="tpu_custom_call" | custom-call | flops 1212153856 | bytes 10000000 | tf_op jit(solution)/shard_map/out_norm/pallas_call | solution.py:469
  228.0 2.1 slice_bitcast_fusion.8
  230.1 2.1 assemble.6.dy_ref
  232.2 19.7 %feed.1 = (bf16[1088,1024]{1,0:T(8,128)(2,1)S(1)}, bf16[1088,1024]{1,0:T(8,128)(2,1)}, bf16[4,1088,256]{2,1,0:T(8,128)(2,1)}, f32[1088,128]{1,0:T(8,128)S(1)}) custom-call(bf16[1088,1024]{1,0:T(8,128)(2,1)} %copy-done.27, bf16[1088,1024]{1,0:T(8,128)(2,1)} %assemble.6.dy_ref, bf16[1088,1088]{1,0:T(8,128)(2,1)} %assemble.7.up_ref, ...), custom_call_target="tpu_custom_call" | custom-call | flops 7272923136 | bytes 20000000 | tf_op jit(solution)/shard_map/feed/pallas_call | solution.py:512
  260.2 3.3 convolution_convert_fusion.1
  266.0 3.3 convolution_convert_fusion
  269.3 9.5 %collective-permute-done.29.got_ref = bf16[1088,256]{1,0:T(8,128)(2,1)S(1)} collective-permute-done((bf16[1088,256]{1,0:T(8,128)(2,1)S(1)}, bf16[1088,256]{1,0:T(8,128)(2,1)S(1)}, u32[]{:S(2)}, u32[]{:S(2)}) %collective-permute-start.29) | collective-permute-done | bytes 557088 | tf_op jit(solution)/shard_map/ppermute | solution.py:617
  278.8 2.5 second_back.1
  286.5 9.1 %collective-permute-done.30.p1 = bf16[1088,256]{1,0:T(8,128)(2,1)S(1)} collective-permute-done((bf16[1088,256]{1,0:T(8,128)(2,1)S(1)}, bf16[1088,256]{1,0:T(8,128)(2,1)S(1)}, u32[]{:S(2)}, u32[]{:S(2)}) %collective-permute-start.30) | collective-permute-done | bytes 557088 | tf_op jit(solution)/shard_map/ppermute | solution.py:617
  298.8 6.2 %convolution_convert_fusion.3 = bf16[1088,1024]{1,0:T(8,128)(2,1)} fusion(bf16[1088,1088]{1,0:T(8,128)(2,1)} %assemble.5.down_t_ref, bf16[1088,1024]{1,0:T(8,128)(2,1)S(1)} %get-tuple-element.134), kind=kOutput, calls=%fused_computation.4 | convolution fusion | flops 2425421824 | bytes 6823936 | tf_op jit(solution)/shard_map/dot_general | solution.py:27
  306.4 5.1 attn_grad.1
  317.2 16.7 %attn_bwd.2 = (f32[320,1024]{1,0:T(8,128)S(1)}, bf16[640,1024]{1,0:T(8,128)(2,1)S(1)}) custom-call(s32[2]{0:T(128)S(1)} %pad_add_fusion.1.info, bf16[320,1024]{1,0:T(8,128)(2,1)S(1)} %copy-done.9, bf16[640,2048]{1,0:T(8,128)(2,1)} %get-tuple-element.87.kv_ref.refs_1_, bf16[320,1024]{1,0:T(8,128)(2,1)S(1)} %get-tuple-element.114.refs_2_, ...), custom_call_target="tpu_custom_call" | custom-call | flops 16000000000 | bytes 6000000 | tf_op jit(solution)/shard_map/attn_bwd/pallas_call | solution.py:393
  335.1 4.2 attn_bwd.3
  344.4 2.2 collective-permute-start.55
  348.4 8.2 %collective-permute-done.55 = bf16[136,1088]{1,0:T(8,128)(2,1)S(1)} collective-permute-done((bf16[136,1088]{1,0:T(8,128)(2,1)S(1)}, bf16[136,1088]{1,0:T(8,128)(2,1)S(1)}, u32[]{:S(2)}, u32[]{:S(2)}) %collective-permute-start.55) | collective-permute-done | bytes 295968 | tf_op jit(solution)/shard_map/ppermute | solution.py:630
  356.6 4.0 collective-permute-done.57
  361.5 2.0 collective-permute-start.58
  364.5 16.4 %collective-permute-done.32 = bf16[640,1024]{1,0:T(8,128)(2,1)S(1)} collective-permute-done((bf16[640,1024]{1,0:T(8,128)(2,1)S(1)}, bf16[640,1024]{1,0:T(8,128)(2,1)S(1)}, u32[]{:S(2)}, u32[]{:S(2)}) %collective-permute-start.32) | collective-permute-done | bytes 1310752 | tf_op jit(solution)/shard_map/ppermute | solution.py:982
  382.6 2.5 convolution_convert_fusion.2
  388.5 4.2 convolution_convert_fusion.4
  392.7 4.2 copy.122
  396.9 3.2 constant_dynamic-slice_fusion.4
  406.3 10.1 %collective-permute-done.36 = bf16[272,1024]{1,0:T(8,128)(2,1)S(1)} collective-permute-done((bf16[272,1024]{1,0:T(8,128)(2,1)S(1)}, bf16[272,1024]{1,0:T(8,128)(2,1)S(1)}, u32[]{:S(2)}, u32[]{:S(2)}) %collective-permute-start.36) | collective-permute-done | bytes 557088 | tf_op jit(solution)/shard_map/ppermute | solution.py:617
  416.5 2.3 multiply_reduce_fusion
  420.4 6.4 %collective-permute-done.45 = bf16[1,4,136,960]{3,2,1,0:T(8,128)(2,1)} collective-permute-done((bf16[1,4,136,960]{3,2,1,0:T(8,128)(2,1)}, bf16[1,4,136,960]{3,2,1,0:T(8,128)(2,1)}, u32[]{:S(2)}, u32[]{:S(2)}) %collective-permute-start.45) | collective-permute-done | bytes 1044512 | tf_op jit(solution)/shard_map/ppermute | solution.py:625
  426.8 2.7 add_bitcast_fusion.2
  444.5 3.1 collective-permute-done.41
  451.7 2.9 add_bitcast_fusion
  454.6 3.2 collective-permute-start.49
  464.1 3.9 collective-permute-start.50
  470.5 5.4 %collective-permute-done.48 = bf16[1,136,1232]{2,1,0:T(8,128)(2,1)S(1)} collective-permute-done((bf16[1,136,1232]{2,1,0:T(8,128)(2,1)S(1)}, bf16[1,136,1232]{2,1,0:T(8,128)(2,1)S(1)}, u32[]{:S(2)}, u32[]{:S(2)}) %collective-permute-start.48) | collective-permute-done | bytes 335136 | tf_op jit(solution)/shard_map/ppermute | solution.py:630
  475.9 3.5 collective-permute-done.50
  493.4 9.8 %collective-permute-done.35 = bf16[272,1024]{1,0:T(8,128)(2,1)S(1)} collective-permute-done((bf16[272,1024]{1,0:T(8,128)(2,1)S(1)}, bf16[272,1024]{1,0:T(8,128)(2,1)S(1)}, u32[]{:S(2)}, u32[]{:S(2)}) %collective-permute-start.35) | collective-permute-done | bytes 557088 | tf_op jit(solution)/shard_map/ppermute | solution.py:617
  503.2 2.6 fusion.24
  (359 shorter events, 130.7 us)
Async XLA Ops:
  2.5 27.5 %collective-permute-start.1 = (bf16[272,816]{1,0:T(8,128)(2,1)S(1)}, bf16[272,816]{1,0:T(8,128)(2,1)}, u32[]{:S(2)}, u32[]{:S(2)}) collective-permute-start(bf16[272,816]{1,0:T(8,128)(2,1)S(1)} %copy.119.own), channel_id=1, source_target_pairs={{0,12},{4,0},{8,4},{12,8},{1,13},{5,1},{9,5},{13,9},{2,14},{6,2},{... | collective-permute-start | bytes 1331720 | tf_op jit(solution)/shard_map/ppermute | solution.py:630
  7.6 23.4 %collective-permute-start = (bf16[272,816]{1,0:T(8,128)(2,1)S(1)}, bf16[272,816]{1,0:T(8,128)(2,1)}, u32[]{:S(2)}, u32[]{:S(2)}) collective-permute-start(bf16[272,816]{1,0:T(8,128)(2,1)S(1)} %copy.119.own), channel_id=1, source_target_pairs={{0,4},{4,8},{8,12},{12,0},{1,5},{5,9},{9,13},{13,1},{2,6},{6,10},{... | collective-permute-start | bytes 1331720 | tf_op jit(solution)/shard_map/ppermute | solution.py:630
  7.6 24.5 %collective-permute-start.8 = (bf16[272,1024]{1,0:T(8,128)(2,1)}, bf16[272,1024]{1,0:T(8,128)(2,1)S(1)}, u32[]{:S(2)}, u32[]{:S(2)}) collective-permute-start(bf16[272,1024]{1,0:T(8,128)(2,1)} %bitcast.9), channel_id=1, source_target_pairs={{0,16},{1,17},{2,18},{3,19},{4,20},{5,21},{6,22},{7,23},{8,24},{9,... | collective-permute-start | bytes 1671176 | tf_op jit(solution)/shard_map/ppermute | solution.py:807
  14.1 15.3 %collective-permute-start.2 = (bf16[272,1152]{1,0:T(8,128)(2,1)S(1)}, bf16[272,1152]{1,0:T(8,128)(2,1)S(1)}, u32[]{:S(2)}, u32[]{:S(2)}) collective-permute-start(bf16[272,1152]{1,0:T(8,128)(2,1)S(1)} %get-tuple-element.253.p0), channel_id=1, source_target_pairs={{0,2},{2,0},{1,3},{3,1},{4,6},{6,4},{5,7},{7,5},{8,10},{10,8},{9,1... | collective-permute-start | bytes 1880072 | tf_op jit(solution)/shard_map/ppermute | solution.py:617
  16.2 400.2 %copy-start.37 = (f32[272]{0:T(512)}, f32[272]{0:T(512)S(1)}, u32[]{:S(2)}) copy-start(f32[272]{0:T(512)S(1)} %convert_element_type.392) | copy-start | bytes 3268
  29.6 6.3 %collective-permute-start.3 = (bf16[2,272,1152]{2,1,0:T(8,128)(2,1)S(1)}, bf16[2,272,1152]{2,1,0:T(8,128)(2,1)S(1)}, u32[]{:S(2)}, u32[]{:S(2)}) collective-permute-start(bf16[2,272,1152]{2,1,0:T(8,128)(2,1)S(1)} %pad_maximum_fusion.3), channel_id=1, source_target_pairs={{0,1},{1,0},{2,3},{3,2},{4,5},{5,4},{6,7},{7,6},{8,9},{9,8},{10,11... | collective-permute-start | bytes 3760136 | tf_op jit(solution)/shard_map/ppermute | solution.py:621
  32.1 15.1 %collective-permute-start.9 = (bf16[272,1024]{1,0:T(8,128)(2,1)S(1)}, bf16[272,1024]{1,0:T(8,128)(2,1)S(1)}, u32[]{:S(2)}, u32[]{:S(2)}) collective-permute-start(bf16[272,1024]{1,0:T(8,128)(2,1)S(1)} %collective-permute-done.8.p0), channel_id=1, source_target_pairs={{0,2},{2,0},{1,3},{3,1},{4,6},{6,4},{5,7},{7,5},{8,10},{10,8},{9,1... | collective-permute-start | bytes 1671176 | tf_op jit(solution)/shard_map/ppermute | solution.py:617
  40.6 23.2 %copy-start.32 = (bf16[80,1088]{1,0:T(8,128)(2,1)S(1)}, bf16[80,1088]{1,0:T(8,128)(2,1)}, u32[]{:S(2)}) copy-start(bf16[80,1088]{1,0:T(8,128)(2,1)} %constant_dynamic-slice_fusion.7) | copy-start | bytes 522244
  47.2 9.6 %collective-permute-start.5 = (bf16[128,816]{1,0:T(8,128)(2,1)S(1)}, bf16[128,816]{1,0:T(8,128)(2,1)S(1)}, u32[]{:S(2)}, u32[]{:S(2)}) collective-permute-start(bf16[128,816]{1,0:T(8,128)(2,1)S(1)} %slice.404), channel_id=1, source_target_pairs={{0,12},{4,0},{8,4},{12,8},{1,13},{5,1},{9,5},{13,9},{2,14},{6,2},{... | collective-permute-start | bytes 626696 | tf_op jit(solution)/shard_map/ppermute | solution.py:630
  50.7 11.0 %collective-permute-start.4 = (bf16[144,816]{1,0:T(8,128)(2,1)S(1)}, bf16[144,816]{1,0:T(8,128)(2,1)S(1)}, u32[]{:S(2)}, u32[]{:S(2)}) collective-permute-start(bf16[144,816]{1,0:T(8,128)(2,1)S(1)} %slice.401), channel_id=1, source_target_pairs={{0,4},{4,8},{8,12},{12,0},{1,5},{5,9},{9,13},{13,1},{2,6},{6,10},{... | collective-permute-start | bytes 705032 | tf_op jit(solution)/shard_map/ppermute | solution.py:630
  50.8 61.1 %collective-permute-start.10 = (bf16[2,272,1024]{2,1,0:T(8,128)(2,1)S(1)}, bf16[2,272,1024]{2,1,0:T(8,128)(2,1)S(1)}, u32[]{:S(2)}, u32[]{:S(2)}) collective-permute-start(bf16[2,272,1024]{2,1,0:T(8,128)(2,1)S(1)} %pad_maximum_fusion.4), channel_id=1, source_target_pairs={{0,1},{1,0},{2,3},{3,2},{4,5},{5,4},{6,7},{7,6},{8,9},{9,8},{10,11... | collective-permute-start | bytes 3342344 | tf_op jit(solution)/shard_map/ppermute | solution.py:621
  50.9 365.5 %copy-start.35 = (f32[1,1024]{1,0:T(1,128)}, f32[1,1024]{1,0:T(1,128)S(1)}, u32[]{:S(2)}) copy-start(f32[1,1024]{1,0:T(1,128)S(1)} %get-tuple-element.278) | copy-start | bytes 12292
  61.7 50.1 %collective-permute-start.21 = (bf16[288,1088]{1,0:T(8,128)(2,1)S(1)}, bf16[288,1088]{1,0:T(8,128)(2,1)S(1)}, u32[]{:S(2)}, u32[]{:S(2)}) collective-permute-start(bf16[288,1088]{1,0:T(8,128)(2,1)S(1)} %pad_maximum_fusion.8), channel_id=1, source_target_pairs={{0,12},{4,0},{8,4},{12,8},{1,13},{5,1},{9,5},{13,9},{2,14},{6,2},{... | collective-permute-start | bytes 1880072 | tf_op jit(solution)/shard_map/ppermute | solution.py:630
  63.5 48.4 %collective-permute-start.20 = (bf16[288,1088]{1,0:T(8,128)(2,1)S(1)}, bf16[288,1088]{1,0:T(8,128)(2,1)S(1)}, u32[]{:S(2)}, u32[]{:S(2)}) collective-permute-start(bf16[288,1088]{1,0:T(8,128)(2,1)S(1)} %pad_maximum_fusion.8), channel_id=1, source_target_pairs={{0,4},{4,8},{8,12},{12,0},{1,5},{5,9},{9,13},{13,1},{2,6},{6,10},{... | collective-permute-start | bytes 1880072 | tf_op jit(solution)/shard_map/ppermute | solution.py:630
  63.7 33.3 %collective-permute-start.15 = (bf16[80,1088]{1,0:T(8,128)(2,1)S(1)}, bf16[80,1088]{1,0:T(8,128)(2,1)S(1)}, u32[]{:S(2)}, u32[]{:S(2)}) collective-permute-start(bf16[80,1088]{1,0:T(8,128)(2,1)S(1)} %copy-done.32), channel_id=1, source_target_pairs={{0,12},{4,0},{8,4},{12,8},{1,13},{5,1},{9,5},{13,9},{2,14},{6,2},{... | collective-permute-start | bytes 522248 | tf_op jit(solution)/shard_map/ppermute | solution.py:630
  67.4 41.3 %collective-permute-start.14 = (bf16[80,1088]{1,0:T(8,128)(2,1)S(1)}, bf16[80,1088]{1,0:T(8,128)(2,1)S(1)}, u32[]{:S(2)}, u32[]{:S(2)}) collective-permute-start(bf16[80,1088]{1,0:T(8,128)(2,1)S(1)} %copy-done.32), channel_id=1, source_target_pairs={{0,8},{4,12},{8,0},{12,4},{1,9},{5,13},{9,1},{13,5},{2,10},{6,14},... | collective-permute-start | bytes 522248 | tf_op jit(solution)/shard_map/ppermute | solution.py:630
  97.1 13.2 %collective-permute-start.13 = (bf16[80,1088]{1,0:T(8,128)(2,1)S(1)}, bf16[80,1088]{1,0:T(8,128)(2,1)S(1)}, u32[]{:S(2)}, u32[]{:S(2)}) collective-permute-start(bf16[80,1088]{1,0:T(8,128)(2,1)S(1)} %copy-done.32), channel_id=1, source_target_pairs={{0,4},{4,8},{8,12},{12,0},{1,5},{5,9},{9,13},{13,1},{2,6},{6,10},{... | collective-permute-start | bytes 522248 | tf_op jit(solution)/shard_map/ppermute | solution.py:630
  108.6 8.0 %collective-permute-start.6 = (bf16[816,144]{1,0:T(8,128)(2,1)S(1)}, bf16[816,144]{1,0:T(8,128)(2,1)S(1)}, u32[]{:S(2)}, u32[]{:S(2)}) collective-permute-start(bf16[816,144]{1,0:T(8,128)(2,1)S(1)} %maximum_maximum_fusion), channel_id=1, source_target_pairs={{1,0},{2,1},{3,2},{5,4},{6,5},{7,6},{9,8},{10,9},{11,10},{13,12},{... | collective-permute-start | bytes 705032 | tf_op jit(solution)/shard_map/ppermute | solution.py:810
  110.3 6.3 %collective-permute-start.7 = (bf16[272,144]{1,0:T(8,128)(2,1)S(1)}, bf16[272,144]{1,0:T(8,128)(2,1)S(1)}, u32[]{:S(2)}, u32[]{:S(2)}) collective-permute-start(bf16[272,144]{1,0:T(8,128)(2,1)S(1)} %maximum_maximum_fusion.1), channel_id=1, source_target_pairs={{1,0},{2,1},{3,2},{5,4},{6,5},{7,6},{9,8},{10,9},{11,10},{13,12},{... | collective-permute-start | bytes 235016 | tf_op jit(solution)/shard_map/ppermute | solution.py:816
  134.2 17.7 %copy-start.8 = (bf16[320,1024]{1,0:T(8,128)(2,1)}, bf16[320,1024]{1,0:T(8,128)(2,1)S(1)}, u32[]{:S(2)}) copy-start(bf16[320,1024]{1,0:T(8,128)(2,1)S(1)} %get-tuple-element.120.q_ref.refs_0_) | copy-start | bytes 1966084
  142.6 61.2 %collective-permute-start.22 = (bf16[576,1088]{1,0:T(8,128)(2,1)S(1)}, bf16[576,1088]{1,0:T(8,128)(2,1)S(1)}, u32[]{:S(2)}, u32[]{:S(2)}) collective-permute-start(bf16[576,1088]{1,0:T(8,128)(2,1)S(1)} %pad_maximum_fusion.2.refs_1_), channel_id=1, source_target_pairs={{0,16},{16,0},{1,17},{17,1},{2,18},{18,2},{3,19},{19,3},{4,20},{20... | collective-permute-start | bytes 3760136 | tf_op jit(solution)/shard_map/ppermute | solution.py:625
  144.7 16.7 %collective-permute-start.11 = (bf16[320,512]{1,0:T(8,128)(2,1)S(1)}, bf16[320,512]{1,0:T(8,128)(2,1)S(1)}, u32[]{:S(2)}, u32[]{:S(2)}) collective-permute-start(bf16[320,512]{1,0:T(8,128)(2,1)S(1)} %get-tuple-element.88.p0), channel_id=1, source_target_pairs={{0,2},{2,0},{1,3},{3,1},{4,6},{6,4},{5,7},{7,5},{8,10},{10,8},{9,1... | collective-permute-start | bytes 983048 | tf_op jit(solution)/shard_map/ppermute | solution.py:617
  147.7 20.0 %collective-permute-start.16 = (bf16[240,1088]{1,0:T(8,128)(2,1)S(1)}, bf16[240,1088]{1,0:T(8,128)(2,1)S(1)}, u32[]{:S(2)}, u32[]{:S(2)}) collective-permute-start(bf16[240,1088]{1,0:T(8,128)(2,1)S(1)} %pad_maximum_fusion.14.refs_1_), channel_id=1, source_target_pairs={{0,2},{2,0},{1,3},{3,1},{4,6},{6,4},{5,7},{7,5},{8,10},{10,8},{9,1... | collective-permute-start | bytes 1566728 | tf_op jit(solution)/shard_map/ppermute | solution.py:617
  147.8 15.7 %collective-permute-start.23 = (bf16[144,1088]{1,0:T(8,128)(2,1)S(1)}, bf16[144,1088]{1,0:T(8,128)(2,1)S(1)}, u32[]{:S(2)}, u32[]{:S(2)}) collective-permute-start(bf16[144,1088]{1,0:T(8,128)(2,1)S(1)} %get-tuple-element.232), channel_id=1, source_target_pairs={{0,4},{4,8},{8,12},{12,0},{1,5},{5,9},{9,13},{13,1},{2,6},{6,10},{... | collective-permute-start | bytes 940040 | tf_op jit(solution)/shard_map/ppermute | solution.py:630
  149.3 26.4 %collective-permute-start.24 = (bf16[144,1088]{1,0:T(8,128)(2,1)S(1)}, bf16[144,1088]{1,0:T(8,128)(2,1)S(1)}, u32[]{:S(2)}, u32[]{:S(2)}) collective-permute-start(bf16[144,1088]{1,0:T(8,128)(2,1)S(1)} %get-tuple-element.233), channel_id=1, source_target_pairs={{0,12},{4,0},{8,4},{12,8},{1,13},{5,1},{9,5},{13,9},{2,14},{6,2},{... | collective-permute-start | bytes 940040 | tf_op jit(solution)/shard_map/ppermute | solution.py:630
  161.4 13.4 %collective-permute-start.18 = (bf16[320,512]{1,0:T(8,128)(2,1)S(1)}, bf16[320,512]{1,0:T(8,128)(2,1)S(1)}, u32[]{:S(2)}, u32[]{:S(2)}) collective-permute-start(bf16[320,512]{1,0:T(8,128)(2,1)S(1)} %get-tuple-element.95.p0), channel_id=1, source_target_pairs={{0,2},{2,0},{1,3},{3,1},{4,6},{6,4},{5,7},{7,5},{8,10},{10,8},{9,1... | collective-permute-start | bytes 983048 | tf_op jit(solution)/shard_map/ppermute | solution.py:617
  163.4 26.6 %collective-permute-start.12 = (bf16[2,320,512]{2,1,0:T(8,128)(2,1)S(1)}, bf16[2,320,512]{2,1,0:T(8,128)(2,1)S(1)}, u32[]{:S(2)}, u32[]{:S(2)}) collective-permute-start(bf16[2,320,512]{2,1,0:T(8,128)(2,1)S(1)} %pad_maximum_fusion.10), channel_id=1, source_target_pairs={{0,1},{1,0},{2,3},{3,2},{4,5},{5,4},{6,7},{7,6},{8,9},{9,8},{10,11... | collective-permute-start | bytes 1966088 | tf_op jit(solution)/shard_map/ppermute | solution.py:621
  167.8 19.0 %collective-permute-start.26 = (bf16[272,1024]{1,0:T(8,128)(2,1)S(1)}, bf16[272,1024]{1,0:T(8,128)(2,1)S(1)}, u32[]{:S(2)}, u32[]{:S(2)}) collective-permute-start(bf16[272,1024]{1,0:T(8,128)(2,1)S(1)} %bitcast.283), channel_id=1, source_target_pairs={{0,2},{2,0},{1,3},{3,1},{4,6},{6,4},{5,7},{7,5},{8,10},{10,8},{9,1... | collective-permute-start | bytes 1671176 | tf_op jit(solution)/shard_map/ppermute | solution.py:617
  174.8 37.2 %collective-permute-start.17 = (bf16[480,1088]{1,0:T(8,128)(2,1)}, bf16[480,1088]{1,0:T(8,128)(2,1)S(1)}, u32[]{:S(2)}, u32[]{:S(2)}) collective-permute-start(bf16[480,1088]{1,0:T(8,128)(2,1)} %pad_maximum_fusion.7), channel_id=1, source_target_pairs={{0,1},{1,0},{2,3},{3,2},{4,5},{5,4},{6,7},{7,6},{8,9},{9,8},{10,11... | collective-permute-start | bytes 3133448 | tf_op jit(solution)/shard_map/ppermute | solution.py:621
  175.8 14.4 %collective-permute-start.19 = (bf16[2,320,512]{2,1,0:T(8,128)(2,1)S(1)}, bf16[2,320,512]{2,1,0:T(8,128)(2,1)S(1)}, u32[]{:S(2)}, u32[]{:S(2)}) collective-permute-start(bf16[2,320,512]{2,1,0:T(8,128)(2,1)S(1)} %pad_maximum_fusion.11), channel_id=1, source_target_pairs={{0,1},{1,0},{2,3},{3,2},{4,5},{5,4},{6,7},{7,6},{8,9},{9,8},{10,11... | collective-permute-start | bytes 1966088 | tf_op jit(solution)/shard_map/ppermute | solution.py:621
  186.7 17.1 %collective-permute-start.25 = (bf16[288,1088]{1,0:T(8,128)(2,1)S(1)}, bf16[288,1088]{1,0:T(8,128)(2,1)S(1)}, u32[]{:S(2)}, u32[]{:S(2)}) collective-permute-start(bf16[288,1088]{1,0:T(8,128)(2,1)S(1)} %pad_maximum_fusion.9.refs_3_), channel_id=1, source_target_pairs={{0,16},{16,0},{1,17},{17,1},{2,18},{18,2},{3,19},{19,3},{4,20},{20... | collective-permute-start | bytes 1880072 | tf_op jit(solution)/shard_map/ppermute | solution.py:625
  190.1 37.9 %collective-permute-start.27 = (bf16[2,272,1024]{2,1,0:T(8,128)(2,1)}, bf16[2,272,1024]{2,1,0:T(8,128)(2,1)}, u32[]{:S(2)}, u32[]{:S(2)}) collective-permute-start(bf16[2,272,1024]{2,1,0:T(8,128)(2,1)} %pad_maximum_fusion.5), channel_id=1, source_target_pairs={{0,1},{1,0},{2,3},{3,2},{4,5},{5,4},{6,7},{7,6},{8,9},{9,8},{10,11... | collective-permute-start | bytes 3342344 | tf_op jit(solution)/shard_map/ppermute | solution.py:621
  190.2 18.3 %copy-start.2 = (bf16[1088,272]{0,1:T(8,128)(2,1)S(1)}, bf16[1088,272]{0,1:T(8,128)(2,1)}, u32[]{:S(2)}) copy-start(bf16[1088,272]{0,1:T(8,128)(2,1)} %param.27) | copy-start | bytes 1775620
  253.4 4.0 collective-permute-start.28
  263.8 15.0 %collective-permute-start.29 = (bf16[1088,256]{1,0:T(8,128)(2,1)S(1)}, bf16[1088,256]{1,0:T(8,128)(2,1)S(1)}, u32[]{:S(2)}, u32[]{:S(2)}) collective-permute-start(bf16[1088,256]{1,0:T(8,128)(2,1)S(1)} %get-tuple-element.221), channel_id=1, source_target_pairs={{0,2},{2,0},{1,3},{3,1},{4,6},{6,4},{5,7},{7,5},{8,10},{10,8},{9,1... | collective-permute-start | bytes 1671176 | tf_op jit(solution)/shard_map/ppermute | solution.py:617
  281.4 14.2 %collective-permute-start.30 = (bf16[1088,256]{1,0:T(8,128)(2,1)S(1)}, bf16[1088,256]{1,0:T(8,128)(2,1)S(1)}, u32[]{:S(2)}, u32[]{:S(2)}) collective-permute-start(bf16[1088,256]{1,0:T(8,128)(2,1)S(1)} %get-tuple-element.108.p0), channel_id=1, source_target_pairs={{0,2},{2,0},{1,3},{3,1},{4,6},{6,4},{5,7},{7,5},{8,10},{10,8},{9,1... | collective-permute-start | bytes 1671176 | tf_op jit(solution)/shard_map/ppermute | solution.py:617
  284.8 57.6 %collective-permute-start.54 = (bf16[2,4,136,1088]{3,2,0,1:T(8,128)(2,1)}, bf16[2,4,136,1088]{3,2,0,1:T(8,128)(2,1)}, u32[]{:S(2)}, u32[]{:S(2)}) collective-permute-start(bf16[2,4,136,1088]{3,2,0,1:T(8,128)(2,1)} %pad_maximum_fusion), channel_id=1, source_target_pairs={{0,16},{16,0},{1,17},{17,1},{2,18},{18,2},{3,19},{19,3},{4,20},{20... | collective-permute-start | bytes 7102472 | tf_op jit(solution)/shard_map/ppermute | solution.py:625
  296.7 8.4 %collective-permute-start.31 = (bf16[2,1088,256]{2,1,0:T(8,128)(2,1)}, bf16[2,1088,256]{2,1,0:T(8,128)(2,1)}, u32[]{:S(2)}, u32[]{:S(2)}) collective-permute-start(bf16[2,1088,256]{2,1,0:T(8,128)(2,1)} %pad_maximum_fusion.6), channel_id=1, source_target_pairs={{0,1},{1,0},{2,3},{3,2},{4,5},{5,4},{6,7},{7,6},{8,9},{9,8},{10,11... | collective-permute-start | bytes 3342344 | tf_op jit(solution)/shard_map/ppermute | solution.py:621
  313.9 21.1 %collective-permute-start.39 = (f32[4,1088]{1,0:T(4,128)S(1)}, f32[4,1088]{1,0:T(4,128)S(1)}, u32[]{:S(2)}, u32[]{:S(2)}) collective-permute-start(f32[4,1088]{1,0:T(4,128)S(1)} %pad_maximum_fusion.21), channel_id=1, source_target_pairs={{0,2},{2,0},{1,3},{3,1},{4,6},{6,4},{5,7},{7,5},{8,10},{10,8},{9,1... | collective-permute-start | bytes 52232 | tf_op jit(solution)/shard_map/ppermute | solution.py:617
  315.4 89.8 %collective-permute-start.46 = (bf16[1,4,136,272]{3,2,1,0:T(8,128)(2,1)}, bf16[1,4,136,272]{3,2,1,0:T(8,128)(2,1)}, u32[]{:S(2)}, u32[]{:S(2)}) collective-permute-start(bf16[1,4,136,272]{3,2,1,0:T(8,128)(2,1)} %get-tuple-element.245), channel_id=1, source_target_pairs={{0,16},{16,0},{1,17},{17,1},{2,18},{18,2},{3,19},{19,3},{4,20},{20... | collective-permute-start | bytes 887816 | tf_op jit(solution)/shard_map/ppermute | solution.py:625
  335.1 5.6 %collective-permute-start.40 = (f32[4,1088]{1,0:T(4,128)S(1)}, f32[4,1088]{1,0:T(4,128)S(1)}, u32[]{:S(2)}, u32[]{:S(2)}) collective-permute-start(f32[4,1088]{1,0:T(4,128)S(1)} %pad_maximum_fusion.22), channel_id=1, source_target_pairs={{0,1},{1,0},{2,3},{3,2},{4,5},{5,4},{6,7},{7,6},{8,9},{9,8},{10,11... | collective-permute-start | bytes 52232 | tf_op jit(solution)/shard_map/ppermute | solution.py:621
  339.4 41.6 %collective-permute-start.32 = (bf16[640,1024]{1,0:T(8,128)(2,1)S(1)}, bf16[640,1024]{1,0:T(8,128)(2,1)S(1)}, u32[]{:S(2)}, u32[]{:S(2)}) collective-permute-start(bf16[640,1024]{1,0:T(8,128)(2,1)S(1)} %get-tuple-element.122), channel_id=1, source_target_pairs={{16,0},{17,1},{18,2},{19,3},{20,4},{21,5},{22,6},{23,7},{24,8},{25... | collective-permute-start | bytes 3932168 | tf_op jit(solution)/shard_map/ppermute | solution.py:982
  344.4 12.1 %collective-permute-start.55 = (bf16[136,1088]{1,0:T(8,128)(2,1)S(1)}, bf16[136,1088]{1,0:T(8,128)(2,1)S(1)}, u32[]{:S(2)}, u32[]{:S(2)}) collective-permute-start(bf16[136,1088]{1,0:T(8,128)(2,1)S(1)} %get-tuple-element.250), channel_id=1, source_target_pairs={{0,4},{4,8},{8,12},{12,0},{1,5},{5,9},{9,13},{13,1},{2,6},{6,10},{... | collective-permute-start | bytes 887816 | tf_op jit(solution)/shard_map/ppermute | solution.py:630
  346.6 14.0 %collective-permute-start.57 = (bf16[136,1088]{1,0:T(8,128)(2,1)S(1)}, bf16[136,1088]{1,0:T(8,128)(2,1)S(1)}, u32[]{:S(2)}, u32[]{:S(2)}) collective-permute-start(bf16[136,1088]{1,0:T(8,128)(2,1)S(1)} %get-tuple-element.251), channel_id=1, source_target_pairs={{0,12},{4,0},{8,4},{12,8},{1,13},{5,1},{9,5},{13,9},{2,14},{6,2},{... | collective-permute-start | bytes 887816 | tf_op jit(solution)/shard_map/ppermute | solution.py:630
  361.5 41.9 %collective-permute-start.58 = (bf16[2,136,1088]{2,1,0:T(8,128)(2,1)}, bf16[2,136,1088]{2,1,0:T(8,128)(2,1)}, u32[]{:S(2)}, u32[]{:S(2)}) collective-permute-start(bf16[2,136,1088]{2,1,0:T(8,128)(2,1)} %pad_maximum_fusion.13), channel_id=1, source_target_pairs={{0,12},{4,0},{8,4},{12,8},{1,13},{5,1},{9,5},{13,9},{2,14},{6,2},{... | collective-permute-start | bytes 1775624 | tf_op jit(solution)/shard_map/ppermute | solution.py:630
  364.5 38.9 %collective-permute-start.56 = (bf16[2,136,1088]{2,1,0:T(8,128)(2,1)}, bf16[2,136,1088]{2,1,0:T(8,128)(2,1)}, u32[]{:S(2)}, u32[]{:S(2)}) collective-permute-start(bf16[2,136,1088]{2,1,0:T(8,128)(2,1)} %pad_maximum_fusion.12), channel_id=1, source_target_pairs={{0,4},{4,8},{8,12},{12,0},{1,5},{5,9},{9,13},{13,1},{2,6},{6,10},{... | collective-permute-start | bytes 1775624 | tf_op jit(solution)/shard_map/ppermute | solution.py:630
  387.5 12.7 %collective-permute-start.33 = (bf16[2,272,1024]{2,1,0:T(8,128)(2,1)}, bf16[2,272,1024]{2,1,0:T(8,128)(2,1)}, u32[]{:S(2)}, u32[]{:S(2)}) collective-permute-start(bf16[2,272,1024]{2,1,0:T(8,128)(2,1)} %dynamic-slice_bitcast_fusion.5), channel_id=1, source_target_pairs={{0,1},{1,0},{2,3},{3,2},{4,5},{5,4},{6,7},{7,6},{8,9},{9,8},{10,11... | collective-permute-start | bytes 3342344 | tf_op jit(solution)/shard_map/ppermute | solution.py:621
  400.0 26.8 %collective-permute-start.45 = (bf16[1,4,136,960]{3,2,1,0:T(8,128)(2,1)}, bf16[1,4,136,960]{3,2,1,0:T(8,128)(2,1)}, u32[]{:S(2)}, u32[]{:S(2)}) collective-permute-start(bf16[1,4,136,960]{3,2,1,0:T(8,128)(2,1)} %get-tuple-element.231), channel_id=1, source_target_pairs={{0,16},{16,0},{1,17},{17,1},{2,18},{18,2},{3,19},{19,3},{4,20},{20... | collective-permute-start | bytes 3133448 | tf_op jit(solution)/shard_map/ppermute | solution.py:625
  401.8 14.7 %collective-permute-start.36 = (bf16[272,1024]{1,0:T(8,128)(2,1)S(1)}, bf16[272,1024]{1,0:T(8,128)(2,1)S(1)}, u32[]{:S(2)}, u32[]{:S(2)}) collective-permute-start(bf16[272,1024]{1,0:T(8,128)(2,1)S(1)} %fusion.6), channel_id=1, source_target_pairs={{0,2},{2,0},{1,3},{3,1},{4,6},{6,4},{5,7},{7,5},{8,10},{10,8},{9,1... | collective-permute-start | bytes 1671176 | tf_op jit(solution)/shard_map/ppermute | solution.py:617
  418.8 12.1 %collective-permute-start.37 = (f32[4,1088]{1,0:T(4,128)S(1)}, f32[4,1088]{1,0:T(4,128)S(1)}, u32[]{:S(2)}, u32[]{:S(2)}) collective-permute-start(f32[4,1088]{1,0:T(4,128)S(1)} %pad_maximum_fusion.20), channel_id=1, source_target_pairs={{0,2},{2,0},{1,3},{3,1},{4,6},{6,4},{5,7},{7,5},{8,10},{10,8},{9,1... | collective-permute-start | bytes 52232 | tf_op jit(solution)/shard_map/ppermute | solution.py:617
  431.5 5.9 %collective-permute-start.38 = (f32[4,1088]{1,0:T(4,128)}, f32[4,1088]{1,0:T(4,128)}, u32[]{:S(2)}, u32[]{:S(2)}) collective-permute-start(f32[4,1088]{1,0:T(4,128)} %fusion.73), channel_id=1, source_target_pairs={{0,1},{1,0},{2,3},{3,2},{4,5},{5,4},{6,7},{7,6},{8,9},{9,8},{10,11... | collective-permute-start | bytes 52232 | tf_op jit(solution)/shard_map/ppermute | solution.py:621
  433.3 53.2 %collective-permute-start.34 = (bf16[2,272,1024]{2,1,0:T(8,128)(2,1)}, bf16[2,272,1024]{2,1,0:T(8,128)(2,1)}, u32[]{:S(2)}, u32[]{:S(2)}) collective-permute-start(bf16[2,272,1024]{2,1,0:T(8,128)(2,1)} %dynamic-slice_bitcast_fusion.4), channel_id=1, source_target_pairs={{0,1},{1,0},{2,3},{3,2},{4,5},{5,4},{6,7},{7,6},{8,9},{9,8},{10,11... | collective-permute-start | bytes 3342344 | tf_op jit(solution)/shard_map/ppermute | solution.py:621
  434.4 27.4 %collective-permute-start.47 = (bf16[136,512]{1,0:T(8,128)(2,1)}, bf16[136,512]{1,0:T(8,128)(2,1)}, u32[]{:S(2)}, u32[]{:S(2)}) collective-permute-start(bf16[136,512]{1,0:T(8,128)(2,1)} %slice_bitcast_fusion.22), channel_id=1, source_target_pairs={{0,4},{4,8},{8,12},{12,0},{1,5},{5,9},{9,13},{13,1},{2,6},{6,10},{... | collective-permute-start | bytes 417800 | tf_op jit(solution)/shard_map/ppermute | solution.py:630
  443.4 4.2 collective-permute-start.41
  449.1 5.5 %collective-permute-start.44 = (f32[7,1088]{1,0:T(8,128)S(1)}, f32[7,1088]{1,0:T(8,128)S(1)}, u32[]{:S(2)}, u32[]{:S(2)}) collective-permute-start(f32[7,1088]{1,0:T(8,128)S(1)} %pad_maximum_fusion.18), channel_id=1, source_target_pairs={{0,12},{4,0},{8,4},{12,8},{1,13},{5,1},{9,5},{13,9},{2,14},{6,2},{... | collective-permute-start | bytes 91400 | tf_op jit(solution)/shard_map/ppermute | solution.py:630
  451.1 6.8 %collective-permute-start.43 = (f32[7,1088]{1,0:T(8,128)S(1)}, f32[7,1088]{1,0:T(8,128)S(1)}, u32[]{:S(2)}, u32[]{:S(2)}) collective-permute-start(f32[7,1088]{1,0:T(8,128)S(1)} %pad_maximum_fusion.18), channel_id=1, source_target_pairs={{0,8},{4,12},{8,0},{12,4},{1,9},{5,13},{9,1},{13,5},{2,10},{6,14},... | collective-permute-start | bytes 91400 | tf_op jit(solution)/shard_map/ppermute | solution.py:630
  451.1 6.8 %collective-permute-start.42 = (f32[7,1088]{1,0:T(8,128)S(1)}, f32[7,1088]{1,0:T(8,128)S(1)}, u32[]{:S(2)}, u32[]{:S(2)}) collective-permute-start(f32[7,1088]{1,0:T(8,128)S(1)} %pad_maximum_fusion.18), channel_id=1, source_target_pairs={{0,4},{4,8},{8,12},{12,0},{1,5},{5,9},{9,13},{13,1},{2,6},{6,10},{... | collective-permute-start | bytes 91400 | tf_op jit(solution)/shard_map/ppermute | solution.py:630
  454.6 8.4 %collective-permute-start.49 = (bf16[136,720]{1,0:T(8,128)(2,1)}, bf16[136,720]{1,0:T(8,128)(2,1)}, u32[]{:S(2)}, u32[]{:S(2)}) collective-permute-start(bf16[136,720]{1,0:T(8,128)(2,1)} %slice_bitcast_fusion.21), channel_id=1, source_target_pairs={{0,12},{4,0},{8,4},{12,8},{1,13},{5,1},{9,5},{13,9},{2,14},{6,2},{... | collective-permute-start | bytes 587528 | tf_op jit(solution)/shard_map/ppermute | solution.py:630
  463.0 12.9 %collective-permute-start.48 = (bf16[1,136,1232]{2,1,0:T(8,128)(2,1)S(1)}, bf16[1,136,1232]{2,1,0:T(8,128)(2,1)S(1)}, u32[]{:S(2)}, u32[]{:S(2)}) collective-permute-start(bf16[1,136,1232]{2,1,0:T(8,128)(2,1)S(1)} %pad_maximum_fusion.15), channel_id=1, source_target_pairs={{0,4},{4,8},{8,12},{12,0},{1,5},{5,9},{9,13},{13,1},{2,6},{6,10},{... | collective-permute-start | bytes 1005320 | tf_op jit(solution)/shard_map/ppermute | solution.py:630
  464.1 15.3 %collective-permute-start.50 = (bf16[1,136,1232]{2,1,0:T(8,128)(2,1)S(1)}, bf16[1,136,1232]{2,1,0:T(8,128)(2,1)S(1)}, u32[]{:S(2)}, u32[]{:S(2)}) collective-permute-start(bf16[1,136,1232]{2,1,0:T(8,128)(2,1)S(1)} %pad_maximum_fusion.16), channel_id=1, source_target_pairs={{0,12},{4,0},{8,4},{12,8},{1,13},{5,1},{9,5},{13,9},{2,14},{6,2},{... | collective-permute-start | bytes 1005320 | tf_op jit(solution)/shard_map/ppermute | solution.py:630
  480.8 8.3 %collective-permute-start.52 = (bf16[136,272]{1,0:T(8,128)(2,1)S(1)}, bf16[136,272]{1,0:T(8,128)(2,1)S(1)}, u32[]{:S(2)}, u32[]{:S(2)}) collective-permute-start(bf16[136,272]{1,0:T(8,128)(2,1)S(1)} %slice.613), channel_id=1, source_target_pairs={{0,2},{2,0},{1,3},{3,1},{4,6},{6,4},{5,7},{7,5},{8,10},{10,8},{9,1... | collective-permute-start | bytes 221960 | tf_op jit(solution)/shard_map/ppermute | solution.py:617
  485.1 4.3 collective-permute-start.51
  487.9 15.3 %collective-permute-start.35 = (bf16[272,1024]{1,0:T(8,128)(2,1)S(1)}, bf16[272,1024]{1,0:T(8,128)(2,1)S(1)}, u32[]{:S(2)}, u32[]{:S(2)}) collective-permute-start(bf16[272,1024]{1,0:T(8,128)(2,1)S(1)} %fusion.7), channel_id=1, source_target_pairs={{0,2},{2,0},{1,3},{3,1},{4,6},{6,4},{5,7},{7,5},{8,10},{10,8},{9,1... | collective-permute-start | bytes 1671176 | tf_op jit(solution)/shard_map/ppermute | solution.py:617
  489.1 3.0 collective-permute-start.53
  (47 other events, 259.4 us)

commit v3 on v2

--- a/solution.py
+++ b/solution.py
@@ -15,6 +15,8 @@
 neg_fill = -1e30
 clip_limit = 8.0
 
+SCALE = 0.02
+
 f32 = jnp.float32
 bf16 = jnp.bfloat16
 
@@ -35,12 +37,21 @@
     return lax.dot_general(left, right, (((0,), (0,)), ((), ())), preferred_element_type=f32)
 
 
-def params():
-    return pltpu.CompilerParams(vmem_limit_bytes=50 * 2**20)
+def params(mib=16):
+    return pltpu.CompilerParams(vmem_limit_bytes=mib * 2**20)
 
 
 def cost(flops, moved, exps=0):
-    return pl.CostEstimate(flops=int(flops), bytes_accessed=int(moved), transcendentals=int(exps))
+    return pl.CostEstimate(
+        flops=int(flops * SCALE), bytes_accessed=int(moved * SCALE), transcendentals=int(exps * SCALE)
+    )
+
+
+def waiting(body, inputs, count):
+    def wrapped(*refs):
+        return body(*refs[:inputs], *refs[inputs + count :])
+
+    return wrapped
 
 
 def shape(dims, kind):
@@ -51,29 +62,32 @@
     return pl.ds(pl.multiple_of(start, 16), length)
 
 
-def assemble_body(plan, fill, starts, *refs):
-    pieces, out_ref = refs[:-1], refs[-1]
+def assemble_body(plan, fill, turned, starts, *refs):
+    pieces, out_ref = (refs[:-2], refs[-2]) if turned else (refs[:-1], refs[-1])
     for piece, source, length, where in plan:
         out_ref[rows_at(starts[where], length), :] = pieces[piece][source : source + length, :]
-    if fill:
-        out_ref[out_ref.shape[0] - fill :, :] = jnp.zeros((fill, out_ref.shape[1]), bf16)
+    if turned:
+        rows = out_ref.shape[0]
+        refs[-1][:rows, :] = out_ref[...].T
+        refs[-1][rows:, :] = jnp.zeros((fill, rows), bf16)
 
 
 def whole(array):
-    return pl.BlockSpec(array.shape, lambda *_: (0,) * array.ndim)
-
-
-def assemble(starts, pieces, plan, rows, fill=0):
-    result = shape((rows + fill, pieces[0].shape[1]), bf16)
+    return VMEM
+
+
+def assemble(starts, pieces, plan, rows, fill=0, turned=False):
+    result = shape((rows, pieces[0].shape[1]), bf16)
+    results = [result, shape((rows + fill, rows), bf16)] if turned else result
     return pl.pallas_call(
-        functools.partial(assemble_body, tuple(plan), fill),
+        functools.partial(assemble_body, tuple(plan), fill, turned),
         grid_spec=pltpu.PrefetchScalarGridSpec(
             num_scalar_prefetch=1,
             grid=(1,),
             in_specs=[whole(piece) for piece in pieces],
-            out_specs=whole(result),
+            out_specs=[whole(each) for each in results] if turned else whole(result),
         ),
-        out_shape=result,
+        out_shape=results,
         compiler_params=params(),
         cost_estimate=cost(0, rows * result.shape[1] * 4),
         name="assemble",
@@ -81,7 +95,10 @@
 
 
 def first_norm_body(own, order, p0, p1, p2, p3, *refs):
-    vec_ref, x_ref, n_ref, stat_ref = (refs[3], *refs[:3]) if own else refs
+    if own:
+        x_ref, n_ref, stat_ref, vec_ref, dy_ref = refs
+    else:
+        vec_ref, x_ref, n_ref, stat_ref = refs
     part = p0.shape[0]
     full, count = x_ref.shape
     if own:
@@ -91,6 +108,7 @@
         x_ref[where, :] = piece[:, :count]
         if own:
             vec_ref[where, :] = piece[:, count : count + 128].astype(f32)
+            dy_ref[where, :] = piece[:, count + 128 :]
     for start in range(0, count, 256):
         cols = slice(start, start + 256)
         x = x_ref[:, cols].astype(f32)
@@ -108,7 +126,7 @@
     results = [shape((full, count), bf16), shape((full, count), bf16), shape((8, count), f32)]
     operands = list(pieces)
     if own:
-        results.append(shape((full + E, 128), f32))
+        results += [shape((full + E, 128), f32), shape((full, count), bf16)]
     else:
         operands.append(vectors)
     return pl.pallas_call(
@@ -126,45 +144,88 @@
     )(order, *operands)
 
 
-def head_weights_body(order, own, left, right, far_a, far_b, near, far, pick_own, pick_next, out_ref):
-    size, cut = own.shape[0], far_a.shape[0]
-
-    def put(owner, extra, rows, piece, edge):
-        out_ref[rows_at(owner * size + extra, rows), :] = (
-            dot_nn(piece, pick_own[...]) + dot_nn(edge, pick_next[...])
-        ).astype(bf16)
-
-    put(order[0], 0, size, own[...], near[:size, :])
-    put(order[1], 0, size, left[...], near[size : 2 * size, :])
-    put(order[3], 0, size, right[...], near[2 * size :, :])
-    put(order[2], 0, cut, far_a[...], far[:cut, :])
-    put(order[2], cut, size - cut, far_b[...], far[cut:, :])
-
-
-def head_weights(order, pieces, pick_own, pick_next):
-    result = shape((pieces[0].shape[0] * 4, pick_own.shape[1]), bf16)
+def near_rows_body(order, own, left, right, pick_own, base_ref, edge_ref, out_ref):
+    size = own.shape[0]
+    wide = pick_own.shape[0]
+    spare = edge_ref.shape[1]
+    for n, piece in ((0, own), (1, left), (3, right)):
+        where = rows_at(order[n] * size, size)
+        base_ref[where, :] = dot_nn(piece[:, :wide], pick_own[...]).astype(bf16)
+        out_ref[where, :] = piece[:, wide:]
+        edge_rows(piece, edge_ref, where, wide // 3)
+
+
+def edge_rows(piece, edge_ref, where, part):
+    spare = 5 * E - part
+    for p in range(3):
+        edge_ref[where, p * spare : (p + 1) * spare] = piece[:, p * part : p * part + spare]
+
+
+def far_rows_body(order, base, edge, out, far_a, far_b, pick_own, base_ref, edge_ref, turned_ref, out_s):
+    size, cut = base.shape[0] // 4, far_a.shape[0]
+    wide = pick_own.shape[0]
+    base_ref[...] = base[...]
+    edge_ref[...] = edge[...]
+    out_s[...] = out[...]
+    for piece, extra in ((far_a, 0), (far_b, cut)):
+        where = rows_at(order[2] * size + extra, piece.shape[0])
+        base_ref[where, :] = dot_nn(piece[:, :wide], pick_own[...]).astype(bf16)
+        out_s[where, :] = piece[:, wide:]
+        edge_rows(piece, edge_ref, where, wide // 3)
+    turned_ref[...] = out_s[...].T
+
+
+def near_rows(order, pieces, pick_own):
+    size = pieces[0].shape[0]
+    results = [
+        shape((4 * size, pick_own.shape[1]), bf16),
+        shape((4 * size, 256), bf16),
+        shape((4 * size, size), bf16),
+    ]
     return pl.pallas_call(
-        head_weights_body,
+        near_rows_body,
+        grid_spec=pltpu.PrefetchScalarGridSpec(
+            num_scalar_prefetch=1, grid=(1,), in_specs=[VMEM] * 4, out_specs=[VMEM] * 3
+        ),
+        out_shape=results,
+        compiler_params=params(),
+        cost_estimate=cost(2 * 816 * 816 * 960, 6 * 10**6),
+        name="near_rows",
+    )(order, *pieces, pick_own)
+
+
+def far_rows(order, near, far, pick_own, wait):
+    size = near[0].shape[0] // 4
+    results = [
+        shape(near[0].shape, bf16),
+        shape(near[1].shape, bf16),
+        shape((size, 4 * size), bf16),
+    ]
+    return pl.pallas_call(
+        waiting(far_rows_body, 7, 1),
         grid_spec=pltpu.PrefetchScalarGridSpec(
             num_scalar_prefetch=1,
             grid=(1,),
-            in_specs=[whole(array) for array in (*pieces, pick_own, pick_next)],
-            out_specs=whole(result),
+            in_specs=[VMEM] * 6 + [ANY],
+            out_specs=[VMEM] * 3,
+            scratch_shapes=[pltpu.VMEM((4 * size, size), bf16)],
         ),
-        out_shape=result,
+        out_shape=results,
         compiler_params=params(),
-        cost_estimate=cost(2 * 960 * 960 * 1088, 6 * 10**6),
-        name="head_weights",
-    )(order, *pieces, pick_own, pick_next)
-
-
-def project_body(width, info, w_ref, bias_ref, own_ref, before_ref, q_ref, kv_ref, w_s):
+        cost_estimate=cost(2 * 272 * 816 * 960, 6 * 10**6),
+        name="far_rows",
+    )(order, *near, *far, pick_own, wait)
+
+
+def project_body(width, info, base_ref, edge_ref, pick_ref, bias_ref, own_ref, before_ref, q_ref, kv_ref, w_ref, w_s):
     step = pl.program_id(0)
     half = pl.num_programs(0) // 2
     mine = (step // half) == info[0]
 
     @pl.when(step == 0)
     def _():
+        edges = edge_ref[:, : pick_ref.shape[0]]
+        w_ref[...] = base_ref[...] + dot_nn(edges, pick_ref[...]).astype(bf16)
         w_s[...] = w_ref[...].T
 
     def keyvals(n_ref):
@@ -184,9 +245,9 @@
         keyvals(before_ref)
 
 
-def project(info, w_heads, bias, own, before, block=512):
+def project(info, base, edges, pick_next, bias, own, before, block=512):
     full, count = own.shape
-    wide = w_heads.shape[1]
+    wide = base.shape[1]
     width = wide // 3
     steps = count // block
     return pl.pallas_call(
@@ -195,8 +256,10 @@
             num_scalar_prefetch=1,
             grid=(2 * steps,),
             in_specs=[
-                pl.BlockSpec((full, wide), lambda i, s: (0, 0)),
-                pl.BlockSpec(bias.shape, lambda i, s: (0, 0)),
+                VMEM,
+                VMEM,
+                VMEM,
+                VMEM,
                 pl.BlockSpec((full, block), lambda i, s: (0, jnp.clip(i - s[0] * steps, 0, steps - 1))),
                 pl.BlockSpec(
                     (full, block), lambda i, s: (0, jnp.clip(i - (1 - s[0]) * steps, 0, steps - 1))
@@ -205,14 +268,19 @@
             out_specs=[
                 pl.BlockSpec((width, block), lambda i, s: (0, jnp.clip(i - s[0] * steps, 0, steps - 1))),
                 pl.BlockSpec((2 * width, block), lambda i, s: (0, i)),
+                VMEM,
             ],
             scratch_shapes=[pltpu.VMEM((wide, full), bf16)],
         ),
-        out_shape=[shape((width, count), bf16), shape((2 * width, 2 * count), bf16)],
-        compiler_params=params(),
+        out_shape=[
+            shape((width, count), bf16),
+            shape((2 * width, 2 * count), bf16),
+            shape((full, wide), bf16),
+        ],
+        compiler_params=params(24),
         cost_estimate=cost(2 * full * count * 5 * width, 10 * 10**6),
         name="project",
-    )(info, w_heads, bias, own, before)
+    )(info, base, edges, pick_next, bias, own, before)
 
 
 def block_limits(info, block, rows):
@@ -309,7 +377,7 @@
             shape((8, rows), f32),
             shape((8, 128), f32),
         ],
-        compiler_params=params(),
+        compiler_params=params(40),
         cost_estimate=cost(8 * 10**9, 6 * 10**6, 4 * 10**6),
         name="attn_fwd",
     )(info, queries, kv_all)
@@ -415,15 +483,14 @@
             shape((width, count), bf16 if last else f32),
             shape((2 * width, count), bf16),
         ],
-        compiler_params=params(),
+        compiler_params=params(40),
         cost_estimate=cost(16 * 10**9, 6 * 10**6, 4 * 10**6),
         name="attn_bwd",
     )(info, queries, kv_all, grad_attn, exact, lse, *([dq_in] if more else []))
 
 
-def out_norm_body(starts, p0, p1, p2, p3, w_ref, x_ref, vec_ref, after_ref, n_ref, stat_ref, attn_ref, w_s):
+def out_norm_body(starts, p0, p1, p2, p3, w_ref, x_ref, vec_ref, after_ref, n_ref, stat_ref, attn_ref):
     fewer = (attn_ref.shape[0] // E) // 4 * E
-    w_s[...] = w_ref[: w_s.shape[1], :].T
     for n, piece in enumerate((p0, p1, p2, p3)):
         attn_ref[rows_at(starts[n], fewer), :] = piece[:fewer, :]
 
@@ -435,7 +502,7 @@
     for start in range(0, count, 256):
         cols = slice(start, start + 256)
         after = x_ref[:, cols].astype(f32) + (
-            dot_nn(w_s[...], attn_ref[:, cols]) + vec_ref[:full, 6:7]
+            dot_nn(w_ref[...], attn_ref[:, cols]) + vec_ref[:full, 6:7]
         )
         mean = jnp.sum(after, axis=0, keepdims=True) * (1.0 / full)
         center = after - mean
@@ -446,7 +513,7 @@
         stat_ref[1:2, cols] = inv
 
 
-def out_norm(starts, pieces, w_out, x_full, vectors, first):
+def out_norm(starts, pieces, w_out_t, x_full, vectors, first):
     full = x_full.shape[0]
     rows, count = pieces[0].shape
     grid_spec = pltpu.PrefetchScalarGridSpec(
@@ -454,7 +521,7 @@
         grid=(1,),
         in_specs=[whole(piece) for piece in pieces]
         + [
-            pl.BlockSpec(w_out.shape, lambda i, _: (0, 0)),
+            pl.BlockSpec(w_out_t.shape, lambda i, _: (0, 0)),
             pl.BlockSpec((full, count), lambda i, _: (0, first)),
             pl.BlockSpec(vectors.shape, lambda i, _: (0, 0)),
         ],
@@ -464,7 +531,6 @@
             pl.BlockSpec((8, count), lambda i, _: (0, 0)),
             pl.BlockSpec((full, count), lambda i, _: (0, 0)),
         ],
-        scratch_shapes=[pltpu.VMEM((full, full), bf16)],
     )
     return pl.pallas_call(
         out_norm_body,
@@ -475,17 +541,19 @@
             shape((8, count), f32),
             shape((full, count), bf16),
         ],
-        compiler_params=params(),
+        compiler_params=params(24),
         cost_estimate=cost(2 * full * full * count, 10**7),
         name="out_norm",
-    )(starts, *pieces, w_out, x_full, vectors)
+    )(starts, *pieces, w_out_t, x_full, vectors)
 
 
 def erf_parts(v):
     return 0.5 * (1.0 + lax.erf(v * (0.5**0.5))), jnp.exp(-0.5 * v * v)
 
 
-def feed_body(n_ref, dy_ref, up_ref, down_t_ref, b_ref, act_ref, grad_ref, part_ref, bias_ref, up_s, down_s):
+def feed_body(
+    info, n_ref, dy_ref, up_ref, down_t_ref, b_ref, act_ref, grad_ref, theirs_ref, mine_ref, bias_ref, up_s, down_s
+):
     step = pl.program_id(0)
 
     @pl.when(step == 0)
@@ -501,45 +569,63 @@
     grad = (grad_act * (cdf + pre * bell * 0.3989422804014327)).astype(bf16)
     grad_ref[...] = grad
     bias_ref[...] += dot_nn(grad, jnp.ones((grad.shape[1], 128), bf16))
-    part_ref[0] = dot_nn(up_ref[...], grad).astype(bf16)
-
-
-def feed(normed, dy, w_up, w_down_t, bias, block=256):
+    part = dot_nn(up_ref[...], grad).astype(bf16)
+
+    @pl.when(step < 2)
+    def _():
+        theirs_ref[0] = part
+
+    @pl.when(step >= 2)
+    def _():
+        mine_ref[0] = part
+
+
+def turn(step, info):
+    return jnp.where(step < 2, 2 * step + 1 - info[0], 2 * (step - 2) + info[0])
+
+
+def feed(core, normed, dy, w_up, w_down_t, bias):
     full, count = normed.shape
     hidden = w_up.shape[1]
-    cols = pl.BlockSpec((full, block), lambda i: (0, i))
-    hid = pl.BlockSpec((hidden, block), lambda i: (0, i))
+    block = count // 4
+    cols = pl.BlockSpec((full, block), lambda i, c: (0, turn(i, c)))
+    hid = pl.BlockSpec((hidden, block), lambda i, c: (0, turn(i, c)))
     return pl.pallas_call(
         feed_body,
-        grid=(count // block,),
-        in_specs=[
-            cols,
-            cols,
-            pl.BlockSpec((full, hidden), lambda i: (0, 0)),
-            pl.BlockSpec((full, hidden), lambda i: (0, 0)),
-            pl.BlockSpec((hidden, 1), lambda i: (0, 0)),
-        ],
-        out_specs=[
-            hid,
-            hid,
-            pl.BlockSpec((1, full, block), lambda i: (i, 0, 0)),
-            pl.BlockSpec((hidden, 128), lambda i: (0, 0)),
-        ],
+        grid_spec=pltpu.PrefetchScalarGridSpec(
+            num_scalar_prefetch=1,
+            grid=(4,),
+            in_specs=[
+                cols,
+                cols,
+                pl.BlockSpec((full, hidden), lambda i, c: (0, 0)),
+                pl.BlockSpec((full, hidden), lambda i, c: (0, 0)),
+                pl.BlockSpec((hidden, 1), lambda i, c: (0, 0)),
+            ],
+            out_specs=[
+                hid,
+                hid,
+                pl.BlockSpec((1, full, block), lambda i, c: (jnp.minimum(i, 1), 0, 0)),
+                pl.BlockSpec((1, full, block), lambda i, c: (jnp.maximum(i - 2, 0), 0, 0)),
+                pl.BlockSpec((hidden, 128), lambda i, c: (0, 0)),
+            ],
+            scratch_shapes=[pltpu.VMEM((hidden, full), bf16), pltpu.VMEM((hidden, full), bf16)],
+        ),
         out_shape=[
             shape((hidden, count), bf16),
             shape((hidden, count), bf16),
-            shape((count // block, full, block), bf16),
+            shape((2, full, block), bf16),
+            shape((2, full, block), bf16),
             shape((hidden, 128), f32),
         ],
-        scratch_shapes=[pltpu.VMEM((hidden, full), bf16), pltpu.VMEM((hidden, full), bf16)],
-        compiler_params=params(),
+        compiler_params=params(40),
         cost_estimate=cost(6 * full * hidden * count, 2 * 10**7, 2 * hidden * count),
         name="feed",
-    )(normed, dy, w_up, w_down_t, bias)
-
-
-def second_back_body(index, mine_ref, got_ref, after_ref, dy_ref, stat_ref, vec_ref, out_ref, sums_ref):
-    back = mine_ref[...] + got_ref[...].astype(f32)
+    )(core, normed, dy, w_up, w_down_t, bias)
+
+
+def second_back_body(index, mine_ref, got_ref, across_ref, after_ref, dy_ref, stat_ref, vec_ref, out_ref, sums_ref):
+    back = mine_ref[0].astype(f32) + got_ref[0].astype(f32) + across_ref[...].astype(f32)
     full = back.shape[0]
     mean, inv = stat_ref[0:1, :], stat_ref[1:2, :]
     unit = (after_ref[...] - mean) * inv
@@ -554,17 +640,19 @@
     sums_ref[:, 2:3] = jnp.sum(low.astype(f32), axis=1, keepdims=True)
 
 
-def second_back(index, mine, got, after, dy, stats, vectors):
-    full, count = mine.shape
+def second_back(index, mine, got, across, after, dy, stats, vectors):
+    full, count = across.shape
     fixed = pl.BlockSpec((full, count), lambda i, c: (0, 0))
     moved = pl.BlockSpec((full, count), lambda i, c: (0, c[0]))
+    part = pl.BlockSpec((1, full, count), lambda i, c: (c[1], 0, 0))
     return pl.pallas_call(
         second_back_body,
         grid_spec=pltpu.PrefetchScalarGridSpec(
             num_scalar_prefetch=1,
             grid=(1,),
             in_specs=[
-                fixed,
+                part,
+                part,
                 fixed,
                 moved,
                 moved,
@@ -574,10 +662,10 @@
             out_specs=[fixed, pl.BlockSpec((full, 8), lambda i, c: (0, 0))],
         ),
         out_shape=[shape((full, count), bf16), shape((full, 8), f32)],
-        compiler_params=params(),
+        compiler_params=params(16),
         cost_estimate=cost(20 * full * count, 5 * 10**6),
         name="second_back",
-    )(index, mine, got, after, dy, stats, vectors)
+    )(index, mine, got, across, after, dy, stats, vectors)
 
 
 def attn_grad_body(info, p0, p1, p2, p3, w_ref, branch_ref, out_ref):
@@ -609,6 +697,122 @@
     )(info, *pieces, w_out)
 
 
+def one_back_body(info, w_ref, dq_ref, one_ref, there_ref, two_ref, theirs_ref, mine_ref, grad_ref):
+    step = pl.program_id(0)
+    width = dq_ref.shape[0]
+
+    @pl.when(step == 0)
+    def _():
+        grad_ref[:width, :] = dq_ref[...]
+
+    @pl.when((step == 0) & (info[1] == 0))
+    def _():
+        grad_ref[width:, :] = (one_ref[...].astype(f32) + there_ref[...].astype(f32)).astype(bf16)
+
+    @pl.when((step == 0) & (info[1] != 0))
+    def _():
+        grad_ref[width:, :] = two_ref[...]
+
+    part = dot_nn(w_ref[0], grad_ref[...]).astype(bf16)
+
+    @pl.when(step < 2)
+    def _():
+        theirs_ref[0] = part
+
+    @pl.when(step >= 2)
+    def _():
+        mine_ref[0] = part
+
+
+def one_back(info, w_heads, dq, dkv_one, dkv_there, dkv_two, wait):
+    full, wide = w_heads.shape
+    count = dq.shape[1]
+    part = full // 4
+    parts = shape((2, part, count), bf16)
+    return pl.pallas_call(
+        waiting(one_back_body, 6, 1),
+        grid_spec=pltpu.PrefetchScalarGridSpec(
+            num_scalar_prefetch=1,
+            grid=(4,),
+            in_specs=[pl.BlockSpec((1, part, wide), lambda i, c: (turn(i, c), 0, 0))]
+            + [whole(array) for array in (dq, dkv_one, dkv_there, dkv_two)]
+            + [ANY],
+            out_specs=[
+                pl.BlockSpec((1, part, count), lambda i, c: (jnp.minimum(i, 1), 0, 0)),
+                pl.BlockSpec((1, part, count), lambda i, c: (jnp.maximum(i - 2, 0), 0, 0)),
+            ],
+            scratch_shapes=[pltpu.VMEM((wide, count), bf16)],
+        ),
+        out_shape=[parts, parts],
+        compiler_params=params(16),
+        cost_estimate=cost(2 * full * wide * count, 10**7),
+        name="one_back",
+    )(info, w_heads.reshape(4, part, wide), dq, dkv_one, dkv_there, dkv_two, wait)
+
+
+def weight_grad_body(info, own_ref, before_ref, dq_ref, one_ref, two_ref, theirs_ref, mine_ref, acc_ref):
+    width = dq_ref.shape[0]
+    acc_ref[:, :width] = dot_nt(own_ref[...], dq_ref[...])
+
+    @pl.when(info[0] == 0)
+    def _():
+        acc_ref[:, width:] = dot_nt(own_ref[...], one_ref[...])
+
+    @pl.when(info[0] != 0)
+    def _():
+        acc_ref[:, width:] = dot_nt(before_ref[...], one_ref[...]) + dot_nt(own_ref[...], two_ref[...])
+
+    chunk = theirs_ref.shape[1]
+    for k in range(4):
+        theirs = ((1 - info[0]) * 4 + k) * chunk
+        mine = (info[0] * 4 + k) * chunk
+        theirs_ref[k] = acc_ref[pl.ds(pl.multiple_of(theirs, 8), chunk), :].astype(bf16)
+        mine_ref[k] = acc_ref[pl.ds(pl.multiple_of(mine, 8), chunk), :].astype(bf16)
+
+
+def weight_grad(info, own, before, dq, dkv_one, dkv_two):
+    rows, count = own.shape
+    columns = 3 * dq.shape[0]
+    result = shape((4, rows // 8, columns), bf16)
+    operands = [own, before, dq, dkv_one, dkv_two]
+    return pl.pallas_call(
+        weight_grad_body,
+        grid_spec=pltpu.PrefetchScalarGridSpec(
+            num_scalar_prefetch=1,
+            grid=(1,),
+            in_specs=[whole(array) for array in operands],
+            out_specs=[whole(result), whole(result)],
+            scratch_shapes=[pltpu.VMEM((rows, columns), f32)],
+        ),
+        out_shape=[result, result],
+        compiler_params=params(24),
+        cost_estimate=cost(3 * rows * columns * count, 8 * 10**6),
+        name="weight_grad",
+    )(info, *operands)
+
+
+def product_body(left_ref, right_ref, out_ref):
+    out_ref[...] = dot_nt(left_ref[...], right_ref[...]).astype(bf16)
+
+
+def product(left, right):
+    rows, count = left.shape
+    columns = right.shape[0]
+    return pl.pallas_call(
+        product_body,
+        grid=(2,),
+        in_specs=[
+            pl.BlockSpec((rows // 2, count), lambda i: (i, 0)),
+            pl.BlockSpec((columns, count), lambda i: (0, 0)),
+        ],
+        out_specs=pl.BlockSpec((rows // 2, columns), lambda i: (i, 0)),
+        out_shape=shape((rows, columns), bf16),
+        compiler_params=params(24),
+        cost_estimate=cost(2 * rows * columns * count, 6 * 10**6),
+        name="product",
+    )(left, right)
+
+
 X_SWAP = [(0, 2), (2, 0), (1, 3), (3, 1)]
 CORE_SWAP = [(0, 1), (1, 0), (2, 3), (3, 2)]
 
@@ -632,6 +836,10 @@
 
 def after(array, *done):
     return lax.optimization_barrier((array,) + done)[0]
+
+
+def after_all(arrays, *done):
+    return lax.optimization_barrier(tuple(arrays) + done)[: len(arrays)]
 
 
 def gather_col(shard):
@@ -640,8 +848,7 @@
     return shard, other, beside[0], beside[1]
 
 
-def gather_col_after(shard, *done):
-    other = after(swap_x(shard), *done)
+def gather_rest(shard, other):
     beside = swap_core(jnp.stack([shard, other]))
     return shard, other, beside[0], beside[1]
 
@@ -650,24 +857,22 @@
     by_core = parts.reshape((2, 2) + parts.shape[1:])
     mine = lax.dynamic_index_in_dim(by_core, core_bit, 1, keepdims=False)
     theirs = lax.dynamic_index_in_dim(by_core, 1 - core_bit, 1, keepdims=False)
-    got = swap_core(theirs)
-
+    return across_sum(mine, swap_core(theirs), x_bit)
+
+
+def across_sum(mine, got, x_bit):
     def of(index):
         return lax.dynamic_index_in_dim(mine, index, 0, keepdims=False).astype(
             f32
         ) + lax.dynamic_index_in_dim(got, index, 0, keepdims=False).astype(f32)
 
-    return got, of(x_bit), swap_x(of(1 - x_bit).astype(bf16))
+    return of(x_bit), swap_x(of(1 - x_bit).astype(bf16))
 
 
 def seq_halves(partials):
-    seq_index = lax.axis_index("seq")
-    chunks = [p.reshape(2, 4, p.shape[0] // 8, p.shape[1]) for p in partials]
-    mine = [lax.dynamic_index_in_dim(c, seq_index, 0, keepdims=False) for c in chunks]
-    theirs = jnp.stack(
-        [lax.dynamic_index_in_dim(c, 1 - seq_index, 0, keepdims=False) for c in chunks]
-    )
-    return jnp.stack(mine), swap_seq(theirs)
+    theirs = jnp.stack([p[0] for p in partials]) if len(partials) > 1 else partials[0][0][None]
+    mine = jnp.stack([p[1] for p in partials]) if len(partials) > 1 else partials[0][1][None]
+    return mine, swap_seq(theirs)
 
 
 def row_chunk(halves, offset):
@@ -704,8 +909,13 @@
     return row_chunk(halves, 0) + near[0].astype(f32) + near[1].astype(f32)
 
 
+def scatter_row(partial):
+    chunks = partial.reshape(2, 4, partial.shape[0] // 8, partial.shape[1])
+    return lax.psum_scatter(chunks, "row", scatter_dimension=1, tiled=False)
+
+
 def scatter_plain(partial):
-    return lax.psum_scatter(partial.astype(f32), ("seq", "row"), scatter_dimension=0, tiled=True)
+    return lax.psum_scatter(partial, ("seq", "row"), scatter_dimension=0, tiled=True).astype(f32)
 
 
 def combine_axis(array, axis, join):
@@ -783,7 +993,7 @@
     vectors = jnp.stack(
         [ln1_gain, ln1_bias, ln2_gain, ln2_bias, b_qv[0], b_qv[1], own_rows(b_out)], axis=1
     )
-    x_sent = jnp.concatenate([x_shard, jnp.pad(vectors, ((0, 0), (0, 121)))], axis=1)
+    x_sent = jnp.concatenate([x_shard, jnp.pad(vectors, ((0, 0), (0, 121))), dy_shard], axis=1)
 
     slot_column = lax.broadcasted_iota(jnp.int32, (1, 3 * width), 1)
     slot_part, slot_index = slot_column // width, slot_column % width
@@ -800,101 +1010,84 @@
     def edge_of(array):
         return jnp.concatenate([array[:, p * part : p * part + spare] for p in range(3)], axis=1)
 
+    where = jnp.stack([seq_index, head_first * E]).astype(jnp.int32)
+    core = core_bit[None].astype(jnp.int32)
     if fast:
-        left = ring(w_flat, "row", 1)
-        right = ring(w_flat, "row", -1)
-        x_pieces = gather_col(x_sent)
+        w_sent = jnp.concatenate(
+            [w_flat, lax.dynamic_slice_in_dim(w_out, col_index * part, part, 1)], axis=1
+        )
+        left = ring(w_sent, "row", 1)
+        right = ring(w_sent, "row", -1)
         x_before = lax.ppermute(x_shard, "seq", [(0, 1)])
-        x_full, normed_one, stats_one, columns = first_norm(order, x_pieces, span)
-        before_pieces = gather_col_after(after(x_before, x_pieces[1]), normed_one)
-        near_edge = lax.ppermute(
-            jnp.concatenate([edge_of(w_flat), edge_of(left), edge_of(right)]), "col", next_to_here
+        w_order = ((row_index - jnp.arange(4, dtype=jnp.int32)) % 4).astype(jnp.int32)
+        near = near_rows(w_order, [w_sent, after(left, x_before), right], pick_own)
+        x_pieces = gather_rest(x_sent, after(swap_x(x_sent), near[2]))
+        x_full, normed_one, stats_one, columns, dy_full = first_norm(order, x_pieces, span)
+        x_across = swap_x(after(x_before, x_pieces[1]))
+        cut = part_rows // 32 * 16 + 16
+        far_a = ring(left[:cut], "row", 1)
+        far_b = ring(right[cut:], "row", -1)
+        w_base, edges, out_mine = far_rows(w_order, near, [far_a, far_b], pick_own, normed_one)
+        edges = lax.ppermute(edges, "col", next_to_here)
+        some, give = 176, 96
+        w_down_rows = w_down.T
+        up_piece = jnp.concatenate(
+            [lax.dynamic_slice_in_dim(w, seq_index * give, some, 0) for w in (w_up, w_down_rows)]
         )
-        cut = part_rows // 32 * 16 + 16
-        far_a = ring(after(left[:cut], normed_one), "row", 1)
-        far_b = ring(after(right[cut:], normed_one), "row", -1)
-        far_edge = lax.ppermute(
-            jnp.concatenate([edge_of(far_a), edge_of(far_b)]), "col", next_to_here
+        up_piece = after(up_piece, out_mine)
+        up_left = ring(up_piece, "row", 1)
+        up_right = ring(up_piece, "row", -1)
+
+        before_pieces = gather_rest(x_before, after(x_across, out_mine))
+        _, normed_before, _ = first_norm(order, before_pieces, span, columns)
+        out_across = swap_x(out_mine)
+        queries, kv_all, w_heads = project(
+            where, w_base, after(edges, normed_before), pick_next, columns, normed_one, normed_before
         )
-        w_order = ((row_index - jnp.arange(4, dtype=jnp.int32)) % 4).astype(jnp.int32)
-        _, normed_before, _ = first_norm(order, before_pieces, span, columns)
-        w_heads = head_weights(
-            w_order,
-            [w_flat, left, right, far_a, far_b, near_edge, after(far_edge, normed_before)],
-            pick_own,
-            pick_next,
+        attn_one = attn_fwd(info, queries, kv_all, slots, 0)
+        attn_across_one = swap_x(attn_one[0])
+        out_pieces = gather_rest(out_mine, after(out_across, attn_one[3]))
+        def given(pieces):
+            return jnp.concatenate(
+                [lax.dynamic_slice_in_dim(p, seq_index * (some - give), give, 0) for p in pieces]
+            )
+
+        attn_two = attn_fwd(info, after(queries, attn_one[3]), kv_all, slots, 1)
+        attn_across_two = swap_x(attn_two[0])
+        up_left, up_right = after_all((up_left, up_right), attn_two[3], attn_across_one)
+        near_mine = (up_left[:some], up_left[some:], up_right[:some], up_right[some:])
+        near_theirs = swap_seq(given(near_mine))
+        far_mine = (ring(near_mine[0], "row", 1), ring(near_mine[3], "row", -1))
+        attn_pieces_one = gather_rest(attn_one[0], after(attn_across_one, attn_two[3]))
+        w_out_t, w_out_all = assemble(
+            (order * part).astype(jnp.int32),
+            after_all(out_pieces, attn_two[3]),
+            [(n, 0, part, n) for n in range(4)],
+            full,
+            E,
+            True,
         )
-        where = jnp.stack([seq_index, head_first * E]).astype(jnp.int32)
-        queries, kv_all = project(where, w_heads, columns, normed_one, normed_before)
-        attn_one = attn_fwd(info, queries, kv_all, slots, 0)
-        attn_pieces_one = gather_col(attn_one[0])
-        attn_two = attn_fwd(info, after(queries, attn_one[3]), kv_all, slots, 1)
-        attn_pieces_two = gather_col(attn_two[0])
-        dy_pieces = gather_col(after(dy_shard, attn_two[3], attn_pieces_one[1]))
-
-        some = part_rows // 64 * 16 + 16
-        piece = after(
-            lax.dynamic_slice_in_dim(w_out, col_index * (some - 16), some, 0), far_a, far_b
-        )
-        mine = jnp.concatenate([ring(piece, "row", 1), ring(piece, "row", 2), ring(piece, "row", -1)])
-        mine = after(mine, attn_one[3])
-        across = swap_x(mine)
-        beside = swap_core(jnp.concatenate([mine, across]))
-        starts = [row_index * part_rows]
-        plan = [(0, 0, part_rows, 0)]
-        for which, base, device in ((1, 0, 0), (2, 0, 1), (3, 0, 2), (3, 3 * some, 3)):
-            for index, away in enumerate((1, 2, 3)):
-                plan.append((which, base + index * some, some, len(starts)))
-                starts.append((row_index - away) % 4 * part_rows + order[device] * (some - 16))
-        w_out_all = assemble(
-            jnp.stack(starts).astype(jnp.int32), [w_out, mine, across, beside], plan, full, E
-        )
-
-        some = part_rows // 32 * 16 + 16
-        other = part_rows - some
-        w_down_rows = w_down.T
-        piece = jnp.concatenate(
-            [
-                lax.dynamic_slice_in_dim(w_up, seq_index * other, some, 0),
-                lax.dynamic_slice_in_dim(w_down_rows, seq_index * other, some, 0),
-            ]
-        )
-        piece = after(piece, far_a, far_b)
-        up_left = ring(piece, "row", 1)
-        up_right = ring(piece, "row", -1)
-        near_mine = after(jnp.concatenate([up_left, up_right]), attn_one[3])
-        near_theirs = swap_seq(near_mine)
-        far_mine = jnp.concatenate(
-            [ring(near_mine[:some], "row", 1), ring(near_mine[3 * some :], "row", -1)]
-        )
-        far_mine = after(far_mine, attn_two[3])
-        far_theirs = swap_seq(far_mine)
-
-        def weight(shard, base):
+        far_theirs = swap_seq(given(far_mine))
+        def weight(shard, which):
             starts = [row_index * part_rows]
             plan = [(0, 0, part_rows, 0)]
-            for which, start, away, bit in (
-                (1, base, 1, seq_index),
-                (1, 2 * some + base, 3, seq_index),
-                (2, base, 1, 1 - seq_index),
-                (2, 2 * some + base, 3, 1 - seq_index),
-                (3, base, 2, seq_index),
-                (4, base, 2, 1 - seq_index),
+            pieces = [shard, near_mine[which], near_mine[2 + which], far_mine[which], near_theirs, far_theirs]
+            mine_at, theirs_at = seq_index * give, (1 - seq_index) * some
+            for piece, start, length, away, at in (
+                (1, 0, some, 1, mine_at),
+                (2, 0, some, 3, mine_at),
+                (3, 0, some, 2, mine_at),
+                (4, which * give, give, 1, theirs_at),
+                (4, (2 + which) * give, give, 3, theirs_at),
+                (5, which * give, give, 2, theirs_at),
             ):
-                plan.append((which, start, some, len(starts)))
-                starts.append((row_index - away) % 4 * part_rows + bit * other)
-            return assemble(
-                jnp.stack(starts).astype(jnp.int32),
-                [shard, near_mine, near_theirs, far_mine, far_theirs],
-                plan,
-                full,
-            )
-
-        w_up_all = weight(w_up, 0)
-        w_down_t = weight(w_down_rows, some)
+                plan.append((piece, start, length, len(starts)))
+                starts.append((row_index - away) % 4 * part_rows + at)
+            return assemble(jnp.stack(starts).astype(jnp.int32), pieces, plan, full)
+
     else:
         x_pieces = gather_col(x_sent)
-        x_full, normed_one, stats_one, columns = first_norm(order, x_pieces, span)
+        x_full, normed_one, stats_one, columns, dy_full = first_norm(order, x_pieces, span)
         w_all = lax.all_gather(w_flat, "row", axis=0, tiled=True)
         edges = lax.ppermute(edge_of(w_all), "col", next_to_here)
         w_heads = (dot_nn(w_all, pick_own) + dot_nn(edges, pick_next)).astype(bf16)
@@ -911,17 +1104,20 @@
         attn_two = attn_fwd(info, queries, kv_all, slots, 1)
         attn_pieces_one = gather_col(attn_one[0])
         attn_pieces_two = gather_col(attn_two[0])
-        dy_pieces = gather_col(dy_shard)
         w_out_all = jnp.pad(lax.all_gather(w_out, "row", axis=0, tiled=True), ((0, E), (0, 0)))
+        w_out_t = w_out_all[:full].T
         w_up_all = lax.all_gather(w_up, "row", axis=0, tiled=True)
         w_down_t = lax.all_gather(w_down.T, "row", axis=0, tiled=True)
-    dy_full = assemble(
-        (order * part).astype(jnp.int32), dy_pieces, [(n, 0, part, n) for n in range(4)], full
-    )
 
     head_rows = (first_head(order) * E).astype(jnp.int32)
-    normal_one = out_norm(head_rows, attn_pieces_one, w_out_all, x_full, columns, 0)
-    normal_two = out_norm(head_rows, attn_pieces_two, w_out_all, x_full, columns, 1)
+    normal_one = out_norm(head_rows, attn_pieces_one, w_out_t, x_full, columns, 0)
+    if fast:
+        attn_pieces_two = gather_rest(attn_two[0], after(attn_across_two, normal_one[2]))
+    normal_two = out_norm(head_rows, attn_pieces_two, w_out_t, x_full, columns, 1)
+    if fast:
+        far_theirs = after(far_theirs, normal_two[2])
+        w_up_all = weight(w_up, 0)
+        w_down_t = weight(w_down_rows, 1)
 
     def joined(index):
         return jnp.concatenate([normal_one[index], normal_two[index]], axis=1)
@@ -940,28 +1136,33 @@
     )
     placed_top = jnp.pad(placed_top, (0, full - H))
 
-    act, grad_pre, back_parts, bup_sums = feed(
-        normed_two, dy_full, w_up_all, w_down_t, b_up.astype(f32)[:, None]
+    act, grad_pre, back_theirs, back_mine, bup_sums = feed(
+        core, normed_two, dy_full, w_up_all, w_down_t, b_up.astype(f32)[:, None]
     )
-    back_core, back_mine, back_got = scatter_col(back_parts, x_bit, core_bit)
-    act_then = after(act, back_core)
-    up_partial = dot_nt(normed_two, after(grad_pre, back_core)).astype(bf16)
-    down_partial = dot_nt(dy_full, act_then).astype(bf16)
+    back_core = swap_core(back_theirs)
+    back_sent = (
+        lax.dynamic_index_in_dim(back_mine, 1 - x_bit, 0, keepdims=False).astype(f32)
+        + lax.dynamic_index_in_dim(back_core, 1 - x_bit, 0, keepdims=False).astype(f32)
+    ).astype(bf16)
+    back_got = swap_x(back_sent)
+    up_partial = product(normed_two, after(grad_pre, back_sent))
+    down_partial = product(dy_full, after(act, back_sent))
 
     branch_rows, row_sums = second_back(
-        col_index[None].astype(jnp.int32),
+        jnp.stack([col_index, x_bit]).astype(jnp.int32),
         back_mine,
-        back_got,
+        back_core,
+        after(back_got, up_partial, down_partial),
         after_attn,
         dy_full,
         stats_two,
         columns,
     )
-    branch_pieces = gather_col(branch_rows)
+    branch_across = swap_x(branch_rows)
     down = dot_nn(w_down_t, after(act, branch_rows)).astype(bf16).reshape(col_count, part, span)
     head_info = jnp.concatenate([jnp.stack([head_first * E, head_count * E]), order]).astype(jnp.int32)
+    branch_pieces = gather_rest(branch_rows, after(branch_across, down))
     branch, grad_attn = attn_grad(head_info, branch_pieces, w_out_all, width)
-    out_partial = dot_nt(attn_all, own_rows(branch)).astype(bf16)
     middle = jnp.concatenate([row_sums[:, :3].T, placed_top[None]])
 
     def join(one, two):
@@ -971,43 +1172,66 @@
     middle = join(middle, swap_x(middle))
     middle = join(middle, swap_core(middle))
 
+    branch_own = own_rows(branch)
+    out_partial = dot_nt(attn_all, branch_own).astype(bf16)
     if fast:
-        feed_halves = seq_halves([up_partial, down_partial])
-        feed_halves = (feed_halves[0], after(feed_halves[1], grad_attn))
-        feed_far = row_sum_one(feed_halves)
-        out_halves = seq_halves([out_partial])
+
+        def halves_of(partial):
+            chunks = partial.reshape(2, 4, partial.shape[0] // 8, partial.shape[1])
+            return [
+                lax.dynamic_index_in_dim(chunks, i, 0, keepdims=False) for i in (1 - seq_index, seq_index)
+            ]
+
+        feed_halves = seq_halves([halves_of(up_partial), halves_of(down_partial)])
+        out_chunks = halves_of(out_partial)
+        down_mine, down_got = scatter_col(down, x_bit, core_bit)
         dq_one, dkv_one = attn_bwd(
-            info, queries, kv_all, after(grad_attn, out_partial), exact, lse, None, slots, 0, False
+            info, after(queries, out_partial), kv_all, grad_attn, exact, lse, None, slots, 0, False
         )
         dkv_there = lax.ppermute(dkv_one, "seq", [(1, 0)])
-        feed_near = row_sum_two(feed_halves, (after(feed_far[0], dq_one), after(feed_far[1], dq_one)))
+        feed_halves = (feed_halves[0], after(feed_halves[1], dq_one))
+        feed_far = row_sum_one(feed_halves)
         dq, dkv_two = attn_bwd(
-            info, after(queries, dq_one), kv_all, grad_attn, exact, lse, dq_one, slots, 1, True
+            info,
+            after(queries, dq_one, down_got, middle, feed_halves[1]),
+            kv_all,
+            grad_attn,
+            exact,
+            lse,
+            dq_one,
+            slots,
+            1,
+            True,
         )
-        dkv = jnp.where(
-            seq_index == 0,
-            (dkv_one.astype(f32) + after(dkv_there, dq).astype(f32)).astype(bf16),
+        chunks = weight_grad(where, normed_one, normed_before, dq, dkv_one, dkv_two)
+        halves = seq_halves([[jnp.concatenate(pair, axis=2) for pair in zip(chunks, out_chunks)]])
+        one_theirs, one_mine = one_back(
+            jnp.stack([core_bit, seq_index]).astype(jnp.int32),
+            w_heads,
+            dq,
+            dkv_one,
+            dkv_there,
             dkv_two,
+            chunks[0],
         )
-        heads_grad = jnp.concatenate([dq, dkv])
-        one_parts = dot_nn(w_heads, heads_grad).astype(bf16).reshape(col_count, part, span)
-        one_core, one_mine, one_got = scatter_col(one_parts, x_bit, core_bit)
-        partial = dot_nt(normed_one, after(heads_grad, one_parts)).astype(bf16)
-        halves = seq_halves([partial])
-        feed_sums = row_sum_end(
-            feed_halves, (after(feed_near[0], one_core, partial), after(feed_near[1], one_core, partial))
+        feed_near = row_sum_two(feed_halves, after_all(feed_far, one_theirs))
+        one_core = swap_core(one_theirs)
+        one_mine, one_got = across_sum(one_mine, one_core, x_bit)
+        halves = (halves[0], after(halves[1], one_got, *feed_near))
+        last_far = row_sum_one(halves)
+        feed_sums = row_sum_end(feed_halves, feed_near)
+        grad_w_up, grad_w_down = feed_sums[0], feed_sums[1].T
+        last_near = row_sum_two(halves, last_far)
+        last = row_sum_end(halves, last_near)[0]
+        summed, out_columns = last[:, : 3 * width], last[:, 3 * width :].astype(bf16)
+        middle = after(middle, *last_far)
+        head_sums = jnp.sum(dq.astype(f32), axis=1), (
+            jnp.sum(dkv_one[width:].astype(f32), axis=1) + jnp.sum(dkv_two[width:].astype(f32), axis=1)
         )
-        grad_w_up, grad_w_down = feed_sums[0], feed_sums[1].T
-        _, down_mine, down_got = scatter_col(after(down, one_mine), x_bit, core_bit)
-        last_halves = (
-            jnp.concatenate([halves[0], out_halves[0]], axis=3),
-            jnp.concatenate([after(halves[1], one_got), after(out_halves[1], one_core)], axis=3),
-        )
-        last_far = row_sum_one(last_halves)
-        last_near = row_sum_two(last_halves, last_far)
-        last = row_sum_end(last_halves, last_near)[0]
-        summed, out_columns = last[:, : 3 * width], last[:, 3 * width :].astype(bf16)
     else:
+        grad_w_up = scatter_plain(up_partial)
+        grad_w_down = scatter_plain(down_partial).T
+        out_columns = scatter_plain(out_partial).astype(bf16)
         dq, pieces = None, []
         for segment in range(seq_count):
             dq, dkv_one = attn_bwd(
@@ -1017,14 +1241,12 @@
         dkv = lax.psum_scatter(
             jnp.concatenate(pieces, axis=1), "seq", scatter_dimension=1, tiled=True
         )
-        grad_w_up = scatter_plain(up_partial)
-        grad_w_down = scatter_plain(down_partial).T
-        out_columns = scatter_plain(out_partial).astype(bf16)
         heads_grad = jnp.concatenate([dq, dkv])
         one_parts = dot_nn(w_heads, heads_grad).astype(bf16).reshape(col_count, part, span)
-        _, one_mine, one_got = scatter_col(one_parts, x_bit, core_bit)
+        one_mine, one_got = scatter_col(one_parts, x_bit, core_bit)
         summed = scatter_plain(dot_nt(normed_one, heads_grad).astype(bf16))
-        _, down_mine, down_got = scatter_col(down, x_bit, core_bit)
+        head_sums = jnp.sum(dq.astype(f32), axis=1), jnp.sum(dkv[width:].astype(f32), axis=1)
+        down_mine, down_got = scatter_col(down, x_bit, core_bit)
     summed = summed.reshape(-1, 3, width)
     grad_w_out = by_index(gather_col(out_columns)).astype(f32)
     block_out = (
@@ -1046,8 +1268,7 @@
         )
 
     grad_w_qkv = to_owner(summed)
-    head_sums = jnp.sum(heads_grad.astype(f32), axis=1)
-    head_sums = jnp.stack([head_sums[:width], head_sums[2 * width :]])
+    head_sums = jnp.stack(head_sums)
     head_sums = lax.dynamic_update_slice_in_dim(
         jnp.zeros((2, full + E), f32), head_sums, head_first * E, 1
     )[:, :full]

time: 514 us -> 449 us (0.87)
  the two profiles are of different devices: /device:TPU:0 before, /device:TPU:18 now
where the time goes in v3:
time: 449 us; the launch traced here: 440 us
  waiting for transfers between devices  136 us (30%)
  Pallas kernels  109 us (24%)
  local copies, waits for them, and re-layouts  76.6 us (17%)
  other arithmetic  57.6 us (13%)
  starting transfers between devices  51.9 us (12%)
  matrix products  5.46 us (1%)
    ppermute x20, waiting for transfers between devices, ring(): lax.ppermute(array, axis, [(i, (i + shift) % count) for i in range(count)])  77.2 us
    unnamed x240, local copies, waits for them, and re-layouts  27.9 us
    ppermute x20, starting transfers between devices, ring(): lax.ppermute(array, axis, [(i, (i + shift) % count) for i in range(count)])  22.7 us
    pallas_call x1, Pallas kernels, feed(): pl.pallas_call(feed_body, grid_spec=pltpu.PrefetchScalarGridSpec(num_scal...  19.7 us
    ppermute x4, waiting for transfers between devices, swap_seq(): return lax.ppermute(array, 'seq', [(0, 1), (1, 0)])  19.4 us
    pallas_call x2, Pallas kernels, attn_bwd(): pl.pallas_call(functools.partial(attn_bwd_body, slots, keys, segment * co...  18.8 us
    ppermute x12, starting transfers between devices, swap_x(): return lax.ppermute(array, 'col', X_SWAP)  15.3 us
    ppermute x1, waiting for transfers between devices, on_device(): dkv_there = lax.ppermute(dkv_one, 'seq', [(1, 0)])  14.5 us
  transfers between devices with their start and end apart: 52, of which 17 were waited for; matrix products, arithmetic and copies ran while one was open for 25% of the time, Pallas kernels for 19%

profile of v3, /device:TPU:18, one launch (start us, length us, event | category | flops | bytes accessed | tf_op | source)
XLA Modules:
  0.0 440.2 jit_solution(10496595241459432417)
XLA Ops:
  0.7 4.4 %collective-permute-start.1 = (bf16[272,1024]{1,0:T(8,128)(2,1)}, bf16[272,1024]{1,0:T(8,128)(2,1)}, u32[]{:S(2)}, u32[]{:S(2)}) collective-permute-start(bf16[272,1024]{1,0:T(8,128)(2,1)} %bitcast.258), channel_id=1, source_target_pairs={{0,16},{1,17},{2,18},{3,19},{4,20},{5,21},{6,22},{7,23},{8,24},{9,... | collective-permute-start | bytes 1671176 | tf_op jit(solution)/shard_map/ppermute | solution.py:1021
  9.5 2.4 fusion.7.p0
  17.5 25.0 %collective-permute-done.left = bf16[272,1088]{1,0:T(8,128)(2,1)} collective-permute-done((bf16[272,1088]{1,0:T(8,128)(2,1)S(1)}, bf16[272,1088]{1,0:T(8,128)(2,1)}, u32[]{:S(2)}, u32[]{:S(2)}) %collective-permute-start) | collective-permute-done | bytes 591904 | tf_op jit(solution)/shard_map/ppermute | solution.py:834
  42.5 3.7 near_rows.1
  56.1 2.4 collective-permute-start.4
  61.1 1.8 slice_bitcast_fusion
  63.0 4.7 %first_norm.2 = (bf16[1088,1024]{1,0:T(8,128)(2,1)S(1)}, bf16[1088,1024]{1,0:T(8,128)(2,1)S(1)}, f32[8,1024]{1,0:T(8,128)S(1)}, f32[1152,128]{1,0:T(8,128)S(1)}, bf16[1088,1024]{1,0:T(8,128)(2,1)S(1)}) custom-call(s32[4]{0:T(128)S(1)} %get-tuple-element.251.order, bf16[272,2176]{1,0:T(8,128)(2,1)} %fusion.7.p0, bf16[272,2176]{1,0:T(8,128)(2,1)S(1)} %copy-done.28, ...), custom_call_target="tpu_custom_call" | custom-call | flops 445644 | bytes 178257 | tf_op jit(solution)/shard_map/first_norm/pallas_call | solution.py:132
  70.5 2.0 collective-permute-done.4.refs_5_
  72.5 2.0 collective-permute-done.3.refs_4_
  74.6 2.5 far_rows.1
  79.3 2.2 pad_maximum_fusion.3
  88.6 2.8 collective-permute-start.7
  95.8 4.3 first_norm.3
  100.1 8.7 %collective-permute-done.7.edge_ref = bf16[1088,256]{1,0:T(8,128)(2,1)S(1)} collective-permute-done((bf16[1088,256]{1,0:T(8,128)(2,1)S(1)}, bf16[1088,256]{1,0:T(8,128)(2,1)S(1)}, u32[]{:S(2)}, u32[]{:S(2)}) %collective-permute-start.7) | collective-permute-done | bytes 557088 | tf_op jit(solution)/shard_map/ppermute | solution.py:1031
  108.8 7.1 %project.1 = (bf16[320,1024]{1,0:T(8,128)(2,1)S(1)}, bf16[640,2048]{1,0:T(8,128)(2,1)S(1)}, bf16[1088,960]{1,0:T(8,128)(2,1)S(1)}) custom-call(s32[2]{0:T(128)S(1)} %pad_add_fusion.2.info, bf16[1088,960]{1,0:T(8,128)(2,1)S(1)} %copy-done.45, bf16[1088,256]{1,0:T(8,128)(2,1)S(1)} %collective-permute-done.7.edge_ref, ...), custom_call_target="tpu_custom_call" | custom-call | flops 71303168 | bytes 200000 | tf_op jit(solution)/shard_map/project/pallas_call | solution.py:253
  117.3 6.8 %attn_fwd.2 = (bf16[320,512]{1,0:T(8,128)(2,1)S(1)}, f32[320,512]{1,0:T(8,128)S(1)}, f32[8,512]{1,0:T(8,128)S(1)}, f32[8,128]{1,0:T(8,128)S(1)}) custom-call(s32[2]{0:T(128)S(1)} %pad_add_fusion.1.info, bf16[320,1024]{1,0:T(8,128)(2,1)S(1)} %get-tuple-element.161.q_ref.refs_0_, bf16[640,2048]{1,0:T(8,128)(2,1)S(1)} %get-tuple-element.110.kv_ref.refs_1_), custom_call_target="tpu_custom_call" | custom-call | flops 160000000 | bytes 120000 | tf_op jit(solution)/shard_map/attn_fwd/pallas_call | solution.py:352
  124.2 7.2 %attn_fwd.3 = (bf16[320,512]{1,0:T(8,128)(2,1)S(1)}, f32[320,512]{1,0:T(8,128)S(1)}, f32[8,512]{1,0:T(8,128)S(1)}, f32[8,128]{1,0:T(8,128)S(1)}) custom-call(s32[2]{0:T(128)S(1)} %pad_add_fusion.1.info, bf16[320,1024]{1,0:T(8,128)(2,1)S(1)} %get-tuple-element.161.q_ref.refs_0_, bf16[640,2048]{1,0:T(8,128)(2,1)S(1)} %get-tuple-element.110.kv_ref.refs_1_), custom_call_target="tpu_custom_call" | custom-call | flops 160000000 | bytes 120000 | tf_op jit(solution)/shard_map/attn_fwd/pallas_call | solution.py:352
  132.3 2.0 collective-permute-start.14
  134.3 2.3 pad_maximum_fusion.2
  142.3 2.0 collective-permute-start.18
  146.2 2.2 copy.101
  148.4 11.3 %collective-permute-done.20.refs_3_ = bf16[176,1088]{1,0:T(8,128)(2,1)} collective-permute-done((bf16[176,1088]{1,0:T(8,128)(2,1)}, bf16[176,1088]{1,0:T(8,128)(2,1)}, u32[]{:S(2)}, u32[]{:S(2)}) %collective-permute-start.20) | collective-permute-done | bytes 383008 | tf_op jit(solution)/shard_map/ppermute | solution.py:834
  163.4 2.7 assemble.3
  167.6 3.3 out_norm.2
  172.0 2.2 pad_maximum_fusion.8
  175.9 2.0 collective-permute-start.21
  178.0 2.2 copy.102.refs_4_
  184.5 4.4 %out_norm.3 = (f32[1088,512]{1,0:T(8,128)S(1)}, bf16[1088,512]{1,0:T(8,128)(2,1)S(1)}, f32[8,512]{1,0:T(8,128)S(1)}, bf16[1088,512]{1,0:T(8,128)(2,1)S(1)}) custom-call(s32[4]{0:T(128)S(1)} %copy-done.81, bf16[320,512]{1,0:T(8,128)(2,1)S(1)} %get-tuple-element.124.p0, bf16[320,512]{1,0:T(8,128)(2,1)} %collective-permute-done.14.p1, ...), custom_call_target="tpu_custom_call" | custom-call | flops 24243076 | bytes 200000 | tf_op jit(solution)/shard_map/out_norm/pallas_call | solution.py:535
  191.6 2.0 assemble.5.up_ref
  195.1 2.3 assemble.4.down_t_ref
  198.8 19.7 %feed.1 = (bf16[1088,1024]{1,0:T(8,128)(2,1)S(1)}, bf16[1088,1024]{1,0:T(8,128)(2,1)S(1)}, bf16[2,1088,256]{2,1,0:T(8,128)(2,1)S(1)}, bf16[2,1088,256]{2,1,0:T(8,128)(2,1)S(1)}, f32[1088,128]{1,0:T(8,128)S(1)}) custom-call(s32[1]{0:T(128)} %bitcast.44.info, bf16[1088,1024]{1,0:T(8,128)(2,1)S(1)} %constant_dynamic-update-slice_fusion.2.n_ref.left_ref, ...), custom_call_target="tpu_custom_call" | custom-call | flops 145458464 | bytes 400000 | tf_op jit(solution)/shard_map/feed/pallas_call | solution.py:593
  223.1 3.3 product.2
  226.4 3.3 product.3
  232.3 4.0 collective-permute-done.23.across_ref
  236.3 1.8 second_back.1
  239.7 3.7 convolution_convert_fusion
  244.6 7.5 %collective-permute-done.26.p1 = bf16[1088,256]{1,0:T(8,128)(2,1)S(1)} collective-permute-done((bf16[1088,256]{1,0:T(8,128)(2,1)S(1)}, bf16[1088,256]{1,0:T(8,128)(2,1)S(1)}, u32[]{:S(2)}, u32[]{:S(2)}) %collective-permute-start.26) | collective-permute-done | bytes 557088 | tf_op jit(solution)/shard_map/ppermute | solution.py:821
  253.2 1.8 pad_maximum_fusion
  262.2 1.9 attn_grad.1
  264.1 1.8 convolution_convert_fusion.1
  266.9 16.2 %attn_bwd.2 = (f32[320,1024]{1,0:T(8,128)S(1)}, bf16[640,1024]{1,0:T(8,128)(2,1)S(1)}) custom-call(s32[2]{0:T(128)S(1)} %copy-done.74, bf16[320,1024]{1,0:T(8,128)(2,1)S(1)} %copy-done.9, bf16[640,2048]{1,0:T(8,128)(2,1)S(1)} %get-tuple-element.110.kv_ref.refs_1_, bf16[320,1024]{1,0:T(8,128)(2,1)S(1)} %get-tuple-element.152.refs_2_, ...), custom_call_target="tpu_custom_call" | custom-call | flops 320000000 | bytes 120000 | tf_op jit(solution)/shard_map/attn_bwd/pallas_call | solution.py:461
  283.1 3.6 fusion.27
  286.8 2.3 copy.108
  290.6 2.0 dynamic-slice_bitcast_fusion.5
  293.3 19.3 %collective-permute-done.30 = bf16[2,4,136,1088]{3,2,0,1:T(8,128)(2,1)} collective-permute-done((bf16[2,4,136,1088]{3,2,0,1:T(8,128)(2,1)}, bf16[2,4,136,1088]{3,2,0,1:T(8,128)(2,1)}, u32[]{:S(2)}, u32[]{:S(2)}) %collective-permute-start.30) | collective-permute-done | bytes 2367520 | tf_op jit(solution)/shard_map/ppermute | solution.py:829
  312.6 2.3 convert_add_fusion
  315.0 2.0 collective-permute-start.37
  317.1 2.6 attn_bwd.3
  319.8 5.6 %weight_grad.1 = (bf16[4,136,960]{2,1,0:T(8,128)(2,1)S(1)}, bf16[4,136,960]{2,1,0:T(8,128)(2,1)S(1)}) custom-call(s32[2]{0:T(128)S(1)} %copy-done.77, bf16[1088,1024]{1,0:T(8,128)(2,1)S(1)} %copy-done.6, bf16[1088,1024]{1,0:T(8,128)(2,1)S(1)} %copy-done.16, bf16[320,1024]{1,0:T(8,128)(2,1)S(1)} %get-tuple-element.162.dq_ref.refs_2_, ...), custom_call_target="tpu_custom_call" | custom-call | flops 64172852 | bytes 160000 | tf_op jit(solution)/shard_map/weight_grad/pallas_call | solution.py:778
  325.6 14.5 %collective-permute-done.31.refs_4_ = bf16[640,1024]{1,0:T(8,128)(2,1)S(1)} collective-permute-done((bf16[640,1024]{1,0:T(8,128)(2,1)}, bf16[640,1024]{1,0:T(8,128)(2,1)S(1)}, u32[]{:S(2)}, u32[]{:S(2)}) %collective-permute-start.31) | collective-permute-done | bytes 1310752 | tf_op jit(solution)/shard_map/ppermute | solution.py:1191
  340.2 4.2 one_back.1
  346.4 2.0 collective-permute-start.40
  353.2 22.5 %collective-permute-done.39 = bf16[2,136,1088]{2,1,0:T(8,128)(2,1)} collective-permute-done((bf16[2,136,1088]{2,1,0:T(8,128)(2,1)}, bf16[2,136,1088]{2,1,0:T(8,128)(2,1)}, u32[]{:S(2)}, u32[]{:S(2)}) %collective-permute-start.39) | collective-permute-done | bytes 591904 | tf_op jit(solution)/shard_map/ppermute | solution.py:834
  375.7 1.8 fusion.5
  378.8 2.7 multiply_reduce_fusion
  383.1 2.6 convert_add_fusion.5
  393.3 2.5 add_bitcast_fusion
  399.2 2.4 collective-permute-done.42
  402.9 2.9 collective-permute-done.43
  407.3 2.7 collective-permute-start.45
  410.0 2.1 collective-permute-start.48
  413.3 7.7 %collective-permute-done.44 = f32[7,1088]{1,0:T(8,128)S(1)} collective-permute-done((f32[7,1088]{1,0:T(8,128)S(1)}, f32[7,1088]{1,0:T(8,128)S(1)}, u32[]{:S(2)}, u32[]{:S(2)}) %collective-permute-start.44) | collective-permute-done | bytes 30496 | tf_op jit(solution)/shard_map/ppermute | solution.py:834
  431.0 1.9 collective-permute-start.49
  433.1 4.4 collective-permute-done.49
  (474 shorter events, 124.7 us)
Async XLA Ops:
  0.7 16.8 %collective-permute-start.1 = (bf16[272,1024]{1,0:T(8,128)(2,1)}, bf16[272,1024]{1,0:T(8,128)(2,1)}, u32[]{:S(2)}, u32[]{:S(2)}) collective-permute-start(bf16[272,1024]{1,0:T(8,128)(2,1)} %bitcast.258), channel_id=1, source_target_pairs={{0,16},{1,17},{2,18},{3,19},{4,20},{5,21},{6,22},{7,23},{8,24},{9,... | collective-permute-start | bytes 1671176 | tf_op jit(solution)/shard_map/ppermute | solution.py:1021
  11.9 37.4 %collective-permute-start.5 = (bf16[272,2176]{1,0:T(8,128)(2,1)}, bf16[272,2176]{1,0:T(8,128)(2,1)S(1)}, u32[]{:S(2)}, u32[]{:S(2)}) collective-permute-start(bf16[272,2176]{1,0:T(8,128)(2,1)} %fusion.7.p0), channel_id=1, source_target_pairs={{0,2},{2,0},{1,3},{3,1},{4,6},{6,4},{5,7},{7,5},{8,10},{10,8},{9,1... | collective-permute-start | bytes 3551240 | tf_op jit(solution)/shard_map/ppermute | solution.py:821
  13.4 29.1 %collective-permute-start.2 = (bf16[272,1088]{1,0:T(8,128)(2,1)S(1)}, bf16[272,1088]{1,0:T(8,128)(2,1)}, u32[]{:S(2)}, u32[]{:S(2)}) collective-permute-start(bf16[272,1088]{1,0:T(8,128)(2,1)S(1)} %pad_maximum_fusion.9.own), channel_id=1, source_target_pairs={{0,12},{4,0},{8,4},{12,8},{1,13},{5,1},{9,5},{13,9},{2,14},{6,2},{... | collective-permute-start | bytes 1775624 | tf_op jit(solution)/shard_map/ppermute | solution.py:834
  13.9 28.6 %collective-permute-start = (bf16[272,1088]{1,0:T(8,128)(2,1)S(1)}, bf16[272,1088]{1,0:T(8,128)(2,1)}, u32[]{:S(2)}, u32[]{:S(2)}) collective-permute-start(bf16[272,1088]{1,0:T(8,128)(2,1)S(1)} %pad_maximum_fusion.9.own), channel_id=1, source_target_pairs={{0,4},{4,8},{8,12},{12,0},{1,5},{5,9},{9,13},{13,1},{2,6},{6,10},{... | collective-permute-start | bytes 1775624 | tf_op jit(solution)/shard_map/ppermute | solution.py:834
  51.1 10.0 %collective-permute-start.6 = (bf16[2,272,2176]{2,1,0:T(8,128)(2,1)}, bf16[2,272,2176]{2,1,0:T(8,128)(2,1)}, u32[]{:S(2)}, u32[]{:S(2)}) collective-permute-start(bf16[2,272,2176]{2,1,0:T(8,128)(2,1)} %pad_maximum_fusion.1), channel_id=1, source_target_pairs={{0,1},{1,0},{2,3},{3,2},{4,5},{5,4},{6,7},{7,6},{8,9},{9,8},{10,11... | collective-permute-start | bytes 7102472 | tf_op jit(solution)/shard_map/ppermute | solution.py:825
  52.3 56.5 %copy-start.76 = (s32[2]{0:T(128)}, s32[2]{0:T(128)S(1)}, u32[]{:S(2)}) copy-start(s32[2]{0:T(128)S(1)} %pad_add_fusion.2.info) | copy-start | bytes 28
  56.1 16.4 %collective-permute-start.4 = (bf16[128,1088]{1,0:T(8,128)(2,1)S(1)}, bf16[128,1088]{1,0:T(8,128)(2,1)S(1)}, u32[]{:S(2)}, u32[]{:S(2)}) collective-permute-start(bf16[128,1088]{1,0:T(8,128)(2,1)S(1)} %slice.358), channel_id=1, source_target_pairs={{0,12},{4,0},{8,4},{12,8},{1,13},{5,1},{9,5},{13,9},{2,14},{6,2},{... | collective-permute-start | bytes 835592 | tf_op jit(solution)/shard_map/ppermute | solution.py:834
  59.5 15.1 %collective-permute-start.3 = (bf16[144,1088]{1,0:T(8,128)(2,1)S(1)}, bf16[144,1088]{1,0:T(8,128)(2,1)S(1)}, u32[]{:S(2)}, u32[]{:S(2)}) collective-permute-start(bf16[144,1088]{1,0:T(8,128)(2,1)S(1)} %slice.357), channel_id=1, source_target_pairs={{0,4},{4,8},{8,12},{12,0},{1,5},{5,9},{9,13},{13,1},{2,6},{6,10},{... | collective-permute-start | bytes 940040 | tf_op jit(solution)/shard_map/ppermute | solution.py:834
  59.6 19.7 %collective-permute-start.8 = (bf16[272,1024]{1,0:T(8,128)(2,1)}, bf16[272,1024]{1,0:T(8,128)(2,1)S(1)}, u32[]{:S(2)}, u32[]{:S(2)}) collective-permute-start(bf16[272,1024]{1,0:T(8,128)(2,1)} %collective-permute-done.1.p0), channel_id=1, source_target_pairs={{0,2},{2,0},{1,3},{3,1},{4,6},{6,4},{5,7},{7,5},{8,10},{10,8},{9,1... | collective-permute-start | bytes 1671176 | tf_op jit(solution)/shard_map/ppermute | solution.py:821
  81.5 12.9 %collective-permute-start.9 = (bf16[2,272,1024]{2,1,0:T(8,128)(2,1)}, bf16[2,272,1024]{2,1,0:T(8,128)(2,1)}, u32[]{:S(2)}, u32[]{:S(2)}) collective-permute-start(bf16[2,272,1024]{2,1,0:T(8,128)(2,1)} %pad_maximum_fusion.3), channel_id=1, source_target_pairs={{0,1},{1,0},{2,3},{3,2},{4,5},{5,4},{6,7},{7,6},{8,9},{9,8},{10,11... | collective-permute-start | bytes 3342344 | tf_op jit(solution)/shard_map/ppermute | solution.py:825
  87.1 37.1 %collective-permute-start.12 = (bf16[272,1088]{1,0:T(8,128)(2,1)}, bf16[272,1088]{1,0:T(8,128)(2,1)S(1)}, u32[]{:S(2)}, u32[]{:S(2)}) collective-permute-start(bf16[272,1088]{1,0:T(8,128)(2,1)} %get-tuple-element.117.refs_0_), channel_id=1, source_target_pairs={{0,2},{2,0},{1,3},{3,1},{4,6},{6,4},{5,7},{7,5},{8,10},{10,8},{9,1... | collective-permute-start | bytes 1775624 | tf_op jit(solution)/shard_map/ppermute | solution.py:821
  88.6 20.2 %collective-permute-start.7 = (bf16[1088,256]{1,0:T(8,128)(2,1)S(1)}, bf16[1088,256]{1,0:T(8,128)(2,1)S(1)}, u32[]{:S(2)}, u32[]{:S(2)}) collective-permute-start(bf16[1088,256]{1,0:T(8,128)(2,1)S(1)} %copy-done.89), channel_id=1, source_target_pairs={{1,0},{2,1},{3,2},{5,4},{6,5},{7,6},{9,8},{10,9},{11,10},{13,12},{... | collective-permute-start | bytes 1671176 | tf_op jit(solution)/shard_map/ppermute | solution.py:1031
  91.5 32.7 %copy-start.73 = (s32[2]{0:T(128)}, s32[2]{0:T(128)S(1)}, u32[]{:S(2)}) copy-start(s32[2]{0:T(128)S(1)} %pad_add_fusion.1.info) | copy-start | bytes 28
  91.5 46.9 %collective-permute-start.17 = (bf16[352,1088]{1,0:T(8,128)(2,1)S(1)}, bf16[352,1088]{1,0:T(8,128)(2,1)S(1)}, u32[]{:S(2)}, u32[]{:S(2)}) collective-permute-start(bf16[352,1088]{1,0:T(8,128)(2,1)S(1)} %pad_maximum_fusion.6), channel_id=1, source_target_pairs={{0,12},{4,0},{8,4},{12,8},{1,13},{5,1},{9,5},{13,9},{2,14},{6,2},{... | collective-permute-start | bytes 2297864 | tf_op jit(solution)/shard_map/ppermute | solution.py:834
  92.1 46.3 %collective-permute-start.16 = (bf16[352,1088]{1,0:T(8,128)(2,1)S(1)}, bf16[352,1088]{1,0:T(8,128)(2,1)S(1)}, u32[]{:S(2)}, u32[]{:S(2)}) collective-permute-start(bf16[352,1088]{1,0:T(8,128)(2,1)S(1)} %pad_maximum_fusion.6), channel_id=1, source_target_pairs={{0,4},{4,8},{8,12},{12,0},{1,5},{5,9},{9,13},{13,1},{2,6},{6,10},{... | collective-permute-start | bytes 2297864 | tf_op jit(solution)/shard_map/ppermute | solution.py:834
  124.1 20.2 %copy-start.58 = (bf16[320,512]{1,0:T(8,128)(2,1)}, bf16[320,512]{1,0:T(8,128)(2,1)S(1)}, u32[]{:S(2)}) copy-start(bf16[320,512]{1,0:T(8,128)(2,1)S(1)} %get-tuple-element.111.p0) | copy-start | bytes 983044
  124.1 14.3 %collective-permute-start.10 = (bf16[320,512]{1,0:T(8,128)(2,1)S(1)}, bf16[320,512]{1,0:T(8,128)(2,1)S(1)}, u32[]{:S(2)}, u32[]{:S(2)}) collective-permute-start(bf16[320,512]{1,0:T(8,128)(2,1)S(1)} %get-tuple-element.111.p0), channel_id=1, source_target_pairs={{0,2},{2,0},{1,3},{3,1},{4,6},{6,4},{5,7},{7,5},{8,10},{10,8},{9,1... | collective-permute-start | bytes 983048 | tf_op jit(solution)/shard_map/ppermute | solution.py:821
  132.3 39.7 %collective-permute-start.14 = (bf16[320,512]{1,0:T(8,128)(2,1)S(1)}, bf16[320,512]{1,0:T(8,128)(2,1)}, u32[]{:S(2)}, u32[]{:S(2)}) collective-permute-start(bf16[320,512]{1,0:T(8,128)(2,1)S(1)} %get-tuple-element.124.p0), channel_id=1, source_target_pairs={{0,2},{2,0},{1,3},{3,1},{4,6},{6,4},{5,7},{7,5},{8,10},{10,8},{9,1... | collective-permute-start | bytes 983048 | tf_op jit(solution)/shard_map/ppermute | solution.py:821
  136.6 25.3 %collective-permute-start.13 = (bf16[2,272,1088]{2,1,0:T(8,128)(2,1)}, bf16[2,272,1088]{2,1,0:T(8,128)(2,1)}, u32[]{:S(2)}, u32[]{:S(2)}) collective-permute-start(bf16[2,272,1088]{2,1,0:T(8,128)(2,1)} %pad_maximum_fusion.2), channel_id=1, source_target_pairs={{0,1},{1,0},{2,3},{3,2},{4,5},{5,4},{6,7},{7,6},{8,9},{9,8},{10,11... | collective-permute-start | bytes 3551240 | tf_op jit(solution)/shard_map/ppermute | solution.py:825
  139.3 20.5 %collective-permute-start.20 = (bf16[176,1088]{1,0:T(8,128)(2,1)}, bf16[176,1088]{1,0:T(8,128)(2,1)}, u32[]{:S(2)}, u32[]{:S(2)}) collective-permute-start(bf16[176,1088]{1,0:T(8,128)(2,1)} %get-tuple-element.274.refs_1_), channel_id=1, source_target_pairs={{0,4},{4,8},{8,12},{12,0},{1,5},{5,9},{9,13},{13,1},{2,6},{6,10},{... | collective-permute-start | bytes 1148936 | tf_op jit(solution)/shard_map/ppermute | solution.py:834
  142.3 31.9 %collective-permute-start.18 = (bf16[176,1088]{1,0:T(8,128)(2,1)}, bf16[176,1088]{1,0:T(8,128)(2,1)}, u32[]{:S(2)}, u32[]{:S(2)}) collective-permute-start(bf16[176,1088]{1,0:T(8,128)(2,1)} %get-tuple-element.277.refs_2_), channel_id=1, source_target_pairs={{0,12},{4,0},{8,4},{12,8},{1,13},{5,1},{9,5},{13,9},{2,14},{6,2},{... | collective-permute-start | bytes 1148936 | tf_op jit(solution)/shard_map/ppermute | solution.py:834
  145.2 15.5 %collective-permute-start.11 = (bf16[2,320,512]{2,1,0:T(8,128)(2,1)}, bf16[2,320,512]{2,1,0:T(8,128)(2,1)}, u32[]{:S(2)}, u32[]{:S(2)}) collective-permute-start(bf16[2,320,512]{2,1,0:T(8,128)(2,1)} %pad_maximum_fusion.7), channel_id=1, source_target_pairs={{0,1},{1,0},{2,3},{3,2},{4,5},{5,4},{6,7},{7,6},{8,9},{9,8},{10,11... | collective-permute-start | bytes 1966088 | tf_op jit(solution)/shard_map/ppermute | solution.py:825
  159.7 18.2 %collective-permute-start.19 = (bf16[384,1088]{0,1:T(8,128)(2,1)}, bf16[384,1088]{0,1:T(8,128)(2,1)}, u32[]{:S(2)}, u32[]{:S(2)}) collective-permute-start(bf16[384,1088]{0,1:T(8,128)(2,1)} %copy.101), channel_id=1, source_target_pairs={{0,16},{16,0},{1,17},{17,1},{2,18},{18,2},{3,19},{19,3},{4,20},{20... | collective-permute-start | bytes 2506760 | tf_op jit(solution)/shard_map/ppermute | solution.py:829
  174.2 7.5 %collective-permute-start.15 = (bf16[2,320,512]{2,1,0:T(8,128)(2,1)}, bf16[2,320,512]{2,1,0:T(8,128)(2,1)}, u32[]{:S(2)}, u32[]{:S(2)}) collective-permute-start(bf16[2,320,512]{2,1,0:T(8,128)(2,1)} %pad_maximum_fusion.8), channel_id=1, source_target_pairs={{0,1},{1,0},{2,3},{3,2},{4,5},{5,4},{6,7},{7,6},{8,9},{9,8},{10,11... | collective-permute-start | bytes 1966088 | tf_op jit(solution)/shard_map/ppermute | solution.py:825
  175.9 13.2 %collective-permute-start.21 = (bf16[192,1088]{1,0:T(8,128)(2,1)}, bf16[192,1088]{1,0:T(8,128)(2,1)}, u32[]{:S(2)}, u32[]{:S(2)}) collective-permute-start(bf16[192,1088]{1,0:T(8,128)(2,1)} %pad_maximum_fusion.12), channel_id=1, source_target_pairs={{0,16},{16,0},{1,17},{17,1},{2,18},{18,2},{3,19},{19,3},{4,20},{20... | collective-permute-start | bytes 1253384 | tf_op jit(solution)/shard_map/ppermute | solution.py:829
  198.8 20.0 %copy-start.20 = (f32[320,1024]{1,0:T(8,128)S(1)}, f32[320,1024]{1,0:T(8,128)}, u32[]{:S(2)}) copy-start(f32[320,1024]{1,0:T(8,128)} %constant_dynamic-update-slice_fusion.5) | copy-start | bytes 3932164
  198.8 20.1 %copy-start.49 = (f32[1088,512]{1,0:T(8,128)S(1)}, f32[1088,512]{1,0:T(8,128)}, u32[]{:S(2)}) copy-start(f32[1088,512]{1,0:T(8,128)} %copy-done.48) | copy-start | bytes 6684676
  218.5 2.8 collective-permute-start.22
  221.5 14.8 %collective-permute-start.23 = (bf16[1088,256]{1,0:T(8,128)(2,1)S(1)}, bf16[1088,256]{1,0:T(8,128)(2,1)S(1)}, u32[]{:S(2)}, u32[]{:S(2)}) collective-permute-start(bf16[1088,256]{1,0:T(8,128)(2,1)S(1)} %fusion.25), channel_id=1, source_target_pairs={{0,2},{2,0},{1,3},{3,1},{4,6},{6,4},{5,7},{7,5},{8,10},{10,8},{9,1... | collective-permute-start | bytes 1671176 | tf_op jit(solution)/shard_map/ppermute | solution.py:821
  238.1 14.0 %collective-permute-start.26 = (bf16[1088,256]{1,0:T(8,128)(2,1)S(1)}, bf16[1088,256]{1,0:T(8,128)(2,1)S(1)}, u32[]{:S(2)}, u32[]{:S(2)}) collective-permute-start(bf16[1088,256]{1,0:T(8,128)(2,1)S(1)} %get-tuple-element.143.p0), channel_id=1, source_target_pairs={{0,2},{2,0},{1,3},{3,1},{4,6},{6,4},{5,7},{7,5},{8,10},{10,8},{9,1... | collective-permute-start | bytes 1671176 | tf_op jit(solution)/shard_map/ppermute | solution.py:821
  244.6 13.0 %collective-permute-start.24 = (bf16[2,272,1024]{2,1,0:T(8,128)(2,1)}, bf16[2,272,1024]{2,1,0:T(8,128)(2,1)}, u32[]{:S(2)}, u32[]{:S(2)}) collective-permute-start(bf16[2,272,1024]{2,1,0:T(8,128)(2,1)} %dynamic-slice_bitcast_fusion.4), channel_id=1, source_target_pairs={{0,1},{1,0},{2,3},{3,2},{4,5},{5,4},{6,7},{7,6},{8,9},{9,8},{10,11... | collective-permute-start | bytes 3342344 | tf_op jit(solution)/shard_map/ppermute | solution.py:825
  253.2 7.6 %collective-permute-start.27 = (bf16[2,1088,256]{2,1,0:T(8,128)(2,1)}, bf16[2,1088,256]{2,1,0:T(8,128)(2,1)}, u32[]{:S(2)}, u32[]{:S(2)}) collective-permute-start(bf16[2,1088,256]{2,1,0:T(8,128)(2,1)} %pad_maximum_fusion.4), channel_id=1, source_target_pairs={{0,1},{1,0},{2,3},{3,2},{4,5},{5,4},{6,7},{7,6},{8,9},{9,8},{10,11... | collective-permute-start | bytes 3342344 | tf_op jit(solution)/shard_map/ppermute | solution.py:825
  255.0 57.5 %collective-permute-start.30 = (bf16[2,4,136,1088]{3,2,0,1:T(8,128)(2,1)}, bf16[2,4,136,1088]{3,2,0,1:T(8,128)(2,1)}, u32[]{:S(2)}, u32[]{:S(2)}) collective-permute-start(bf16[2,4,136,1088]{3,2,0,1:T(8,128)(2,1)} %pad_maximum_fusion), channel_id=1, source_target_pairs={{0,16},{16,0},{1,17},{17,1},{2,18},{18,2},{3,19},{19,3},{4,20},{20... | collective-permute-start | bytes 7102472 | tf_op jit(solution)/shard_map/ppermute | solution.py:829
  259.2 23.8 %collective-permute-start.25 = (bf16[272,1024]{1,0:T(8,128)(2,1)S(1)}, bf16[272,1024]{1,0:T(8,128)(2,1)S(1)}, u32[]{:S(2)}, u32[]{:S(2)}) collective-permute-start(bf16[272,1024]{1,0:T(8,128)(2,1)S(1)} %fusion.8), channel_id=1, source_target_pairs={{0,2},{2,0},{1,3},{3,1},{4,6},{6,4},{5,7},{7,5},{8,10},{10,8},{9,1... | collective-permute-start | bytes 1671176 | tf_op jit(solution)/shard_map/ppermute | solution.py:821
  265.9 24.6 %collective-permute-start.28 = (f32[4,1088]{1,0:T(4,128)S(1)}, f32[4,1088]{1,0:T(4,128)S(1)}, u32[]{:S(2)}, u32[]{:S(2)}) collective-permute-start(f32[4,1088]{1,0:T(4,128)S(1)} %pad_maximum_fusion.19), channel_id=1, source_target_pairs={{0,2},{2,0},{1,3},{3,1},{4,6},{6,4},{5,7},{7,5},{8,10},{10,8},{9,1... | collective-permute-start | bytes 52232 | tf_op jit(solution)/shard_map/ppermute | solution.py:821
  289.1 23.5 %copy-start.90 = (bf16[1,4,136,1088]{3,2,0,1:T(8,128)(2,1)S(1)}, bf16[1,4,136,1088]{3,2,0,1:T(8,128)(2,1)}, u32[]{:S(2)}) copy-start(bf16[1,4,136,1088]{3,2,0,1:T(8,128)(2,1)} %get-tuple-element.258) | copy-start | bytes 3551236
  289.1 51.1 %collective-permute-start.31 = (bf16[640,1024]{1,0:T(8,128)(2,1)}, bf16[640,1024]{1,0:T(8,128)(2,1)S(1)}, u32[]{:S(2)}, u32[]{:S(2)}) collective-permute-start(bf16[640,1024]{1,0:T(8,128)(2,1)} %copy-done.24), channel_id=1, source_target_pairs={{16,0},{17,1},{18,2},{19,3},{20,4},{21,5},{22,6},{23,7},{24,8},{25... | collective-permute-start | bytes 3932168 | tf_op jit(solution)/shard_map/ppermute | solution.py:1191
  290.6 2.1 collective-permute-start.29
  314.9 29.5 %collective-permute-start.38 = (bf16[136,1088]{1,0:T(8,128)(2,1)S(1)}, bf16[136,1088]{1,0:T(8,128)(2,1)S(1)}, u32[]{:S(2)}, u32[]{:S(2)}) collective-permute-start(bf16[136,1088]{1,0:T(8,128)(2,1)S(1)} %get-tuple-element.282), channel_id=1, source_target_pairs={{0,12},{4,0},{8,4},{12,8},{1,13},{5,1},{9,5},{13,9},{2,14},{6,2},{... | collective-permute-start | bytes 887816 | tf_op jit(solution)/shard_map/ppermute | solution.py:834
  315.0 29.5 %collective-permute-start.37 = (bf16[136,1088]{1,0:T(8,128)(2,1)S(1)}, bf16[136,1088]{1,0:T(8,128)(2,1)S(1)}, u32[]{:S(2)}, u32[]{:S(2)}) collective-permute-start(bf16[136,1088]{1,0:T(8,128)(2,1)S(1)} %get-tuple-element.283), channel_id=1, source_target_pairs={{0,4},{4,8},{8,12},{12,0},{1,5},{5,9},{9,13},{13,1},{2,6},{6,10},{... | collective-permute-start | bytes 887816 | tf_op jit(solution)/shard_map/ppermute | solution.py:834
  319.8 20.3 %copy-start.43 = (bf16[1088,960]{1,0:T(8,128)(2,1)S(1)}, bf16[1088,960]{1,0:T(8,128)(2,1)}, u32[]{:S(2)}) copy-start(bf16[1088,960]{1,0:T(8,128)(2,1)} %copy-done.42) | copy-start | bytes 6266884
  319.8 20.3 %copy-start.82 = (s32[2]{0:T(128)S(1)}, s32[2]{0:T(128)}, u32[]{:S(2)}) copy-start(s32[2]{0:T(128)} %pad_add_fusion.4.refs_0_) | copy-start | bytes 28
  344.4 6.0 %collective-permute-start.32 = (bf16[2,272,1024]{2,1,0:T(8,128)(2,1)S(1)}, bf16[2,272,1024]{2,1,0:T(8,128)(2,1)}, u32[]{:S(2)}, u32[]{:S(2)}) collective-permute-start(bf16[2,272,1024]{2,1,0:T(8,128)(2,1)S(1)} %get-tuple-element.167), channel_id=1, source_target_pairs={{0,1},{1,0},{2,3},{3,2},{4,5},{5,4},{6,7},{7,6},{8,9},{9,8},{10,11... | collective-permute-start | bytes 3342344 | tf_op jit(solution)/shard_map/ppermute | solution.py:825
  345.4 30.2 %collective-permute-start.39 = (bf16[2,136,1088]{2,1,0:T(8,128)(2,1)}, bf16[2,136,1088]{2,1,0:T(8,128)(2,1)}, u32[]{:S(2)}, u32[]{:S(2)}) collective-permute-start(bf16[2,136,1088]{2,1,0:T(8,128)(2,1)} %pad_maximum_fusion.10), channel_id=1, source_target_pairs={{0,4},{4,8},{8,12},{12,0},{1,5},{5,9},{9,13},{13,1},{2,6},{6,10},{... | collective-permute-start | bytes 1775624 | tf_op jit(solution)/shard_map/ppermute | solution.py:834
  346.4 29.3 %collective-permute-start.40 = (bf16[2,136,1088]{2,1,0:T(8,128)(2,1)}, bf16[2,136,1088]{2,1,0:T(8,128)(2,1)}, u32[]{:S(2)}, u32[]{:S(2)}) collective-permute-start(bf16[2,136,1088]{2,1,0:T(8,128)(2,1)} %pad_maximum_fusion.11), channel_id=1, source_target_pairs={{0,12},{4,0},{8,4},{12,8},{1,13},{5,1},{9,5},{13,9},{2,14},{6,2},{... | collective-permute-start | bytes 1775624 | tf_op jit(solution)/shard_map/ppermute | solution.py:834
  350.0 33.1 %collective-permute-start.36 = (bf16[1,4,136,1232]{3,2,1,0:T(8,128)(2,1)}, bf16[1,4,136,1232]{3,2,1,0:T(8,128)(2,1)}, u32[]{:S(2)}, u32[]{:S(2)}) collective-permute-start(bf16[1,4,136,1232]{3,2,1,0:T(8,128)(2,1)} %maximum_bitcast_fusion), channel_id=1, source_target_pairs={{0,16},{16,0},{1,17},{17,1},{2,18},{18,2},{3,19},{19,3},{4,20},{20... | collective-permute-start | bytes 4021256 | tf_op jit(solution)/shard_map/ppermute | solution.py:829
  350.3 25.4 %copy-start.91 = (bf16[1,4,136,1088]{3,2,0,1:T(8,128)(2,1)S(1)}, bf16[1,4,136,1088]{3,2,0,1:T(8,128)(2,1)}, u32[]{:S(2)}) copy-start(bf16[1,4,136,1088]{3,2,0,1:T(8,128)(2,1)} %get-tuple-element.258) | copy-start | bytes 3551236
  351.7 27.0 %collective-permute-start.33 = (bf16[272,1024]{1,0:T(8,128)(2,1)S(1)}, bf16[272,1024]{1,0:T(8,128)(2,1)S(1)}, u32[]{:S(2)}, u32[]{:S(2)}) collective-permute-start(bf16[272,1024]{1,0:T(8,128)(2,1)S(1)} %fusion.26), channel_id=1, source_target_pairs={{0,2},{2,0},{1,3},{3,1},{4,6},{6,4},{5,7},{7,5},{8,10},{10,8},{9,1... | collective-permute-start | bytes 1671176 | tf_op jit(solution)/shard_map/ppermute | solution.py:821
  381.4 4.9 %collective-permute-start.34 = (f32[4,1088]{1,0:T(4,128)S(1)}, f32[4,1088]{1,0:T(4,128)S(1)}, u32[]{:S(2)}, u32[]{:S(2)}) collective-permute-start(f32[4,1088]{1,0:T(4,128)S(1)} %pad_maximum_fusion.22), channel_id=1, source_target_pairs={{0,2},{2,0},{1,3},{3,1},{4,6},{6,4},{5,7},{7,5},{8,10},{10,8},{9,1... | collective-permute-start | bytes 52232 | tf_op jit(solution)/shard_map/ppermute | solution.py:821
  387.0 5.5 %collective-permute-start.35 = (f32[4,1088]{1,0:T(4,128)}, f32[4,1088]{1,0:T(4,128)}, u32[]{:S(2)}, u32[]{:S(2)}) collective-permute-start(f32[4,1088]{1,0:T(4,128)} %fusion.71), channel_id=1, source_target_pairs={{0,1},{1,0},{2,3},{3,2},{4,5},{5,4},{6,7},{7,6},{8,9},{9,8},{10,11... | collective-permute-start | bytes 52232 | tf_op jit(solution)/shard_map/ppermute | solution.py:825
  389.3 6.6 %collective-permute-start.41 = (bf16[136,512]{1,0:T(8,128)(2,1)}, bf16[136,512]{1,0:T(8,128)(2,1)}, u32[]{:S(2)}, u32[]{:S(2)}) collective-permute-start(bf16[136,512]{1,0:T(8,128)(2,1)} %slice_bitcast_fusion.22), channel_id=1, source_target_pairs={{0,4},{4,8},{8,12},{12,0},{1,5},{5,9},{9,13},{13,1},{2,6},{6,10},{... | collective-permute-start | bytes 417800 | tf_op jit(solution)/shard_map/ppermute | solution.py:834
  391.0 10.7 %collective-permute-start.42 = (bf16[136,720]{1,0:T(8,128)(2,1)}, bf16[136,720]{1,0:T(8,128)(2,1)}, u32[]{:S(2)}, u32[]{:S(2)}) collective-permute-start(bf16[136,720]{1,0:T(8,128)(2,1)} %slice_bitcast_fusion.21), channel_id=1, source_target_pairs={{0,12},{4,0},{8,4},{12,8},{1,13},{5,1},{9,5},{13,9},{2,14},{6,2},{... | collective-permute-start | bytes 587528 | tf_op jit(solution)/shard_map/ppermute | solution.py:834
  397.0 25.2 %copy-start.110 = (s32[272]{0:T(512)S(1)}, s32[272]{0:T(512)}, u32[]{:S(2)}) copy-start(s32[272]{0:T(512)} %add_select_fusion.2) | copy-start | bytes 3268
  397.1 27.2 %copy-start.114 = (f32[3]{0:T(128)S(1)}, f32[3]{0:T(128)}, u32[]{:S(2)}) copy-start(f32[3]{0:T(128)} %pad.32.clone) | copy-start | bytes 40
  397.1 27.9 %copy-start.97 = (bf16[272,3,272]{2,0,1:T(8,128)(2,1)S(1)}, bf16[272,3,272]{2,0,1:T(8,128)(2,1)}, u32[]{:S(2)}) copy-start(bf16[272,3,272]{2,0,1:T(8,128)(2,1)} %param.19) | copy-start | bytes 1331716
  397.8 28.3 %collective-permute-start.47 = (bf16[1,136,1232]{2,1,0:T(8,128)(2,1)}, bf16[1,136,1232]{2,1,0:T(8,128)(2,1)}, u32[]{:S(2)}, u32[]{:S(2)}) collective-permute-start(bf16[1,136,1232]{2,1,0:T(8,128)(2,1)} %pad_maximum_fusion.13), channel_id=1, source_target_pairs={{0,4},{4,8},{8,12},{12,0},{1,5},{5,9},{9,13},{13,1},{2,6},{6,10},{... | collective-permute-start | bytes 1005320 | tf_op jit(solution)/shard_map/ppermute | solution.py:834
  401.7 4.0 collective-permute-start.43
  405.8 7.5 %collective-permute-start.46 = (f32[7,1088]{1,0:T(8,128)S(1)}, f32[7,1088]{1,0:T(8,128)S(1)}, u32[]{:S(2)}, u32[]{:S(2)}) collective-permute-start(f32[7,1088]{1,0:T(8,128)S(1)} %pad_maximum_fusion.17), channel_id=1, source_target_pairs={{0,12},{4,0},{8,4},{12,8},{1,13},{5,1},{9,5},{13,9},{2,14},{6,2},{... | collective-permute-start | bytes 91400 | tf_op jit(solution)/shard_map/ppermute | solution.py:834
  407.3 6.1 %collective-permute-start.45 = (f32[7,1088]{1,0:T(8,128)S(1)}, f32[7,1088]{1,0:T(8,128)S(1)}, u32[]{:S(2)}, u32[]{:S(2)}) collective-permute-start(f32[7,1088]{1,0:T(8,128)S(1)} %pad_maximum_fusion.17), channel_id=1, source_target_pairs={{0,8},{4,12},{8,0},{12,4},{1,9},{5,13},{9,1},{13,5},{2,10},{6,14},... | collective-permute-start | bytes 91400 | tf_op jit(solution)/shard_map/ppermute | solution.py:834
  409.9 11.1 %collective-permute-start.44 = (f32[7,1088]{1,0:T(8,128)S(1)}, f32[7,1088]{1,0:T(8,128)S(1)}, u32[]{:S(2)}, u32[]{:S(2)}) collective-permute-start(f32[7,1088]{1,0:T(8,128)S(1)} %pad_maximum_fusion.17), channel_id=1, source_target_pairs={{0,4},{4,8},{8,12},{12,0},{1,5},{5,9},{9,13},{13,1},{2,6},{6,10},{... | collective-permute-start | bytes 91400 | tf_op jit(solution)/shard_map/ppermute | solution.py:834
  410.0 16.2 %collective-permute-start.48 = (bf16[1,136,1232]{2,1,0:T(8,128)(2,1)S(1)}, bf16[1,136,1232]{2,1,0:T(8,128)(2,1)S(1)}, u32[]{:S(2)}, u32[]{:S(2)}) collective-permute-start(bf16[1,136,1232]{2,1,0:T(8,128)(2,1)S(1)} %pad_maximum_fusion.14), channel_id=1, source_target_pairs={{0,12},{4,0},{8,4},{12,8},{1,13},{5,1},{9,5},{13,9},{2,14},{6,2},{... | collective-permute-start | bytes 1005320 | tf_op jit(solution)/shard_map/ppermute | solution.py:834
  427.6 5.3 %collective-permute-start.50 = (bf16[136,272]{1,0:T(8,128)(2,1)S(1)}, bf16[136,272]{1,0:T(8,128)(2,1)S(1)}, u32[]{:S(2)}, u32[]{:S(2)}) collective-permute-start(bf16[136,272]{1,0:T(8,128)(2,1)S(1)} %slice.558), channel_id=1, source_target_pairs={{0,2},{2,0},{1,3},{3,1},{4,6},{6,4},{5,7},{7,5},{8,10},{10,8},{9,1... | collective-permute-start | bytes 221960 | tf_op jit(solution)/shard_map/ppermute | solution.py:821
  431.0 6.5 %collective-permute-start.49 = (f32[136,144]{0,1:T(8,128)S(1)}, f32[136,144]{0,1:T(8,128)S(1)}, u32[]{:S(2)}, u32[]{:S(2)}) collective-permute-start(f32[136,144]{0,1:T(8,128)S(1)} %bitcast.269), channel_id=1, source_target_pairs={{0,1},{1,2},{2,3},{4,5},{5,6},{6,7},{8,9},{9,10},{10,11},{12,13},{... | collective-permute-start | bytes 235016 | tf_op jit(solution)/shard_map/ppermute | solution.py:1265
  433.0 5.7 %collective-permute-start.51 = (bf16[2,136,272]{2,1,0:T(8,128)(2,1)S(1)}, bf16[2,136,272]{2,1,0:T(8,128)(2,1)S(1)}, u32[]{:S(2)}, u32[]{:S(2)}) collective-permute-start(bf16[2,136,272]{2,1,0:T(8,128)(2,1)S(1)} %pad_maximum_fusion.15), channel_id=1, source_target_pairs={{0,1},{1,0},{2,3},{3,2},{4,5},{5,4},{6,7},{7,6},{8,9},{9,8},{10,11... | collective-permute-start | bytes 443912 | tf_op jit(solution)/shard_map/ppermute | solution.py:825
  (104 other events, 496.6 us)
